TPU v7x, 256 devices: a whole 4x4x8 slice. The times are simulated.
256 devices in a mesh: expert: 32 (over y, z), cuts: 8 (over x, core).
Axes of the slice: x: 4, y: 4, z: 8, core: 2. Of those that a mesh axis runs over, the one named last changes fastest.
Arguments:
- tokens: bfloat16 [8192, 3072], P('expert', 'cuts'), may hold values from -6 to 6
- out_grad: bfloat16 [8192, 3072], P('expert', 'cuts'), may hold values from -3 to 3
- gate_logit: float32 [8192], P('expert'), may hold values from -2 to 2
- expert_ids: int32 [8192, 1], P('expert'), may hold values from 0 to 31; in each aligned block of 256 rows (0 to 255, 256 to 511, ...) at most 16 rows name the same one
- w_gate: bfloat16 [32, 3072, 4096], P('expert', None, 'cuts'), may hold values from -0.109375 to 0.109375
- w_up: bfloat16 [32, 3072, 4096], P('expert', None, 'cuts'), may hold values from -0.109375 to 0.109375
- w_down: bfloat16 [32, 4096, 3072], P('expert', 'cuts'), may hold values from -0.09375 to 0.09375
Outputs:
- input_grad: bfloat16 [8192, 3072], P('expert', 'cuts')
- logit_grad: float32 [8192], P('expert')
- down_stats: float32 [32, 3, 1024, 1024], P('expert', None, 'cuts')
Inputs may be any that keep to these rules, and one draw needn't show every extreme that they name: `expert_ids`: in the rows of one device (aligned blocks of 256 rows) no expert is named by more than 16 rows, and in every draw some expert is named by exactly 16 rows of some device.
All inputs are finite; a program needn't handle non-finite values.
Results may differ from a plain program's by a relative error of at most 0.019.
Values may be sent and summed in bfloat16 or wider, within the bound.
No kernel may reach another device: no remote copies, remote signals or barrier semaphores. Data moves between devices by JAX's collectives and lax.ppermute only.
A program may use at most 128 MiB of HBM per device.

v0:
```python
import jax
import jax.numpy as jnp
from jax import lax
from jax.sharding import PartitionSpec as P

FF = 4096
BLOCK = 1024


def pack_rows(values, slot_index, total):
    empty = jnp.zeros((total, values.shape[1]), values.dtype)
    return empty.at[slot_index].set(values)


def shards(tokens, out_grad, gate_logit, expert_ids, w_gate, w_up, w_down):
    experts = lax.axis_size("expert")
    tok_rows = tokens.shape[0]
    capacity = 2 * tok_rows // experts
    total = experts * capacity
    gate_score = jax.nn.sigmoid(gate_logit)
    weighted = (gate_score[:, None] * out_grad.astype(jnp.float32)).astype(jnp.bfloat16)
    routed = expert_ids[:, 0]
    onehot = (routed[:, None] == jnp.arange(experts, dtype=jnp.int32)[None, :]).astype(jnp.int32)
    arrival = jnp.sum((jnp.cumsum(onehot, axis=0) - 1) * onehot, axis=1)
    slot_index = routed * capacity + arrival
    full_tok, full_wt = (
        lax.all_gather(tokens, "cuts", axis=1, tiled=True),
        lax.all_gather(weighted, "cuts", axis=1, tiled=True),
    )
    routed_tok, routed_wt = (
        lax.all_to_all(
            pack_rows(full_tok, slot_index, total),
            "expert",
            split_axis=0,
            concat_axis=0,
            tiled=True,
        ),
        lax.all_to_all(
            pack_rows(full_wt, slot_index, total), "expert", split_axis=0, concat_axis=0, tiled=True
        ),
    )
    gate_mat = w_gate[0]
    up_mat = w_up[0]
    down_mat = w_down[0]
    contract_last = (((1,), (1,)), ((), ()))
    gate_pre = jnp.dot(routed_tok, gate_mat, preferred_element_type=jnp.float32)
    up_pre = jnp.dot(routed_tok, up_mat, preferred_element_type=jnp.float32)
    gate_sig = jax.nn.sigmoid(gate_pre)
    gate_act = gate_pre * gate_sig
    hidden = (gate_act * up_pre).astype(jnp.bfloat16)
    hidden_grad = lax.dot_general(
        routed_wt, down_mat, contract_last, preferred_element_type=jnp.float32
    )
    dot_local = jnp.sum(hidden.astype(jnp.float32) * hidden_grad, axis=1)
    silu_slope = gate_sig * (1.0 + gate_pre * (1.0 - gate_sig))
    gate_grad = (hidden_grad * up_pre * silu_slope).astype(jnp.bfloat16)
    up_grad = (hidden_grad * gate_act).astype(jnp.bfloat16)
    input_part = lax.dot_general(
        gate_grad, gate_mat, contract_last, preferred_element_type=jnp.float32
    )
    input_part = input_part + lax.dot_general(
        up_grad, up_mat, contract_last, preferred_element_type=jnp.float32
    )
    grad_down = lax.dot_general(
        hidden, routed_wt, (((0,), (0,)), ((), ())), preferred_element_type=jnp.float32
    ).astype(jnp.bfloat16)
    blocked = grad_down.reshape(grad_down.shape[0], grad_down.shape[1] // BLOCK, BLOCK)
    stats_rows = lax.psum_scatter(
        (
            jnp.einsum("fkb,fkc->bkc", blocked, blocked, preferred_element_type=jnp.float32) / FF
        ).astype(jnp.bfloat16),
        "cuts",
        scatter_dimension=0,
        tiled=True,
    ).astype(jnp.float32)
    down_stats = jnp.transpose(stats_rows, (1, 0, 2))
    dot_total = lax.psum(dot_local, "cuts").astype(jnp.bfloat16)
    back_rows, back_dot = (
        lax.all_to_all(
            input_part.astype(jnp.bfloat16), "expert", split_axis=0, concat_axis=0, tiled=True
        ),
        lax.all_to_all(dot_total, "expert", split_axis=0, concat_axis=0, tiled=True),
    )
    own_rows = back_rows[slot_index].astype(jnp.float32)
    input_grad = lax.psum_scatter(
        own_rows.astype(jnp.bfloat16), "cuts", scatter_dimension=1, tiled=True
    )
    gate_dot = back_dot[slot_index].astype(jnp.float32)
    logit_grad = (1.0 - gate_score) * gate_dot
    return (input_grad, logit_grad, down_stats[None])


def solution(mesh):
    return jax.shard_map(
        shards,
        mesh=mesh,
        in_specs=(
            P("expert", "cuts"),
            P("expert", "cuts"),
            P("expert"),
            P("expert", None),
            P("expert", None, "cuts"),
            P("expert", None, "cuts"),
            P("expert", "cuts", None),
        ),
        out_specs=(P("expert", "cuts"), P("expert"), P("expert", None, "cuts", None)),
        check_vma=False,
    )
```

profile of v0, /device:TPU:32, one launch (start us, length us, event | category | flops | bytes accessed | tf_op | source)
XLA Modules:
  0.0 401.1 jit_solution(6777116507066052781)
XLA Ops:
  7.2 0.0 copy-start
  7.2 0.0 all-gather.5.cloned.1.call-start
  7.2 0.7 all-gather.5.cloned.1.call-update
  7.9 0.9 fusion.18
  8.8 0.6 reduce-window.6
  9.4 0.2 slice_reduce_fusion
  9.6 0.8 fusion.17
  10.4 0.7 compare_select_fusion
  11.1 28.6 %all-gather.5.cloned.1.call-done = bf16[256,3072]{1,0:T(8,128)(2,1)} async-done(((bf16[256,384]{1,0:T(8,128)(2,1)}), bf16[256,3072]{1,0:T(8,128)(2,1)}) %all-gather.5.cloned.1.call-update) | async-done | bytes 1572880 | tf_op jit(solution)/shard_map/all_gather | solution.py:27
  39.7 5.8 %scatter_custom_fusion.1 = bf16[512,3072]{1,0:T(8,128)(2,1)} fusion(s32[256]{0:T(256)S(1)} %bitcast.70, bf16[256,3072]{1,0:T(8,128)(2,1)} %all-gather.5.cloned.1.call-done, bf16[]{:T(256)} %constant.8.clone.1), kind=kCustom, calls=%fused_computation.17 | custom fusion | bytes 3146240 | tf_op jit(solution)/shard_map/scatter | solution.py:12
  45.4 0.0 copy-start.7
  45.4 0.0 copy-start.6
  45.4 10.3 %all-to-all-start.1 = ((bf16[32,16,3072]{2,1,0:T(8,128)(2,1)}), bf16[32,16,3072]{2,1,0:T(8,128)(2,1)}, u32[]{:S(2)}, u32[]{:S(2)}) async-start(bf16[32,16,3072]{2,1,0:T(8,128)(2,1)} %bitcast.61), calls=%async_computation.1 | async-start | bytes 6291456 | tf_op jit(solution)/shard_map/all_to_all | solution.py:31
  55.7 0.0 all-gather.3.cloned.1.call-start
  55.8 0.0 copy-done.7
  55.8 0.0 copy-done.6
  55.8 0.8 multiply_convert_fusion.6
  56.6 0.0 all-gather.3.cloned.1.call-update
  56.6 28.9 %all-gather.3.cloned.1.call-done = bf16[256,3072]{1,0:T(8,128)(2,1)} async-done(((bf16[256,384]{1,0:T(8,128)(2,1)}), bf16[256,3072]{1,0:T(8,128)(2,1)}) %all-gather.3.cloned.1.call-update) | async-done | bytes 1572880 | tf_op jit(solution)/shard_map/all_gather | solution.py:28
  85.5 5.8 %scatter_custom_fusion = bf16[512,3072]{1,0:T(8,128)(2,1)} fusion(s32[256]{0:T(256)S(1)} %bitcast.71, bf16[256,3072]{1,0:T(8,128)(2,1)} %all-gather.3.cloned.1.call-done, bf16[]{:T(256)} %constant.8.clone.1), kind=kCustom, calls=%fused_computation.19 | custom fusion | bytes 3146240 | tf_op jit(solution)/shard_map/scatter | solution.py:12
  91.3 36.1 %all-to-all-done.1 = bf16[32,16,3072]{2,1,0:T(8,128)(2,1)} async-done(((bf16[32,16,3072]{2,1,0:T(8,128)(2,1)}), bf16[32,16,3072]{2,1,0:T(8,128)(2,1)}, u32[]{:S(2)}, u32[]{:S(2)}) %all-to-all-start.1) | async-done | bytes 3145760 | tf_op jit(solution)/shard_map/all_to_all | solution.py:31
  127.3 8.3 %all-to-all-start = ((bf16[32,16,3072]{2,1,0:T(8,128)(2,1)}), bf16[32,16,3072]{2,1,0:T(8,128)(2,1)}, u32[]{:S(2)}, u32[]{:S(2)}) async-start(bf16[32,16,3072]{2,1,0:T(8,128)(2,1)} %bitcast.62), calls=%async_computation | async-start | bytes 6291456 | tf_op jit(solution)/shard_map/all_to_all | solution.py:38
  135.6 0.0 copy-done
  135.6 0.0 copy-start.3
  135.6 4.8 %fusion.2 = f32[512,512]{0,1:T(8,128)} fusion(bf16[512,3072]{1,0:T(8,128)(2,1)} %bitcast.9, bf16[1,3072,512]{2,1,0:T(8,128)(2,1)S(1)} %copy-done), kind=kOutput, calls=%fused_computation.9 | convolution fusion | flops 1610612736 | bytes 7340032 | tf_op jit(solution)/shard_map/dot_general | solution.py:46
  140.5 0.0 copy-done.3
  140.5 4.7 %fusion.5 = f32[512,512]{0,1:T(8,128)} fusion(bf16[512,3072]{1,0:T(8,128)(2,1)} %bitcast.9, bf16[1,3072,512]{2,1,0:T(8,128)(2,1)S(1)} %copy-done.3), kind=kOutput, calls=%fused_computation.12 | convolution fusion | flops 1610612736 | bytes 7340032 | tf_op jit(solution)/shard_map/dot_general | solution.py:47
  145.2 61.7 %all-to-all-done = bf16[32,16,3072]{2,1,0:T(8,128)(2,1)} async-done(((bf16[32,16,3072]{2,1,0:T(8,128)(2,1)}), bf16[32,16,3072]{2,1,0:T(8,128)(2,1)}, u32[]{:S(2)}, u32[]{:S(2)}) %all-to-all-start) | async-done | bytes 3145760 | tf_op jit(solution)/shard_map/all_to_all | solution.py:38
  206.9 0.0 copy-start.2
  206.9 0.0 copy-start.5
  206.9 6.3 %multiply_reduce_fusion = (f32[512]{0:T(512)S(1)}, bf16[512,512]{0,1:T(8,128)(2,1)}, f32[512,512]{0,1:T(8,128)S(1)}) fusion(f32[512,512]{0,1:T(8,128)} %fusion.5, f32[512,512]{0,1:T(8,128)} %fusion.2, bf16[512,3072]{1,0:T(8,128)(2,1)} %bitcast.6, bf16[1,512,3072]{2,1,0:T(8,128)(2,1)} %param.13), kind=kOutput, calls=%fused_computation.21 | convolution fusion | flops 1612971520 | bytes 9963520 | tf_op jit(solution)/shard_map/dot_general | solution.py:51
  213.3 0.0 copy-done.2
  213.3 0.0 copy-done.5
  213.3 0.0 copy-start.4
  213.3 2.2 fusion
  215.5 0.0 copy-done.4
  215.5 3.7 add_convert_fusion
  219.1 9.7 %all-to-all-start.2 = ((bf16[32,16,3072]{2,1,0:T(8,128)(2,1)}), bf16[32,16,3072]{2,1,0:T(8,128)(2,1)S(1)}, u32[]{:S(2)}, u32[]{:S(2)}) async-start(bf16[32,16,3072]{2,1,0:T(8,128)(2,1)} %bitcast.60), calls=%async_computation.2 | async-start | bytes 6291456 | tf_op jit(solution)/shard_map/all_to_all | solution.py:79
  228.9 0.0 reduce-scatter.7.cloned.1.call-start
  228.9 71.1 %all-to-all-done.2 = bf16[32,16,3072]{2,1,0:T(8,128)(2,1)S(1)} async-done(((bf16[32,16,3072]{2,1,0:T(8,128)(2,1)}), bf16[32,16,3072]{2,1,0:T(8,128)(2,1)S(1)}, u32[]{:S(2)}, u32[]{:S(2)}) %all-to-all-start.2) | async-done | bytes 3145760 | tf_op jit(solution)/shard_map/all_to_all | solution.py:79
  300.1 2.7 gather_fusion
  302.8 2.6 copy.23
  305.4 0.0 reduce-scatter.7.cloned.1.call-update
  305.4 0.3 reduce-scatter.9.cloned.1.call-start
  305.7 3.9 convolution_convert_fusion
  309.5 2.8 copy.19
  312.4 9.0 %multiply_convert_fusion = bf16[3,1024,1024]{2,1,0:T(8,128)(2,1)} fusion(bf16[512,3,1024]{0,2,1:T(8,128)(2,1)} %bitcast.65), kind=kOutput, calls=%fused_computation.4 | convolution fusion | flops 3227516928 | bytes 9437184 | tf_op jit(solution)/shard_map/fkb,fkc->bkc/dot_general | solution.py:70
  321.3 8.7 %copy.27 = bf16[1024,3072]{1,0:T(8,128)(2,1)} copy(bf16[1024,3072]{0,1:T(8,128)(2,1)} %bitcast.63) | data formatting | bytes 12582912
  330.0 0.0 reduce-scatter.9.cloned.1.call-update
  330.0 12.4 %psum.7 = bf16[512]{0:T(512)(128)(2,1)S(1)} all-reduce(f32[512]{0:T(512)S(1)} %get-tuple-element.12), channel_id=1, replica_groups=mesh['expert'=32,'cuts'=8] {'cuts'}, use_global_device_ids=true, to_apply=%region_7.8 | all-reduce | flops 512 | bytes 3072 | tf_op jit(solution)/shard_map/psum | solution.py:77
  342.5 0.1 all_to_all.44
  342.6 18.6 %all_to_all.49 = bf16[32,16,1]{1,2,0:T(2,128)(2,1)S(1)} all-to-all(bf16[32,16,1]{1,2,0:T(2,128)(2,1)S(1)} %all_to_all.44), channel_id=1, replica_groups=mesh['expert'=32,'cuts'=8] {'expert'}, dimensions={0} | all-to-all | bytes 2048 | tf_op jit(solution)/shard_map/all_to_all | solution.py:82
  361.1 0.1 reduce.1
  361.2 0.1 all_to_all.43
  361.3 1.9 gather_fusion.1
  363.2 0.6 convert_multiply_fusion
  363.8 0.0 reduce-scatter.7.cloned.1.call-done
  363.8 1.7 copy.24
  365.6 21.1 %reduce-scatter.9.cloned.1.call-done = bf16[128,3072]{1,0:T(8,128)(2,1)} async-done(((bf16[1024,3072]{1,0:T(8,128)(2,1)}), bf16[128,3072]{1,0:T(8,128)(2,1)}) %reduce-scatter.9.cloned.1.call-update) | async-done | bytes 786448
  386.7 0.0 copy-start.1
  386.7 2.4 copy.28
  389.1 2.4 convert_bitcast_fusion
  391.5 3.0 copy.21
  394.5 0.0 copy-done.1
  (4 shorter events, 0.1 us)
Async XLA Ops:
  7.2 128.5 %copy-start = (bf16[1,3072,512]{2,1,0:T(8,128)(2,1)S(1)}, bf16[1,3072,512]{2,1,0:T(8,128)(2,1)}, u32[]{:S(2)}) copy-start(bf16[1,3072,512]{2,1,0:T(8,128)(2,1)} %param.11) | copy-start | bytes 9437188
  7.2 32.5 %all-gather.5.cloned.1.call-start = ((), (), s32[]{:S(2)}) async-start(), calls=%async_computation.7 | async-start | bytes 1769472 | tf_op jit(solution)/shard_map/all_gather | solution.py:27
  45.4 10.3 %copy-start.7 = (f32[256]{0:T(256)S(1)}, f32[256]{0:T(256)}, u32[]{:S(2)}) copy-start(f32[256]{0:T(256)} %param.9) | copy-start | bytes 3076
  45.4 10.4 %copy-start.6 = (bf16[256,384]{1,0:T(8,128)(2,1)S(1)}, bf16[256,384]{1,0:T(8,128)(2,1)}, u32[]{:S(2)}) copy-start(bf16[256,384]{1,0:T(8,128)(2,1)} %param.8) | copy-start | bytes 589828
  45.4 81.9 %all-to-all-start.1 = ((bf16[32,16,3072]{2,1,0:T(8,128)(2,1)}), bf16[32,16,3072]{2,1,0:T(8,128)(2,1)}, u32[]{:S(2)}, u32[]{:S(2)}) async-start(bf16[32,16,3072]{2,1,0:T(8,128)(2,1)} %bitcast.61), calls=%async_computation.1 | async-start | bytes 6291456 | tf_op jit(solution)/shard_map/all_to_all | solution.py:31
  55.7 29.8 %all-gather.3.cloned.1.call-start = ((), (), s32[]{:S(2)}) async-start(), calls=%async_computation.6 | async-start | bytes 1769472 | tf_op jit(solution)/shard_map/all_gather | solution.py:28
  127.3 79.6 %all-to-all-start = ((bf16[32,16,3072]{2,1,0:T(8,128)(2,1)}), bf16[32,16,3072]{2,1,0:T(8,128)(2,1)}, u32[]{:S(2)}, u32[]{:S(2)}) async-start(bf16[32,16,3072]{2,1,0:T(8,128)(2,1)} %bitcast.62), calls=%async_computation | async-start | bytes 6291456 | tf_op jit(solution)/shard_map/all_to_all | solution.py:38
  135.6 4.9 %copy-start.3 = (bf16[1,3072,512]{2,1,0:T(8,128)(2,1)S(1)}, bf16[1,3072,512]{2,1,0:T(8,128)(2,1)}, u32[]{:S(2)}) copy-start(bf16[1,3072,512]{2,1,0:T(8,128)(2,1)} %param.12) | copy-start | bytes 9437188
  206.9 6.3 %copy-start.2 = (f32[512,512]{0,1:T(8,128)S(1)}, f32[512,512]{0,1:T(8,128)}, u32[]{:S(2)}) copy-start(f32[512,512]{0,1:T(8,128)} %fusion.2) | copy-start | bytes 3145732
  206.9 6.3 %copy-start.5 = (f32[512,512]{0,1:T(8,128)S(1)}, f32[512,512]{0,1:T(8,128)}, u32[]{:S(2)}) copy-start(f32[512,512]{0,1:T(8,128)} %fusion.5) | copy-start | bytes 3145732
  213.3 2.2 copy-start.4
  219.1 80.9 %all-to-all-start.2 = ((bf16[32,16,3072]{2,1,0:T(8,128)(2,1)}), bf16[32,16,3072]{2,1,0:T(8,128)(2,1)S(1)}, u32[]{:S(2)}, u32[]{:S(2)}) async-start(bf16[32,16,3072]{2,1,0:T(8,128)(2,1)} %bitcast.60), calls=%async_computation.2 | async-start | bytes 6291456 | tf_op jit(solution)/shard_map/all_to_all | solution.py:79
  228.9 134.9 %reduce-scatter.7.cloned.1.call-start = ((), (), s32[]{:S(2)}) async-start(), calls=%async_computation.8 | async-start | bytes 1769472
  305.4 81.3 %reduce-scatter.9.cloned.1.call-start = ((), (), s32[]{:S(2)}) async-start(), calls=%async_computation.9 | async-start | bytes 7077888
  386.7 7.8 %copy-start.1 = (bf16[1,3072,512]{2,1,0:T(8,128)(2,1)S(1)}, bf16[1,3072,512]{2,1,0:T(8,128)(2,1)}, u32[]{:S(2)}) copy-start(bf16[1,3072,512]{2,1,0:T(8,128)(2,1)} %param.11) | copy-start | bytes 9437188
Sparse Core Ops, SparseCore 0:
  9.9 29.7 all-gather.4
  59.0 26.4 all-gather.2
  305.5 34.7 reduce-scatter.6
  342.8 43.8 reduce-scatter.8
where the time goes:
time: 403 us; the launch traced here: 401 us
  waiting for transfers between devices  248 us (62%)
  local copies, waits for them, and re-layouts  37.9 us (9%)
  matrix products  34.6 us (9%)
  blocking collectives  31 us (8%)
  starting transfers between devices  28.6 us (7%)
  between operations  13.9 us (3%)
  other arithmetic  6.78 us (2%)
    all_to_all x1, waiting for transfers between devices, shards(): lax.all_to_all(input_part.astype(jnp.bfloat16), 'expert', split_axis=0, c...  71.1 us
    all_to_all x1, waiting for transfers between devices, shards(): lax.all_to_all(pack_rows(full_wt, slot_index, total), 'expert', split_axi...  61.7 us
    all_to_all x1, waiting for transfers between devices, shards(): lax.all_to_all(pack_rows(full_tok, slot_index, total), 'expert', split_ax...  36.1 us
    all_gather x1, waiting for transfers between devices, shards(): lax.all_gather(weighted, 'cuts', axis=1, tiled=True)  28.9 us
    all_gather x1, waiting for transfers between devices, shards(): lax.all_gather(tokens, 'cuts', axis=1, tiled=True)  28.6 us
    unnamed x6, waiting for transfers between devices  21.9 us
    all_to_all x1, blocking collectives, shards(): lax.all_to_all(dot_total, 'expert', split_axis=0, concat_axis=0, tiled=True)  18.6 us
    unnamed x21, local copies, waits for them, and re-layouts  18.5 us
  transfers between devices with their start and end apart: 7, of which 6 were waited for; matrix products, arithmetic and copies ran while one was open for 12% of the time, Pallas kernels for 0%

commit v1 on v0

v1 whole, which is shorter than its diff:
```python
import functools

import jax
import jax.numpy as jnp
from jax import lax
from jax.experimental import pallas as pl
from jax.experimental.pallas import tpu as pltpu
from jax.sharding import PartitionSpec as P

FF = 4096
BLOCK = 1024
F32 = jnp.float32
BF16 = jnp.bfloat16
VMEM = pltpu.VMEM
LAST = (((1,), (1,)), ((), ()))
FIRST = (((0,), (0,)), ((), ()))


def dot(a, b, dims=(((1,), (0,)), ((), ()))):
    return lax.dot_general(a, b, dims, preferred_element_type=F32)


def iota(shape, dim):
    return lax.broadcasted_iota(jnp.int32, shape, dim)


def whole():
    return pl.BlockSpec(memory_space=VMEM)


def call(body, out, inputs, flops=0, name=None, scratch=(), scalars=1, limit=48):
    moved = sum(x.size * x.dtype.itemsize for x in inputs) + sum(
        o.size * o.dtype.itemsize for o in out
    )
    specs = [pl.BlockSpec(memory_space=pltpu.SMEM)] * scalars
    specs += [whole()] * (len(inputs) - scalars)
    return pl.pallas_call(
        body,
        out_shape=out,
        in_specs=specs,
        out_specs=[whole()] * len(out),
        scratch_shapes=list(scratch),
        compiler_params=pltpu.CompilerParams(vmem_limit_bytes=limit << 20),
        cost_estimate=pl.CostEstimate(flops=flops, bytes_accessed=moved, transcendentals=0),
        name=name,
    )(*inputs)


def column(row):
    return jnp.transpose(jnp.broadcast_to(row, (8, row.shape[1])))[:, :1]


def pack_kernel(capacity, ids_ref, logit_ref, tok_ref, grad_ref, tok_out, wt_out, slot_out):
    ids = ids_ref[...]
    rows = ids.shape[1]
    total = tok_out.shape[0]
    mine = ids == iota((total // capacity, rows), 0)
    earlier = (iota((rows, rows), 0) < iota((rows, rows), 1)).astype(F32).astype(BF16)
    before = dot(mine.astype(F32).astype(BF16), earlier)
    arrival = jnp.sum(jnp.where(mine, before, 0.0), axis=0, keepdims=True)
    slot = ids * capacity + arrival.astype(jnp.int32)
    slot_out[...] = jnp.broadcast_to(slot, slot_out.shape)
    place = (slot == iota((total, rows), 0)).astype(F32).astype(BF16)
    tok_out[...] = dot(place, tok_ref[...]).astype(BF16)
    score = column(jax.nn.sigmoid(logit_ref[...]))
    weighted = (score * grad_ref[...].astype(F32)).astype(BF16)
    wt_out[...] = dot(place, weighted).astype(BF16)


def unpack_kernel(slot_ref, logit_ref, back_ref, grad_out, logit_out):
    total = back_ref.shape[0]
    rows, width = grad_out.shape
    slot = jnp.transpose(slot_ref[...])[:, :1]
    place = (slot == iota((rows, total), 1)).astype(F32).astype(BF16)
    own = dot(place, back_ref[...])
    grad_out[...] = own[:, :width].astype(BF16)
    gate_dot = jnp.transpose(own[:, width:])[:1]
    logit_out[...] = (1.0 - jax.nn.sigmoid(logit_ref[...])) * gate_dot


def block_of(cut, hop, other, chips):
    chip = (cut // 2 + chips - hop) % chips
    core = cut % 2
    return 2 * chip + (1 - core if other else core)


def at(index, size):
    return pl.ds(pl.multiple_of(index * size, size), size)


def gates_kernel(chips, cut_ref, *refs):
    near, far = refs[:chips], refs[chips : 2 * chips]
    gate_ref, up_ref, hid_out, act_out, slope_out, send_out, keep_out, gram = refs[2 * chips :]
    cut = cut_ref[0]
    width = near[0].shape[1]
    for ref, out in ((gate_ref, act_out), (up_ref, slope_out)):
        for k in range(chips):
            rows = jnp.concatenate([near[k][...], far[k][...]], axis=1)
            mat = jnp.concatenate(
                [ref[at(block_of(cut, k, o, chips), width), :] for o in (False, True)], axis=0
            )
            if k == 0:
                out[...] = dot(rows, mat)
            else:
                out[...] += dot(rows, mat)
    gate_pre = act_out[...]
    up_pre = slope_out[...]
    sig = jax.nn.sigmoid(gate_pre)
    act = gate_pre * sig
    hidden = (act * up_pre).astype(BF16)
    act_out[...] = act
    slope_out[...] = up_pre * (sig * (1.0 + gate_pre * (1.0 - sig)))
    hid_out[...] = hidden
    gram[...] = dot(hidden, hidden, LAST)
    half = send_out.shape[0]
    keep_out[...] = gram[at(cut % 2, half), :].astype(BF16)
    send_out[...] = gram[at(1 - cut % 2, half), :].astype(BF16)


def hidden_kernel(chips, cut_ref, *refs):
    near, far = refs[:chips], refs[chips : 2 * chips]
    down_ref, hid_ref, act_ref, slope_ref, both_out, dot_out, acc = refs[2 * chips :]
    cut = cut_ref[0]
    width = near[0].shape[1]
    for k in range(chips):
        rows = jnp.concatenate([near[k][...], far[k][...]], axis=1)
        mat = jnp.concatenate(
            [down_ref[:, at(block_of(cut, k, o, chips), width)] for o in (False, True)], axis=1
        )
        if k == 0:
            acc[...] = dot(rows, mat, LAST)
        else:
            acc[...] += dot(rows, mat, LAST)
    grad = acc[...]
    ff = grad.shape[1]
    both_out[:, :ff] = (grad * slope_ref[...]).astype(BF16)
    both_out[:, ff:] = (grad * act_ref[...]).astype(BF16)
    dots = jnp.sum(hid_ref[...].astype(F32) * grad, axis=1, keepdims=True)
    dot_out[...] = jnp.transpose(jnp.broadcast_to(dots, (dots.shape[0], 128)))[:8]


def part_kernel(where_ref, both_ref, gate_own, gate_oth, up_own, up_oth, keep_out, send_out):
    gate = jnp.concatenate([gate_own[...], gate_oth[...]], axis=0)
    up = jnp.concatenate([up_own[...], up_oth[...]], axis=0)
    out = dot(both_ref[...], jnp.concatenate([gate, up], axis=1), LAST).astype(BF16)
    width = keep_out.shape[1]
    keep_out[...] = out[:, :width]
    send_out[...] = out[:, width:]


def part(where, both, gate_mat, up_mat, width):
    rows, ff = both.shape[0], gate_mat.shape[1]
    mats = [pl.BlockSpec((width, ff), lambda i, w, j=j: (w[j], 0)) for j in (0, 1, 0, 1)]
    out = jax.ShapeDtypeStruct((rows, width), BF16)
    full = pl.BlockSpec((rows, width), lambda i, w: (0, 0))
    return pl.pallas_call(
        part_kernel,
        out_shape=[out, out],
        grid_spec=pltpu.PrefetchScalarGridSpec(
            num_scalar_prefetch=1,
            grid=(1,),
            in_specs=[pl.BlockSpec((rows, 2 * ff), lambda i, w: (0, 0))] + mats,
            out_specs=[full, full],
        ),
        compiler_params=pltpu.CompilerParams(vmem_limit_bytes=48 << 20),
        cost_estimate=pl.CostEstimate(
            flops=8 * rows * ff * width, bytes_accessed=6 << 20, transcendentals=0
        ),
        name="input_part",
    )(where, both, gate_mat, gate_mat, up_mat, up_mat)


def final_kernel(chips, *refs):
    sums, dots, out = refs[:chips], refs[chips : 2 * chips], refs[2 * chips]
    total = sums[0][...].astype(F32)
    gate_dot = dots[0][...]
    for k in range(1, chips):
        total = total + sums[k][...].astype(F32)
        gate_dot = gate_dot + dots[k][...]
    width = total.shape[1]
    out[:, :width] = total.astype(BF16)
    lane = jnp.transpose(jnp.broadcast_to(gate_dot[:1], (128, gate_dot.shape[1])))
    out[:, width:] = lane.astype(BF16)


def split_kernel(chips, cut_ref, keep_ref, recv_ref, *refs):
    outs, half = refs[:chips], refs[chips]
    half[...] = keep_ref[...].astype(F32) + recv_ref[...].astype(F32)
    chip = cut_ref[0] // 2
    for k in range(chips):
        outs[k][...] = half[at((chip + k) % chips, outs[k].shape[0]), :].astype(BF16)


def stats_kernel(chips, cut_ref, *refs):
    near, far = refs[:chips], refs[chips : 2 * chips]
    own_k = refs[2 * chips : 3 * chips]
    oth_k, out, rows, gram = refs[3 * chips :]
    cut = cut_ref[0]
    width = near[0].shape[1]
    piece = own_k[0].shape[0]
    for k in range(chips):
        rows[:, at(block_of(cut, k, False, chips), width)] = near[k][...]
        rows[:, at(block_of(cut, k, True, chips), width)] = far[k][...]
        chip = (cut // 2 + chips - k) % chips
        gram[at(cut % 2 * chips + chip, piece), :] = own_k[k][...]
        gram[at((1 - cut % 2) * chips + chip, piece), :] = oth_k[k * piece : (k + 1) * piece, :]
    share = out.shape[1]
    blocks = out.shape[0]
    per = BLOCK // share
    own = jnp.concatenate([rows[:, at(per * j + cut, share)] for j in range(blocks)], axis=1)
    mixed = dot(gram[...], own).astype(BF16)
    for j in range(blocks):
        out[j] = dot(
            mixed[:, j * share : (j + 1) * share], rows[:, j * BLOCK : (j + 1) * BLOCK], FIRST
        ) * (1.0 / FF)


def shards(tokens, out_grad, gate_logit, expert_ids, w_gate, w_up, w_down):
    experts = lax.axis_size("expert")
    cuts = lax.axis_size("cuts")
    chips = cuts // 2
    tok_rows, width = tokens.shape
    capacity = 2 * tok_rows // experts
    total = experts * capacity
    gate_mat, up_mat, down_mat = w_gate[0], w_up[0], w_down[0]
    ff, feats = down_mat.shape
    shape = jax.ShapeDtypeStruct
    cut = lax.axis_index("cuts").astype(jnp.int32)
    where = cut.reshape(1)

    def hop(x, k):
        if k == 0:
            return x
        return lax.ppermute(
            x, "cuts", [(2 * i + c, 2 * ((i + k) % chips) + c) for i in range(chips) for c in (0, 1)]
        )

    def swap(x):
        return lax.ppermute(x, "cuts", [(i, i ^ 1) for i in range(cuts)])

    def exchange(x):
        return lax.all_to_all(x, "expert", split_axis=0, concat_axis=0, tiled=True)

    order = [0, 1, 3, 2]
    ids = expert_ids.reshape(1, tok_rows)
    logit = gate_logit.reshape(1, tok_rows)
    tok_pack, wt_pack, slot = call(
        functools.partial(pack_kernel, capacity),
        [
            shape((total, width), BF16),
            shape((total, width), BF16),
            shape((8, tok_rows), jnp.int32),
        ],
        (ids, logit, tokens, out_grad),
        4 * total * tok_rows * width,
        "pack",
        scalars=0,
    )

    def gathered(packed):
        rows = exchange(packed.reshape(experts, capacity, width)).reshape(total, width)
        near = [hop(rows, k) for k in range(chips)]
        return near, [swap(x) for x in near]

    tok_near, tok_far = gathered(tok_pack)
    wt_near, wt_far = gathered(wt_pack)

    half = total // 2
    hidden, act, slope, gram_send, gram_keep = call(
        functools.partial(gates_kernel, chips),
        [
            shape((total, ff), BF16),
            shape((total, ff), F32),
            shape((total, ff), F32),
            shape((half, total), BF16),
            shape((half, total), BF16),
        ],
        (where, *tok_near, *tok_far, gate_mat, up_mat),
        4 * total * feats * ff + 2 * total * total * ff,
        "gates",
        scratch=[VMEM((total, total), F32)],
    )
    both, dots = call(
        functools.partial(hidden_kernel, chips),
        [shape((total, 2 * ff), BF16), shape((8, total), F32)],
        (where, *wt_near, *wt_far, down_mat, hidden, act, slope),
        2 * total * feats * ff,
        "hidden_grad",
        scratch=[VMEM((total, ff), F32)],
    )

    chip, core = cut // 2, cut % 2
    sums = [None] * chips
    for k in (2, 1, 3, 0):
        base = 2 * ((chip + k) % chips)
        keep, send = part(
            jnp.stack([base + core, base + 1 - core]), both, gate_mat, up_mat, width
        )
        chip_sum = (keep.astype(F32) + swap(send).astype(F32)).astype(BF16)
        sums[k] = hop(chip_sum, k)
    chip_dots = dots + swap(dots)
    all_dots = [hop(chip_dots, k) for k in range(chips)]

    pieces = call(
        functools.partial(split_kernel, chips),
        [shape((half // chips, total), BF16)] * chips,
        (where, gram_keep, swap(gram_send)),
        0,
        "gram_split",
        scratch=[VMEM((half, total), F32)],
    )
    mine = sum(hop(pieces[k], k).astype(F32) for k in range(chips)).astype(BF16)
    gram_own = [hop(mine, k) for k in range(chips)]
    gram_oth = swap(jnp.concatenate(gram_own, axis=0))
    blocks = feats // BLOCK
    (stats,) = call(
        functools.partial(stats_kernel, chips),
        [shape((blocks, BLOCK // cuts, BLOCK), F32)],
        (where, *wt_near, *wt_far, *gram_own, gram_oth),
        4 * total * total * feats // cuts + 2 * total * BLOCK * feats // cuts,
        "stats",
        scratch=[VMEM((total, feats), BF16), VMEM((total, total), BF16)],
    )

    (payload,) = call(
        functools.partial(final_kernel, chips),
        [shape((total, width + 128), BF16)],
        (*sums, *all_dots),
        0,
        "final",
        scalars=0,
    )
    back = exchange(payload.reshape(experts, capacity, width + 128)).reshape(total, width + 128)
    input_grad, logit_grad = call(
        unpack_kernel,
        [shape((tok_rows, width), BF16), shape((1, tok_rows), F32)],
        (slot, logit, back),
        2 * tok_rows * total * (width + 128),
        "unpack",
        scalars=0,
    )
    return input_grad, logit_grad.reshape(tok_rows), stats[None]


def solution(mesh):
    return jax.shard_map(
        shards,
        mesh=mesh,
        in_specs=(
            P("expert", "cuts"),
            P("expert", "cuts"),
            P("expert"),
            P("expert", None),
            P("expert", None, "cuts"),
            P("expert", None, "cuts"),
            P("expert", "cuts", None),
        ),
        out_specs=(P("expert", "cuts"), P("expert"), P("expert", None, "cuts", None)),
        check_vma=False,
    )
```

time: 403 us -> 177 us (0.44)
  waiting for transfers between devices: 248 us -> 66.4 us
  matrix products: 34.6 us -> 0 us
  Pallas kernels: 0 us -> 31.2 us
  local copies, waits for them, and re-layouts: 37.9 us -> 9.59 us
  between operations: 13.9 us -> 1.05 us
  starting transfers between devices: 28.6 us -> 38.1 us
  blocking collectives: 31 us -> 26 us
    all_to_all x3 -> x2, waiting for transfers between devices: 169 us -> 9.84 us  [exchange(): return lax.all_to_all(x, 'expert', split_axis=0, concat_axis=0, tiled=True)]
    all_gather x2 -> x0, waiting for transfers between devices: 57.5 us -> none  [the longest x1 28.9 us: shards(): lax.all_gather(weighted, 'cuts', axis=1, tiled=True)]
    ppermute x0 -> x33, waiting for transfers between devices: none -> 56.6 us  [the longest x18 53.9 us: hop(): lax.ppermute(x, 'cuts', [(2 * i + c, 2 * ((i + k) % chips) + c) for i in...]
    dot_general x7 -> x0, matrix products: 34.6 us -> none  [the longest x1 8.96 us: shards(): jnp.einsum('fkb,fkc->bkc', blocked, blocked, preferred_element_type=jnp.f...]
    pallas_call x0 -> x11, Pallas kernels: none -> 31.2 us  [the longest x7 19.8 us: call(): pl.pallas_call(body, out_shape=out, in_specs=specs, out_specs=[whole()] *...]
    ppermute x0 -> x33, starting transfers between devices: none -> 23.6 us  [the longest x18 20.9 us: hop(): lax.ppermute(x, 'cuts', [(2 * i + c, 2 * ((i + k) % chips) + c) for i in...]
    unnamed x6 -> x0, waiting for transfers between devices: 21.9 us -> none
    all_to_all x3 -> x2, starting transfers between devices: 28.3 us -> 14.6 us  [exchange(): return lax.all_to_all(x, 'expert', split_axis=0, concat_axis=0, tiled=True)]
  transfers between devices with their start and end apart: 7 -> 35, of which waited for: 6 -> 15; matrix products, arithmetic and copies ran while one was open for 12% -> 2% of each run, Pallas kernels for 0% -> 12%
where the time goes in v1:
time: 177 us; the launch traced here: 175 us
  waiting for transfers between devices  66.4 us (38%)
  starting transfers between devices  38.1 us (22%)
  Pallas kernels  31.2 us (18%)
  blocking collectives  26 us (15%)
  local copies, waits for them, and re-layouts  9.59 us (5%)
  other arithmetic  2.91 us (2%)
    ppermute x18, waiting for transfers between devices, hop(): lax.ppermute(x, 'cuts', [(2 * i + c, 2 * ((i + k) % chips) + c) for i in...  53.9 us
    all_to_all x1, blocking collectives, exchange(): return lax.all_to_all(x, 'expert', split_axis=0, concat_axis=0, tiled=True)  26 us
    ppermute x18, starting transfers between devices, hop(): lax.ppermute(x, 'cuts', [(2 * i + c, 2 * ((i + k) % chips) + c) for i in...  20.9 us
    pallas_call x7, Pallas kernels, call(): pl.pallas_call(body, out_shape=out, in_specs=specs, out_specs=[whole()] *...  19.8 us
    all_to_all x2, starting transfers between devices, exchange(): return lax.all_to_all(x, 'expert', split_axis=0, concat_axis=0, tiled=True)  14.6 us
    pallas_call x4, Pallas kernels, part(): pl.pallas_call(part_kernel, out_shape=[out, out], grid_spec=pltpu.Prefetc...  11.5 us
    all_to_all x2, waiting for transfers between devices, exchange(): return lax.all_to_all(x, 'expert', split_axis=0, concat_axis=0, tiled=True)  9.84 us
    unnamed x66, local copies, waits for them, and re-layouts  9.59 us
  transfers between devices with their start and end apart: 35, of which 15 were waited for; matrix products, arithmetic and copies ran while one was open for 2% of the time, Pallas kernels for 12%

profile of v1, /device:TPU:32, one launch (start us, length us, event | category | flops | bytes accessed | tf_op | source)
XLA Modules:
  0.0 175.4 jit_solution(11498115570307677956)
XLA Ops:
  0.6 0.7 copy-done.26
  1.3 0.9 copy-done.30
  2.2 0.9 copy-done.31
  3.2 0.7 copy-done.32
  3.8 1.4 pack.1
  5.2 26.0 %all_to_all.15 = bf16[32,16,384]{2,1,0:T(8,128)(2,1)S(1)} all-to-all(bf16[32,16,384]{2,1,0:T(8,128)(2,1)S(1)} %bitcast.43), channel_id=1, replica_groups=mesh['expert'=32,'cuts'=8] {'expert'}, dimensions={0} | all-to-all | bytes 786432 | tf_op jit(solution)/shard_map/all_to_all | solution.py:242
  31.2 4.8 %all-to-all-start = ((bf16[32,16,384]{2,1,0:T(8,128)(2,1)}), bf16[32,16,384]{2,1,0:T(8,128)(2,1)S(1)}, u32[]{:S(2)}, u32[]{:S(2)}) async-start(bf16[32,16,384]{2,1,0:T(8,128)(2,1)} %bitcast.5), calls=%async_computation | async-start | bytes 786432 | tf_op jit(solution)/shard_map/all_to_all | solution.py:242
  36.1 2.8 %collective-permute-start.9 = (bf16[512,384]{1,0:T(8,128)(2,1)S(1)}, bf16[512,384]{1,0:T(8,128)(2,1)S(1)}, u32[]{:S(2)}, u32[]{:S(2)}) collective-permute-start(bf16[512,384]{1,0:T(8,128)(2,1)S(1)} %bitcast.39), channel_id=1, source_target_pairs={{0,6},{1,7},{2,0},{3,1},{4,2},{5,3},{6,4},{7,5},{8,14},{9,15},{10,... | collective-permute-start | bytes 1179656 | tf_op jit(solution)/shard_map/ppermute | solution.py:234
  39.0 0.8 collective-permute-start.8
  39.8 0.9 collective-permute-start.7
  40.7 9.8 %all-to-all-done = bf16[32,16,384]{2,1,0:T(8,128)(2,1)S(1)} async-done(((bf16[32,16,384]{2,1,0:T(8,128)(2,1)}), bf16[32,16,384]{2,1,0:T(8,128)(2,1)S(1)}, u32[]{:S(2)}, u32[]{:S(2)}) %all-to-all-start) | async-done | bytes 393248 | tf_op jit(solution)/shard_map/all_to_all | solution.py:242
  50.5 2.8 %collective-permute-start.2 = (bf16[512,384]{1,0:T(8,128)(2,1)S(1)}, bf16[512,384]{1,0:T(8,128)(2,1)S(1)}, u32[]{:S(2)}, u32[]{:S(2)}) collective-permute-start(bf16[512,384]{1,0:T(8,128)(2,1)S(1)} %bitcast.31), channel_id=1, source_target_pairs={{0,6},{1,7},{2,0},{3,1},{4,2},{5,3},{6,4},{7,5},{8,14},{9,15},{10,... | collective-permute-start | bytes 1179656 | tf_op jit(solution)/shard_map/ppermute | solution.py:234
  53.2 0.8 collective-permute-start.1
  54.1 2.6 %collective-permute-done.9.refs_3_ = bf16[512,384]{1,0:T(8,128)(2,1)S(1)} collective-permute-done((bf16[512,384]{1,0:T(8,128)(2,1)S(1)}, bf16[512,384]{1,0:T(8,128)(2,1)S(1)}, u32[]{:S(2)}, u32[]{:S(2)}) %collective-permute-start.9) | collective-permute-done | bytes 393248 | tf_op jit(solution)/shard_map/ppermute | solution.py:234
  56.7 4.3 %collective-permute-done.7.refs_1_ = bf16[512,384]{1,0:T(8,128)(2,1)S(1)} collective-permute-done((bf16[512,384]{1,0:T(8,128)(2,1)S(1)}, bf16[512,384]{1,0:T(8,128)(2,1)S(1)}, u32[]{:S(2)}, u32[]{:S(2)}) %collective-permute-start.7) | collective-permute-done | bytes 393248 | tf_op jit(solution)/shard_map/ppermute | solution.py:234
  61.0 12.3 %collective-permute-done.2.refs_3_ = bf16[512,384]{1,0:T(8,128)(2,1)S(1)} collective-permute-done((bf16[512,384]{1,0:T(8,128)(2,1)S(1)}, bf16[512,384]{1,0:T(8,128)(2,1)S(1)}, u32[]{:S(2)}, u32[]{:S(2)}) %collective-permute-start.2) | collective-permute-done | bytes 393248 | tf_op jit(solution)/shard_map/ppermute | solution.py:234
  73.3 0.7 pad_add_fusion.where_ref
  73.9 0.4 collective-permute-start.3
  74.4 2.6 %collective-permute-done.refs_1_ = bf16[512,384]{1,0:T(8,128)(2,1)S(1)} collective-permute-done((bf16[512,384]{1,0:T(8,128)(2,1)S(1)}, bf16[512,384]{1,0:T(8,128)(2,1)S(1)}, u32[]{:S(2)}, u32[]{:S(2)}) %collective-permute-start) | collective-permute-done | bytes 393248 | tf_op jit(solution)/shard_map/ppermute | solution.py:234
  76.9 0.5 collective-permute-start.5
  77.4 0.3 collective-permute-start.4
  77.8 8.0 %gates.1 = (bf16[512,512]{1,0:T(8,128)(2,1)S(1)}, f32[512,512]{1,0:T(8,128)S(1)}, f32[512,512]{1,0:T(8,128)}, bf16[256,512]{1,0:T(8,128)(2,1)}, bf16[256,512]{1,0:T(8,128)(2,1)S(1)}) custom-call(s32[1]{0:T(128)} %bitcast.4.cut_ref, bf16[512,384]{1,0:T(8,128)(2,1)S(1)} %bitcast.42, bf16[512,384]{1,0:T(8,128)(2,1)S(1)} %collective-permute-done.7.refs_1_, ...), custom_call_target="tpu_custom_call" | custom-call | flops 3489660928 | bytes 12582916 | tf_op jit(solution)/shard_map/gates/pallas_call | solution.py:37
  85.9 1.3 copy-done.4
  87.2 1.0 copy-done.7
  88.2 1.0 copy-done.10
  89.2 4.4 %hidden_grad.1 = (bf16[512,1024]{1,0:T(8,128)(2,1)S(1)}, f32[8,512]{1,0:T(8,128)S(1)}) custom-call(s32[1]{0:T(128)} %bitcast.4.cut_ref, bf16[512,384]{1,0:T(8,128)(2,1)S(1)} %bitcast.35, bf16[512,384]{1,0:T(8,128)(2,1)S(1)} %copy-done.10, bf16[512,384]{1,0:T(8,128)(2,1)S(1)} %copy-done.7, bf16[512,384]{1,0:T(8,128)(2,1)S(1)} %copy-done.4, ...), custom_call_target="tpu_custom_call" | custom-call | flops 1610612736 | bytes 9977860 | tf_op jit(solution)/shard_map/hidden_grad/pallas_call | solution.py:37
  93.7 3.4 %input_part.7 = (bf16[512,384]{1,0:T(8,128)(2,1)S(1)}, bf16[512,384]{1,0:T(8,128)(2,1)}) custom-call(s32[2]{0:T(128)S(1)} %pad_add_fusion.3.where_ref, bf16[512,1024]{1,0:T(8,128)(2,1)S(1)} %get-tuple-element.33.both_ref, bf16[3072,512]{1,0:T(8,128)(2,1)S(1)} %bitcast.23, bf16[3072,512]{1,0:T(8,128)(2,1)S(1)} %bitcast.24, bf16[3072,512]{1,0:T(8,128)(2,1)} %bitcast.48, ...), custom_call_target="tpu_custom_call" | custom-call | flops 805306368 | bytes 6291456 | tf_op jit(solution)/shard_map/input_part/pallas_call | solution.py:156
  97.1 0.8 copy-done.20
  97.9 0.2 collective-permute-start.19
  98.1 0.6 pad_add_fusion.1.where_ref
  98.8 1.2 copy-done.2
  100.1 2.7 %input_part.6 = (bf16[512,384]{1,0:T(8,128)(2,1)S(1)}, bf16[512,384]{1,0:T(8,128)(2,1)S(1)}) custom-call(s32[2]{0:T(128)S(1)} %pad_add_fusion.2.where_ref, bf16[512,1024]{1,0:T(8,128)(2,1)S(1)} %copy-done.2, bf16[3072,512]{1,0:T(8,128)(2,1)S(1)} %bitcast.25, bf16[3072,512]{1,0:T(8,128)(2,1)S(1)} %bitcast.26, bf16[3072,512]{1,0:T(8,128)(2,1)} %bitcast.50, ...), custom_call_target="tpu_custom_call" | custom-call | flops 805306368 | bytes 6291456 | tf_op jit(solution)/shard_map/input_part/pallas_call | solution.py:156
  102.8 0.4 collective-permute-start.17
  103.1 2.7 %input_part.5 = (bf16[512,384]{1,0:T(8,128)(2,1)S(1)}, bf16[512,384]{1,0:T(8,128)(2,1)S(1)}) custom-call(s32[2]{0:T(128)S(1)} %copy-done.29, bf16[512,1024]{1,0:T(8,128)(2,1)S(1)} %copy-done.2, bf16[3072,512]{1,0:T(8,128)(2,1)S(1)} %bitcast.27, bf16[3072,512]{1,0:T(8,128)(2,1)S(1)} %bitcast.28, bf16[3072,512]{1,0:T(8,128)(2,1)} %bitcast.52, ...), custom_call_target="tpu_custom_call" | custom-call | flops 805306368 | bytes 6291456 | tf_op jit(solution)/shard_map/input_part/pallas_call | solution.py:156
  105.8 0.3 collective-permute-start.15
  106.1 2.7 %input_part.4 = (bf16[512,384]{1,0:T(8,128)(2,1)S(1)}, bf16[512,384]{1,0:T(8,128)(2,1)S(1)}) custom-call(s32[2]{0:T(128)S(1)} %copy-done.28, bf16[512,1024]{1,0:T(8,128)(2,1)S(1)} %copy-done.2, bf16[3072,512]{1,0:T(8,128)(2,1)S(1)} %bitcast.29, bf16[3072,512]{1,0:T(8,128)(2,1)S(1)} %bitcast.30, bf16[3072,512]{1,0:T(8,128)(2,1)} %bitcast.54, ...), custom_call_target="tpu_custom_call" | custom-call | flops 805306368 | bytes 6291456 | tf_op jit(solution)/shard_map/input_part/pallas_call | solution.py:156
  108.8 0.4 collective-permute-start.14
  109.2 1.1 add_convert_fusion
  110.3 1.2 collective-permute-start.20
  111.6 0.4 collective-permute-start.18
  112.2 0.9 collective-permute-start.16
  113.0 1.2 collective-permute-done.21
  114.2 2.8 %collective-permute-start.24 = (f32[8,512]{1,0:T(8,128)S(1)}, f32[8,512]{1,0:T(8,128)S(1)}, u32[]{:S(2)}, u32[]{:S(2)}) collective-permute-start(f32[8,512]{1,0:T(8,128)S(1)} %add.94.refs_4_), channel_id=1, source_target_pairs={{0,6},{1,7},{2,0},{3,1},{4,2},{5,3},{6,4},{7,5},{8,14},{9,15},{10,... | collective-permute-start | bytes 49160 | tf_op jit(solution)/shard_map/ppermute | solution.py:234
  117.0 13.5 %collective-permute-done.24.refs_7_ = f32[8,512]{1,0:T(8,128)S(1)} collective-permute-done((f32[8,512]{1,0:T(8,128)S(1)}, f32[8,512]{1,0:T(8,128)S(1)}, u32[]{:S(2)}, u32[]{:S(2)}) %collective-permute-start.24) | collective-permute-done | bytes 16416 | tf_op jit(solution)/shard_map/ppermute | solution.py:234
  130.5 0.7 collective-permute-start.23
  131.2 4.5 %collective-permute-done.23.refs_6_ = f32[8,512]{1,0:T(8,128)S(1)} collective-permute-done((f32[8,512]{1,0:T(8,128)S(1)}, f32[8,512]{1,0:T(8,128)S(1)}, u32[]{:S(2)}, u32[]{:S(2)}) %collective-permute-start.23) | collective-permute-done | bytes 16416 | tf_op jit(solution)/shard_map/ppermute | solution.py:234
  135.8 0.1 add_convert_fusion.3.refs_0_
  135.9 4.8 %collective-permute-done.22.refs_5_ = f32[8,512]{1,0:T(8,128)S(1)} collective-permute-done((f32[8,512]{1,0:T(8,128)S(1)}, f32[8,512]{1,0:T(8,128)S(1)}, u32[]{:S(2)}, u32[]{:S(2)}) %collective-permute-start.22) | collective-permute-done | bytes 16416 | tf_op jit(solution)/shard_map/ppermute | solution.py:234
  140.7 1.2 final.1
  141.9 9.8 %all-to-all-start.2 = ((bf16[32,16,512]{2,1,0:T(8,128)(2,1)}), bf16[32,16,512]{2,1,0:T(8,128)(2,1)S(1)}, u32[]{:S(2)}, u32[]{:S(2)}) async-start(bf16[32,16,512]{2,1,0:T(8,128)(2,1)} %bitcast.18), calls=%async_computation.2 | async-start | bytes 1048576 | tf_op jit(solution)/shard_map/all_to_all | solution.py:242
  151.7 1.1 gram_split.1
  152.9 1.2 collective-permute-start.27
  154.1 2.0 %collective-permute-start.28 = (bf16[64,512]{1,0:T(8,128)(2,1)S(1)}, bf16[64,512]{1,0:T(8,128)(2,1)S(1)}, u32[]{:S(2)}, u32[]{:S(2)}) collective-permute-start(bf16[64,512]{1,0:T(8,128)(2,1)S(1)} %get-tuple-element.50), channel_id=1, source_target_pairs={{0,6},{1,7},{2,0},{3,1},{4,2},{5,3},{6,4},{7,5},{8,14},{9,15},{10,... | collective-permute-start | bytes 196616 | tf_op jit(solution)/shard_map/ppermute | solution.py:234
  156.2 2.9 %collective-permute-done.26 = bf16[64,512]{1,0:T(8,128)(2,1)S(1)} collective-permute-done((bf16[64,512]{1,0:T(8,128)(2,1)S(1)}, bf16[64,512]{1,0:T(8,128)(2,1)S(1)}, u32[]{:S(2)}, u32[]{:S(2)}) %collective-permute-start.26) | collective-permute-done | bytes 65568 | tf_op jit(solution)/shard_map/ppermute | solution.py:234
  159.1 0.9 collective-permute-done.28
  160.0 2.5 %collective-permute-start.31 = (bf16[64,512]{1,0:T(8,128)(2,1)S(1)}, bf16[64,512]{1,0:T(8,128)(2,1)S(1)}, u32[]{:S(2)}, u32[]{:S(2)}) collective-permute-start(bf16[64,512]{1,0:T(8,128)(2,1)S(1)} %add_convert_fusion.4.refs_8_), channel_id=1, source_target_pairs={{0,6},{1,7},{2,0},{3,1},{4,2},{5,3},{6,4},{7,5},{8,14},{9,15},{10,... | collective-permute-start | bytes 196616 | tf_op jit(solution)/shard_map/ppermute | solution.py:234
  162.4 1.0 collective-permute-start.30
  163.5 1.5 collective-permute-done.31.refs_11_
  165.0 3.3 %collective-permute-done.30.refs_10_ = bf16[64,512]{1,0:T(8,128)(2,1)S(1)} collective-permute-done((bf16[64,512]{1,0:T(8,128)(2,1)S(1)}, bf16[64,512]{1,0:T(8,128)(2,1)S(1)}, u32[]{:S(2)}, u32[]{:S(2)}) %collective-permute-start.30) | collective-permute-done | bytes 65568 | tf_op jit(solution)/shard_map/ppermute | solution.py:234
  168.2 0.7 collective-permute-done.29.refs_9_
  169.1 1.5 collective-permute-done.32.refs_12_
  170.6 1.0 copy-done.19
  171.6 2.5 %stats.1 = f32[3,128,1024]{2,1,0:T(8,128)} custom-call(s32[1]{0:T(128)} %bitcast.4.cut_ref, bf16[512,384]{1,0:T(8,128)(2,1)S(1)} %bitcast.36, bf16[512,384]{1,0:T(8,128)(2,1)S(1)} %copy-done.11, bf16[512,384]{1,0:T(8,128)(2,1)S(1)} %copy-done.8, bf16[512,384]{1,0:T(8,128)(2,1)S(1)} %copy-done.5, bf16[512,384]{1,0:T(8,128)(2,1)S(1)} %copy-done.13, ...), custom_call_target="tpu_custom_call" | custom-call | flops 805306368 | bytes 5242884 | tf_op jit(solution)/shard_map/stats/pallas_call | solution.py:37
  174.2 1.2 unpack.1
  (95 shorter events, 0.9 us)
Async XLA Ops:
  1.3 0.9 copy-start.30
  5.2 26.0 %copy-start.24 = (s32[8,256]{1,0:T(8,128)}, s32[8,256]{1,0:T(8,128)S(1)}, u32[]{:S(2)}) copy-start(s32[8,256]{1,0:T(8,128)S(1)} %get-tuple-element.27.slot_ref) | copy-start | bytes 24580
  31.2 19.3 %all-to-all-start = ((bf16[32,16,384]{2,1,0:T(8,128)(2,1)}), bf16[32,16,384]{2,1,0:T(8,128)(2,1)S(1)}, u32[]{:S(2)}, u32[]{:S(2)}) async-start(bf16[32,16,384]{2,1,0:T(8,128)(2,1)} %bitcast.5), calls=%async_computation | async-start | bytes 786432 | tf_op jit(solution)/shard_map/all_to_all | solution.py:242
  36.0 17.2 %collective-permute-start.10 = (bf16[512,384]{1,0:T(8,128)(2,1)S(1)}, bf16[512,384]{1,0:T(8,128)(2,1)S(1)}, u32[]{:S(2)}, u32[]{:S(2)}) collective-permute-start(bf16[512,384]{1,0:T(8,128)(2,1)S(1)} %bitcast.38), channel_id=1, source_target_pairs={{0,1},{1,0},{2,3},{3,2},{4,5},{5,4},{6,7},{7,6},{8,9},{9,8},{10,11... | collective-permute-start | bytes 1179656 | tf_op jit(solution)/shard_map/ppermute | solution.py:239
  36.1 20.6 %collective-permute-start.9 = (bf16[512,384]{1,0:T(8,128)(2,1)S(1)}, bf16[512,384]{1,0:T(8,128)(2,1)S(1)}, u32[]{:S(2)}, u32[]{:S(2)}) collective-permute-start(bf16[512,384]{1,0:T(8,128)(2,1)S(1)} %bitcast.39), channel_id=1, source_target_pairs={{0,6},{1,7},{2,0},{3,1},{4,2},{5,3},{6,4},{7,5},{8,14},{9,15},{10,... | collective-permute-start | bytes 1179656 | tf_op jit(solution)/shard_map/ppermute | solution.py:234
  39.0 17.7 %collective-permute-start.8 = (bf16[512,384]{1,0:T(8,128)(2,1)S(1)}, bf16[512,384]{1,0:T(8,128)(2,1)S(1)}, u32[]{:S(2)}, u32[]{:S(2)}) collective-permute-start(bf16[512,384]{1,0:T(8,128)(2,1)S(1)} %bitcast.40), channel_id=1, source_target_pairs={{0,4},{1,5},{2,6},{3,7},{4,0},{5,1},{6,2},{7,3},{8,12},{9,13},{10,... | collective-permute-start | bytes 1179656 | tf_op jit(solution)/shard_map/ppermute | solution.py:234
  39.8 21.2 %collective-permute-start.7 = (bf16[512,384]{1,0:T(8,128)(2,1)S(1)}, bf16[512,384]{1,0:T(8,128)(2,1)S(1)}, u32[]{:S(2)}, u32[]{:S(2)}) collective-permute-start(bf16[512,384]{1,0:T(8,128)(2,1)S(1)} %bitcast.41), channel_id=1, source_target_pairs={{0,2},{1,3},{2,4},{3,5},{4,6},{5,7},{6,0},{7,1},{8,10},{9,11},{10,... | collective-permute-start | bytes 1179656 | tf_op jit(solution)/shard_map/ppermute | solution.py:234
  50.5 22.8 %collective-permute-start.2 = (bf16[512,384]{1,0:T(8,128)(2,1)S(1)}, bf16[512,384]{1,0:T(8,128)(2,1)S(1)}, u32[]{:S(2)}, u32[]{:S(2)}) collective-permute-start(bf16[512,384]{1,0:T(8,128)(2,1)S(1)} %bitcast.31), channel_id=1, source_target_pairs={{0,6},{1,7},{2,0},{3,1},{4,2},{5,3},{6,4},{7,5},{8,14},{9,15},{10,... | collective-permute-start | bytes 1179656 | tf_op jit(solution)/shard_map/ppermute | solution.py:234
  53.2 20.7 %collective-permute-start.1 = (bf16[512,384]{1,0:T(8,128)(2,1)S(1)}, bf16[512,384]{1,0:T(8,128)(2,1)S(1)}, u32[]{:S(2)}, u32[]{:S(2)}) collective-permute-start(bf16[512,384]{1,0:T(8,128)(2,1)S(1)} %bitcast.32), channel_id=1, source_target_pairs={{0,4},{1,5},{2,6},{3,7},{4,0},{5,1},{6,2},{7,3},{8,12},{9,13},{10,... | collective-permute-start | bytes 1179656 | tf_op jit(solution)/shard_map/ppermute | solution.py:234
  56.7 20.2 %collective-permute-start = (bf16[512,384]{1,0:T(8,128)(2,1)S(1)}, bf16[512,384]{1,0:T(8,128)(2,1)S(1)}, u32[]{:S(2)}, u32[]{:S(2)}) collective-permute-start(bf16[512,384]{1,0:T(8,128)(2,1)S(1)} %bitcast.33), channel_id=1, source_target_pairs={{0,2},{1,3},{2,4},{3,5},{4,6},{5,7},{6,0},{7,1},{8,10},{9,11},{10,... | collective-permute-start | bytes 1179656 | tf_op jit(solution)/shard_map/ppermute | solution.py:234
  56.7 20.2 %collective-permute-start.13 = (bf16[512,384]{1,0:T(8,128)(2,1)S(1)}, bf16[512,384]{1,0:T(8,128)(2,1)}, u32[]{:S(2)}, u32[]{:S(2)}) collective-permute-start(bf16[512,384]{1,0:T(8,128)(2,1)S(1)} %collective-permute-done.9.refs_3_), channel_id=1, source_target_pairs={{0,1},{1,0},{2,3},{3,2},{4,5},{5,4},{6,7},{7,6},{8,9},{9,8},{10,11... | collective-permute-start | bytes 1179656 | tf_op jit(solution)/shard_map/ppermute | solution.py:239
  61.0 16.5 %collective-permute-start.12 = (bf16[512,384]{1,0:T(8,128)(2,1)S(1)}, bf16[512,384]{1,0:T(8,128)(2,1)}, u32[]{:S(2)}, u32[]{:S(2)}) collective-permute-start(bf16[512,384]{1,0:T(8,128)(2,1)S(1)} %collective-permute-done.8.refs_2_), channel_id=1, source_target_pairs={{0,1},{1,0},{2,3},{3,2},{4,5},{5,4},{6,7},{7,6},{8,9},{9,8},{10,11... | collective-permute-start | bytes 1179656 | tf_op jit(solution)/shard_map/ppermute | solution.py:239
  73.2 12.5 %copy-start.3 = (bf16[512,384]{1,0:T(8,128)(2,1)}, bf16[512,384]{1,0:T(8,128)(2,1)S(1)}, u32[]{:S(2)}) copy-start(bf16[512,384]{1,0:T(8,128)(2,1)S(1)} %collective-permute-done.2.refs_3_) | copy-start | bytes 1179652
  73.2 4.5 %collective-permute-start.11 = (bf16[512,384]{1,0:T(8,128)(2,1)S(1)}, bf16[512,384]{1,0:T(8,128)(2,1)}, u32[]{:S(2)}, u32[]{:S(2)}) collective-permute-start(bf16[512,384]{1,0:T(8,128)(2,1)S(1)} %collective-permute-done.7.refs_1_), channel_id=1, source_target_pairs={{0,1},{1,0},{2,3},{3,2},{4,5},{5,4},{6,7},{7,6},{8,9},{9,8},{10,11... | collective-permute-start | bytes 1179656 | tf_op jit(solution)/shard_map/ppermute | solution.py:239
  73.9 11.9 %copy-start.6 = (bf16[512,384]{1,0:T(8,128)(2,1)}, bf16[512,384]{1,0:T(8,128)(2,1)S(1)}, u32[]{:S(2)}) copy-start(bf16[512,384]{1,0:T(8,128)(2,1)S(1)} %collective-permute-done.1.refs_2_) | copy-start | bytes 1179652
  73.9 11.9 %collective-permute-start.3 = (bf16[512,384]{1,0:T(8,128)(2,1)S(1)}, bf16[512,384]{1,0:T(8,128)(2,1)S(1)}, u32[]{:S(2)}, u32[]{:S(2)}) collective-permute-start(bf16[512,384]{1,0:T(8,128)(2,1)S(1)} %bitcast.34), channel_id=1, source_target_pairs={{0,1},{1,0},{2,3},{3,2},{4,5},{5,4},{6,7},{7,6},{8,9},{9,8},{10,11... | collective-permute-start | bytes 1179656 | tf_op jit(solution)/shard_map/ppermute | solution.py:239
  76.9 8.9 %copy-start.9 = (bf16[512,384]{1,0:T(8,128)(2,1)}, bf16[512,384]{1,0:T(8,128)(2,1)S(1)}, u32[]{:S(2)}) copy-start(bf16[512,384]{1,0:T(8,128)(2,1)S(1)} %collective-permute-done.refs_1_) | copy-start | bytes 1179652
  76.9 8.9 %collective-permute-start.6 = (bf16[512,384]{1,0:T(8,128)(2,1)S(1)}, bf16[512,384]{1,0:T(8,128)(2,1)S(1)}, u32[]{:S(2)}, u32[]{:S(2)}) collective-permute-start(bf16[512,384]{1,0:T(8,128)(2,1)S(1)} %collective-permute-done.2.refs_3_), channel_id=1, source_target_pairs={{0,1},{1,0},{2,3},{3,2},{4,5},{5,4},{6,7},{7,6},{8,9},{9,8},{10,11... | collective-permute-start | bytes 1179656 | tf_op jit(solution)/shard_map/ppermute | solution.py:239
  76.9 8.9 %collective-permute-start.5 = (bf16[512,384]{1,0:T(8,128)(2,1)S(1)}, bf16[512,384]{1,0:T(8,128)(2,1)S(1)}, u32[]{:S(2)}, u32[]{:S(2)}) collective-permute-start(bf16[512,384]{1,0:T(8,128)(2,1)S(1)} %collective-permute-done.1.refs_2_), channel_id=1, source_target_pairs={{0,1},{1,0},{2,3},{3,2},{4,5},{5,4},{6,7},{7,6},{8,9},{9,8},{10,11... | collective-permute-start | bytes 1179656 | tf_op jit(solution)/shard_map/ppermute | solution.py:239
  77.4 8.4 %collective-permute-start.4 = (bf16[512,384]{1,0:T(8,128)(2,1)S(1)}, bf16[512,384]{1,0:T(8,128)(2,1)S(1)}, u32[]{:S(2)}, u32[]{:S(2)}) collective-permute-start(bf16[512,384]{1,0:T(8,128)(2,1)S(1)} %collective-permute-done.refs_1_), channel_id=1, source_target_pairs={{0,1},{1,0},{2,3},{3,2},{4,5},{5,4},{6,7},{7,6},{8,9},{9,8},{10,11... | collective-permute-start | bytes 1179656 | tf_op jit(solution)/shard_map/ppermute | solution.py:239
  85.8 7.8 %copy-start.22 = (bf16[256,512]{1,0:T(8,128)(2,1)}, bf16[256,512]{1,0:T(8,128)(2,1)S(1)}, u32[]{:S(2)}) copy-start(bf16[256,512]{1,0:T(8,128)(2,1)S(1)} %get-tuple-element.45.keep_ref) | copy-start | bytes 786436
  85.8 7.8 %copy-start.12 = (bf16[512,384]{1,0:T(8,128)(2,1)}, bf16[512,384]{1,0:T(8,128)(2,1)S(1)}, u32[]{:S(2)}) copy-start(bf16[512,384]{1,0:T(8,128)(2,1)S(1)} %collective-permute-done.3.refs_4_) | copy-start | bytes 1179652
  85.8 7.8 %copy-start.14 = (bf16[512,384]{1,0:T(8,128)(2,1)}, bf16[512,384]{1,0:T(8,128)(2,1)S(1)}, u32[]{:S(2)}) copy-start(bf16[512,384]{1,0:T(8,128)(2,1)S(1)} %collective-permute-done.6.refs_7_) | copy-start | bytes 1179652
  85.9 7.8 %copy-start.16 = (bf16[512,384]{1,0:T(8,128)(2,1)}, bf16[512,384]{1,0:T(8,128)(2,1)S(1)}, u32[]{:S(2)}) copy-start(bf16[512,384]{1,0:T(8,128)(2,1)S(1)} %collective-permute-done.5.refs_6_) | copy-start | bytes 1179652
  85.9 7.8 %copy-start.18 = (bf16[512,384]{1,0:T(8,128)(2,1)}, bf16[512,384]{1,0:T(8,128)(2,1)S(1)}, u32[]{:S(2)}) copy-start(bf16[512,384]{1,0:T(8,128)(2,1)S(1)} %collective-permute-done.4.refs_5_) | copy-start | bytes 1179652
  85.9 1.3 copy-start.4
  87.2 1.0 copy-start.7
  88.2 1.0 copy-start.10
  89.2 4.5 %copy-start = (bf16[1,3072,512]{2,1,0:T(8,128)(2,1)S(1)}, bf16[1,3072,512]{2,1,0:T(8,128)(2,1)}, u32[]{:S(2)}) copy-start(bf16[1,3072,512]{2,1,0:T(8,128)(2,1)} %param.11) | copy-start | bytes 9437188
  93.6 3.5 %copy-start.1 = (bf16[512,1024]{1,0:T(8,128)(2,1)}, bf16[512,1024]{1,0:T(8,128)(2,1)S(1)}, u32[]{:S(2)}) copy-start(bf16[512,1024]{1,0:T(8,128)(2,1)S(1)} %get-tuple-element.33.both_ref) | copy-start | bytes 3145732
  97.9 11.3 %collective-permute-start.19 = (bf16[512,384]{1,0:T(8,128)(2,1)}, bf16[512,384]{1,0:T(8,128)(2,1)}, u32[]{:S(2)}, u32[]{:S(2)}) collective-permute-start(bf16[512,384]{1,0:T(8,128)(2,1)} %get-tuple-element.41), channel_id=1, source_target_pairs={{0,1},{1,0},{2,3},{3,2},{4,5},{5,4},{6,7},{7,6},{8,9},{9,8},{10,11... | collective-permute-start | bytes 1179656 | tf_op jit(solution)/shard_map/ppermute | solution.py:239
  98.8 1.2 copy-start.2
  100.1 3.0 %copy-start.29 = (s32[2]{0:T(128)S(1)}, s32[2]{0:T(128)}, u32[]{:S(2)}) copy-start(s32[2]{0:T(128)} %pad_add_fusion.1.where_ref) | copy-start | bytes 28
  102.8 3.4 %copy-start.28 = (s32[2]{0:T(128)S(1)}, s32[2]{0:T(128)}, u32[]{:S(2)}) copy-start(s32[2]{0:T(128)} %pad_add_fusion.where_ref) | copy-start | bytes 28
  102.8 8.7 %collective-permute-start.17 = (bf16[512,384]{1,0:T(8,128)(2,1)S(1)}, bf16[512,384]{1,0:T(8,128)(2,1)S(1)}, u32[]{:S(2)}, u32[]{:S(2)}) collective-permute-start(bf16[512,384]{1,0:T(8,128)(2,1)S(1)} %get-tuple-element.39), channel_id=1, source_target_pairs={{0,1},{1,0},{2,3},{3,2},{4,5},{5,4},{6,7},{7,6},{8,9},{9,8},{10,11... | collective-permute-start | bytes 1179656 | tf_op jit(solution)/shard_map/ppermute | solution.py:239
  105.8 3.4 %copy-start.21 = (bf16[512,384]{1,0:T(8,128)(2,1)S(1)}, bf16[512,384]{1,0:T(8,128)(2,1)}, u32[]{:S(2)}) copy-start(bf16[512,384]{1,0:T(8,128)(2,1)} %copy-done.20) | copy-start | bytes 1179652
  105.8 6.2 %collective-permute-start.15 = (bf16[512,384]{1,0:T(8,128)(2,1)S(1)}, bf16[512,384]{1,0:T(8,128)(2,1)S(1)}, u32[]{:S(2)}, u32[]{:S(2)}) collective-permute-start(bf16[512,384]{1,0:T(8,128)(2,1)S(1)} %get-tuple-element.37), channel_id=1, source_target_pairs={{0,1},{1,0},{2,3},{3,2},{4,5},{5,4},{6,7},{7,6},{8,9},{9,8},{10,11... | collective-permute-start | bytes 1179656 | tf_op jit(solution)/shard_map/ppermute | solution.py:239
  108.8 26.9 %collective-permute-start.14 = (bf16[512,384]{1,0:T(8,128)(2,1)S(1)}, bf16[512,384]{1,0:T(8,128)(2,1)S(1)}, u32[]{:S(2)}, u32[]{:S(2)}) collective-permute-start(bf16[512,384]{1,0:T(8,128)(2,1)S(1)} %get-tuple-element.35), channel_id=1, source_target_pairs={{0,1},{1,0},{2,3},{3,2},{4,5},{5,4},{6,7},{7,6},{8,9},{9,8},{10,11... | collective-permute-start | bytes 1179656 | tf_op jit(solution)/shard_map/ppermute | solution.py:239
  110.3 30.4 %collective-permute-start.20 = (bf16[512,384]{1,0:T(8,128)(2,1)S(1)}, bf16[512,384]{1,0:T(8,128)(2,1)S(1)}, u32[]{:S(2)}, u32[]{:S(2)}) collective-permute-start(bf16[512,384]{1,0:T(8,128)(2,1)S(1)} %add_convert_fusion), channel_id=1, source_target_pairs={{0,6},{1,7},{2,0},{3,1},{4,2},{5,3},{6,4},{7,5},{8,14},{9,15},{10,... | collective-permute-start | bytes 1179656 | tf_op jit(solution)/shard_map/ppermute | solution.py:234
  111.5 40.3 %copy-start.23 = (bf16[256,512]{1,0:T(8,128)(2,1)S(1)}, bf16[256,512]{1,0:T(8,128)(2,1)}, u32[]{:S(2)}) copy-start(bf16[256,512]{1,0:T(8,128)(2,1)} %copy-done.22) | copy-start | bytes 786436
  111.6 29.1 %collective-permute-start.18 = (bf16[512,384]{1,0:T(8,128)(2,1)S(1)}, bf16[512,384]{1,0:T(8,128)(2,1)S(1)}, u32[]{:S(2)}, u32[]{:S(2)}) collective-permute-start(bf16[512,384]{1,0:T(8,128)(2,1)S(1)} %add_convert_fusion.1), channel_id=1, source_target_pairs={{0,4},{1,5},{2,6},{3,7},{4,0},{5,1},{6,2},{7,3},{8,12},{9,13},{10,... | collective-permute-start | bytes 1179656 | tf_op jit(solution)/shard_map/ppermute | solution.py:234
  112.1 58.5 %copy-start.5 = (bf16[512,384]{1,0:T(8,128)(2,1)S(1)}, bf16[512,384]{1,0:T(8,128)(2,1)}, u32[]{:S(2)}) copy-start(bf16[512,384]{1,0:T(8,128)(2,1)} %copy-done.3) | copy-start | bytes 1179652
  112.1 58.5 %copy-start.8 = (bf16[512,384]{1,0:T(8,128)(2,1)S(1)}, bf16[512,384]{1,0:T(8,128)(2,1)}, u32[]{:S(2)}) copy-start(bf16[512,384]{1,0:T(8,128)(2,1)} %copy-done.6) | copy-start | bytes 1179652
  112.1 58.5 %copy-start.11 = (bf16[512,384]{1,0:T(8,128)(2,1)S(1)}, bf16[512,384]{1,0:T(8,128)(2,1)}, u32[]{:S(2)}) copy-start(bf16[512,384]{1,0:T(8,128)(2,1)} %copy-done.9) | copy-start | bytes 1179652
  112.1 58.5 %copy-start.13 = (bf16[512,384]{1,0:T(8,128)(2,1)S(1)}, bf16[512,384]{1,0:T(8,128)(2,1)}, u32[]{:S(2)}) copy-start(bf16[512,384]{1,0:T(8,128)(2,1)} %copy-done.12) | copy-start | bytes 1179652
  112.2 58.5 %copy-start.15 = (bf16[512,384]{1,0:T(8,128)(2,1)S(1)}, bf16[512,384]{1,0:T(8,128)(2,1)}, u32[]{:S(2)}) copy-start(bf16[512,384]{1,0:T(8,128)(2,1)} %copy-done.14) | copy-start | bytes 1179652
  112.2 58.5 %copy-start.17 = (bf16[512,384]{1,0:T(8,128)(2,1)S(1)}, bf16[512,384]{1,0:T(8,128)(2,1)}, u32[]{:S(2)}) copy-start(bf16[512,384]{1,0:T(8,128)(2,1)} %copy-done.16) | copy-start | bytes 1179652
  112.2 28.5 %collective-permute-start.16 = (bf16[512,384]{1,0:T(8,128)(2,1)S(1)}, bf16[512,384]{1,0:T(8,128)(2,1)S(1)}, u32[]{:S(2)}, u32[]{:S(2)}) collective-permute-start(bf16[512,384]{1,0:T(8,128)(2,1)S(1)} %add_convert_fusion.2), channel_id=1, source_target_pairs={{0,2},{1,3},{2,4},{3,5},{4,6},{5,7},{6,0},{7,1},{8,10},{9,11},{10,... | collective-permute-start | bytes 1179656 | tf_op jit(solution)/shard_map/ppermute | solution.py:234
  113.0 1.2 collective-permute-start.21
  114.2 16.3 %collective-permute-start.24 = (f32[8,512]{1,0:T(8,128)S(1)}, f32[8,512]{1,0:T(8,128)S(1)}, u32[]{:S(2)}, u32[]{:S(2)}) collective-permute-start(f32[8,512]{1,0:T(8,128)S(1)} %add.94.refs_4_), channel_id=1, source_target_pairs={{0,6},{1,7},{2,0},{3,1},{4,2},{5,3},{6,4},{7,5},{8,14},{9,15},{10,... | collective-permute-start | bytes 49160 | tf_op jit(solution)/shard_map/ppermute | solution.py:234
  130.5 5.2 %collective-permute-start.23 = (f32[8,512]{1,0:T(8,128)S(1)}, f32[8,512]{1,0:T(8,128)S(1)}, u32[]{:S(2)}, u32[]{:S(2)}) collective-permute-start(f32[8,512]{1,0:T(8,128)S(1)} %add.94.refs_4_), channel_id=1, source_target_pairs={{0,4},{1,5},{2,6},{3,7},{4,0},{5,1},{6,2},{7,3},{8,12},{9,13},{10,... | collective-permute-start | bytes 49160 | tf_op jit(solution)/shard_map/ppermute | solution.py:234
  135.8 16.0 %collective-permute-start.25 = (bf16[256,512]{1,0:T(8,128)(2,1)}, bf16[256,512]{1,0:T(8,128)(2,1)}, u32[]{:S(2)}, u32[]{:S(2)}) collective-permute-start(bf16[256,512]{1,0:T(8,128)(2,1)} %get-tuple-element.46), channel_id=1, source_target_pairs={{0,1},{1,0},{2,3},{3,2},{4,5},{5,4},{6,7},{7,6},{8,9},{9,8},{10,11... | collective-permute-start | bytes 786440 | tf_op jit(solution)/shard_map/ppermute | solution.py:239
  135.8 5.0 %collective-permute-start.22 = (f32[8,512]{1,0:T(8,128)S(1)}, f32[8,512]{1,0:T(8,128)S(1)}, u32[]{:S(2)}, u32[]{:S(2)}) collective-permute-start(f32[8,512]{1,0:T(8,128)S(1)} %add.94.refs_4_), channel_id=1, source_target_pairs={{0,2},{1,3},{2,4},{3,5},{4,6},{5,7},{6,0},{7,1},{8,10},{9,11},{10,... | collective-permute-start | bytes 49160 | tf_op jit(solution)/shard_map/ppermute | solution.py:234
  141.9 32.2 %all-to-all-start.2 = ((bf16[32,16,512]{2,1,0:T(8,128)(2,1)}), bf16[32,16,512]{2,1,0:T(8,128)(2,1)S(1)}, u32[]{:S(2)}, u32[]{:S(2)}) async-start(bf16[32,16,512]{2,1,0:T(8,128)(2,1)} %bitcast.18), calls=%async_computation.2 | async-start | bytes 1048576 | tf_op jit(solution)/shard_map/all_to_all | solution.py:242
  152.8 21.4 %copy-start.25 = (s32[8,256]{1,0:T(8,128)S(1)}, s32[8,256]{1,0:T(8,128)}, u32[]{:S(2)}) copy-start(s32[8,256]{1,0:T(8,128)} %copy-done.24) | copy-start | bytes 24580
  152.8 21.4 %copy-start.27 = (f32[256]{0:T(256)S(1)}, f32[256]{0:T(256)}, u32[]{:S(2)}) copy-start(f32[256]{0:T(256)} %param.9) | copy-start | bytes 3076
  152.8 6.3 %collective-permute-start.26 = (bf16[64,512]{1,0:T(8,128)(2,1)S(1)}, bf16[64,512]{1,0:T(8,128)(2,1)S(1)}, u32[]{:S(2)}, u32[]{:S(2)}) collective-permute-start(bf16[64,512]{1,0:T(8,128)(2,1)S(1)} %get-tuple-element.48), channel_id=1, source_target_pairs={{0,2},{1,3},{2,4},{3,5},{4,6},{5,7},{6,0},{7,1},{8,10},{9,11},{10,... | collective-permute-start | bytes 196616 | tf_op jit(solution)/shard_map/ppermute | solution.py:234
  152.9 6.2 %collective-permute-start.27 = (bf16[64,512]{1,0:T(8,128)(2,1)S(1)}, bf16[64,512]{1,0:T(8,128)(2,1)S(1)}, u32[]{:S(2)}, u32[]{:S(2)}) collective-permute-start(bf16[64,512]{1,0:T(8,128)(2,1)S(1)} %get-tuple-element.49), channel_id=1, source_target_pairs={{0,4},{1,5},{2,6},{3,7},{4,0},{5,1},{6,2},{7,3},{8,12},{9,13},{10,... | collective-permute-start | bytes 196616 | tf_op jit(solution)/shard_map/ppermute | solution.py:234
  154.1 5.8 %collective-permute-start.28 = (bf16[64,512]{1,0:T(8,128)(2,1)S(1)}, bf16[64,512]{1,0:T(8,128)(2,1)S(1)}, u32[]{:S(2)}, u32[]{:S(2)}) collective-permute-start(bf16[64,512]{1,0:T(8,128)(2,1)S(1)} %get-tuple-element.50), channel_id=1, source_target_pairs={{0,6},{1,7},{2,0},{3,1},{4,2},{5,3},{6,4},{7,5},{8,14},{9,15},{10,... | collective-permute-start | bytes 196616 | tf_op jit(solution)/shard_map/ppermute | solution.py:234
  160.0 5.0 %collective-permute-start.31 = (bf16[64,512]{1,0:T(8,128)(2,1)S(1)}, bf16[64,512]{1,0:T(8,128)(2,1)S(1)}, u32[]{:S(2)}, u32[]{:S(2)}) collective-permute-start(bf16[64,512]{1,0:T(8,128)(2,1)S(1)} %add_convert_fusion.4.refs_8_), channel_id=1, source_target_pairs={{0,6},{1,7},{2,0},{3,1},{4,2},{5,3},{6,4},{7,5},{8,14},{9,15},{10,... | collective-permute-start | bytes 196616 | tf_op jit(solution)/shard_map/ppermute | solution.py:234
  162.4 5.8 %collective-permute-start.30 = (bf16[64,512]{1,0:T(8,128)(2,1)S(1)}, bf16[64,512]{1,0:T(8,128)(2,1)S(1)}, u32[]{:S(2)}, u32[]{:S(2)}) collective-permute-start(bf16[64,512]{1,0:T(8,128)(2,1)S(1)} %add_convert_fusion.4.refs_8_), channel_id=1, source_target_pairs={{0,4},{1,5},{2,6},{3,7},{4,0},{5,1},{6,2},{7,3},{8,12},{9,13},{10,... | collective-permute-start | bytes 196616 | tf_op jit(solution)/shard_map/ppermute | solution.py:234
  163.5 5.5 %collective-permute-start.29 = (bf16[64,512]{1,0:T(8,128)(2,1)S(1)}, bf16[64,512]{1,0:T(8,128)(2,1)S(1)}, u32[]{:S(2)}, u32[]{:S(2)}) collective-permute-start(bf16[64,512]{1,0:T(8,128)(2,1)S(1)} %add_convert_fusion.4.refs_8_), channel_id=1, source_target_pairs={{0,2},{1,3},{2,4},{3,5},{4,6},{5,7},{6,0},{7,1},{8,10},{9,11},{10,... | collective-permute-start | bytes 196616 | tf_op jit(solution)/shard_map/ppermute | solution.py:234
  169.0 1.6 collective-permute-start.32
  170.6 1.0 copy-start.19
  (4 other events, 3.1 us)

commit v2 on v1

v2 whole, which is shorter than its diff:
```python
import functools

import jax
import jax.numpy as jnp
from jax import lax
from jax.experimental import pallas as pl
from jax.experimental.pallas import tpu as pltpu
from jax.sharding import PartitionSpec as P

FF = 4096
BLOCK = 1024
F32 = jnp.float32
BF16 = jnp.bfloat16
VMEM = pltpu.VMEM
LAST = (((1,), (1,)), ((), ()))
FIRST = (((0,), (0,)), ((), ()))


def dot(a, b, dims=(((1,), (0,)), ((), ()))):
    return lax.dot_general(a, b, dims, preferred_element_type=F32)


def iota(shape, dim):
    return lax.broadcasted_iota(jnp.int32, shape, dim)


def whole():
    return pl.BlockSpec(memory_space=VMEM)


def call(body, out, inputs, flops=0, name=None, scratch=(), scalars=1, limit=14, after=(), light=False):
    moved = sum(x.size * x.dtype.itemsize for x in inputs) + sum(
        o.size * o.dtype.itemsize for o in out
    )
    if light:
        flops, moved = 0, 0
    specs = [pl.BlockSpec(memory_space=pltpu.SMEM)] * scalars
    specs += [whole()] * (len(inputs) - scalars)
    specs += [pl.BlockSpec(memory_space=pl.ANY)] * len(after)
    count = len(inputs)

    def kernel(*refs):
        body(*refs[:count], *refs[count + len(after) :])

    return pl.pallas_call(
        kernel,
        out_shape=out,
        in_specs=specs,
        out_specs=[whole()] * len(out),
        scratch_shapes=list(scratch),
        compiler_params=pltpu.CompilerParams(vmem_limit_bytes=limit << 20),
        cost_estimate=pl.CostEstimate(flops=flops, bytes_accessed=moved, transcendentals=0),
        name=name,
    )(*inputs, *after)


def column(row):
    return jnp.transpose(jnp.broadcast_to(row, (8, row.shape[1])))[:, :1]


def pack_kernel(capacity, cut_ref, ids_hbm, logit_hbm, tok_hbm, grad_hbm, out, slot_out, *scratch):
    ids_ref, logit_ref, tok_ref, grad_ref, sems = scratch
    copies = [
        pltpu.make_async_copy(src, dst, sems.at[n])
        for n, (src, dst) in enumerate(
            [
                (ids_hbm, ids_ref),
                (logit_hbm, logit_ref),
                (grad_hbm, grad_ref),
                (tok_hbm, tok_ref),
            ]
        )
    ]
    for copy in copies:
        copy.start()
    copies[0].wait()
    ids = ids_ref[...]
    rows, width = tok_ref.shape
    total = out.shape[0]
    mine = ids == iota((total // capacity, rows), 0)
    earlier = (iota((rows, rows), 0) < iota((rows, rows), 1)).astype(F32).astype(BF16)
    before = dot(mine.astype(F32).astype(BF16), earlier)
    arrival = jnp.sum(jnp.where(mine, before, 0.0), axis=0, keepdims=True)
    slot = ids * capacity + arrival.astype(jnp.int32)
    slot_out[...] = jnp.broadcast_to(slot, slot_out.shape)
    place = (slot == iota((total, rows), 0)).astype(F32).astype(BF16)
    copies[1].wait()
    score = column(jax.nn.sigmoid(logit_ref[...]))
    copies[2].wait()
    weighted = (score * grad_ref[...].astype(F32)).astype(BF16)
    copies[3].wait()
    both = jnp.concatenate([tok_ref[...], weighted], axis=1)
    out[...] = dot(place, both).astype(BF16)


def unpack_kernel(slot_ref, logit_ref, back_ref, grad_out, logit_out):
    total = back_ref.shape[0]
    rows, width = grad_out.shape
    slot = jnp.transpose(slot_ref[...])[:, :1]
    place = (slot == iota((rows, total), 1)).astype(F32).astype(BF16)
    own = dot(place, back_ref[...])
    grad_out[...] = own[:, :width].astype(BF16)
    gate_dot = jnp.transpose(own[:, width:])[:1]
    logit_out[...] = (1.0 - jax.nn.sigmoid(logit_ref[...])) * gate_dot


def block_of(cut, hop, other, chips):
    chip = (cut // 2 + chips - hop) % chips
    core = cut % 2
    return 2 * chip + (1 - core if other else core)


def at(index, size):
    return pl.ds(pl.multiple_of(index * size, size), size)


def gates_kernel(chips, cut_ref, *refs):
    count = 2 * chips - 1
    near, far = refs[:count], refs[count : 2 * count]
    gate_ref, up_ref, hid_out, act_out, slope_out, send_out, keep_out, gram = refs[2 * count :]
    cut = cut_ref[0]
    width = near[0].shape[1]

    def rows_of(k):
        parts = [
            [side[0][...]] if k == 0 else [side[2 * k - 1][...], side[2 * k][...]]
            for side in (near, far)
        ]
        return jnp.concatenate([jnp.concatenate(p, axis=0) for p in parts], axis=1)

    for ref, out in ((gate_ref, act_out), (up_ref, slope_out)):
        for k in range(chips):
            mat = [ref[at(block_of(cut, k, o, chips), width), :] for o in (False, True)]
            mat = jnp.concatenate(mat, axis=0)
            if k == 0:
                out[...] = dot(rows_of(k), mat)
            else:
                out[...] += dot(rows_of(k), mat)
    gate_pre = act_out[...]
    up_pre = slope_out[...]
    sig = jax.nn.sigmoid(gate_pre)
    act = gate_pre * sig
    hidden = (act * up_pre).astype(BF16)
    act_out[...] = act
    slope_out[...] = up_pre * (sig * (1.0 + gate_pre * (1.0 - sig)))
    hid_out[...] = hidden
    gram[...] = dot(hidden, hidden, LAST)
    half = send_out.shape[0]
    keep_out[...] = gram[at(cut % 2, half), :].astype(BF16)
    send_out[...] = gram[at(1 - cut % 2, half), :].astype(BF16)


def encode(flat, width, base):
    rest = flat.shape[1] - width
    over = jnp.concatenate([flat[:, width:], jnp.zeros((8, width - rest), F32)], axis=1)
    left = jnp.concatenate([flat[:, :width], over], axis=0)
    row = iota(left.shape, 0) % 8 - base
    tail = jnp.zeros_like(left)
    for n in range(2):
        term = left.astype(BF16).astype(F32)
        tail = jnp.where(row == n, term, tail)
        left = left - term
    return tail.astype(BF16)


def decode(tail, total):
    flat = [jnp.sum(tail[8 * n : 8 * n + 8], axis=0, keepdims=True) for n in range(2)]
    return jnp.concatenate([flat[0], flat[1][:, : total - flat[0].shape[1]]], axis=1)


def down_product(down_ref, cut, near, far, hop, chips):
    width = near.shape[1]
    mat = [down_ref[:, at(block_of(cut, hop, o, chips), width)] for o in (False, True)]
    rows = jnp.concatenate([near[...], far[...]], axis=1)
    return dot(rows, jnp.concatenate(mat, axis=1), LAST)


def own_hidden_kernel(chips, cut_ref, near, far, down_ref, out):
    out[...] = down_product(down_ref, cut_ref[0], near, far, 0, chips)


def hidden_kernel(chips, cut_ref, *refs):
    near, far = refs[: chips - 1], refs[chips - 1 : 2 * chips - 2]
    down_ref, first_ref, hid_ref, act_ref, slope_ref = refs[2 * chips - 2 : 2 * chips + 3]
    both_out, tail_out, relay_out, acc = refs[2 * chips + 3 :]
    cut = cut_ref[0]
    for k in range(1, chips):
        start = first_ref if k == 1 else acc
        acc[...] = start[...] + down_product(down_ref, cut, near[k - 1], far[k - 1], k, chips)
    grad = acc[...]
    ff = grad.shape[1]
    both_out[:, :ff] = (grad * slope_ref[...]).astype(BF16)
    both_out[:, ff:] = (grad * act_ref[...]).astype(BF16)
    dots = jnp.sum(hid_ref[...].astype(F32) * grad, axis=1, keepdims=True)
    flat = jnp.transpose(jnp.broadcast_to(dots, (dots.shape[0], 128)))[:8]
    width = near[0].shape[1]
    tail_out[...] = encode(flat, width, 2 * (cut % 2))
    relay_out[...] = encode(flat, width, 4 + 2 * (cut % 2))


def part_kernel(cut_ref, both_ref, tail_ref, gate_own, gate_oth, up_own, up_oth, *refs):
    keep_out, send_out = refs[-2:]
    gate = jnp.concatenate([gate_own[...], gate_oth[...]], axis=0)
    up = jnp.concatenate([up_own[...], up_oth[...]], axis=0)
    out = dot(both_ref[...], jnp.concatenate([gate, up], axis=1), LAST).astype(BF16)
    total, width = both_ref.shape[0], keep_out.shape[1]
    keep_out[:total, :] = out[:, :width]
    send_out[:total, :] = out[:, width:]
    keep_out[total:, :] = tail_ref[...]
    send_out[total:, :] = tail_ref[...]


def part(where, both, tail, gate_mat, up_mat, width, hop, chips, after):
    rows, ff = both.shape[0], gate_mat.shape[1]
    mats = [
        pl.BlockSpec((width, ff), lambda i, w, o=o: (block_of(w[0], chips - hop, o, chips), 0))
        for o in (False, True, False, True)
    ]
    long = rows + tail.shape[0]
    out = jax.ShapeDtypeStruct((long, width), BF16)
    full = pl.BlockSpec((long, width), lambda i, w: (0, 0))
    return pl.pallas_call(
        part_kernel,
        out_shape=[out, out],
        grid_spec=pltpu.PrefetchScalarGridSpec(
            num_scalar_prefetch=1,
            grid=(1,),
            in_specs=[
                pl.BlockSpec((rows, 2 * ff), lambda i, w: (0, 0)),
                pl.BlockSpec(tail.shape, lambda i, w: (0, 0)),
            ]
            + mats
            + [pl.BlockSpec(memory_space=pl.ANY)] * len(after),
            out_specs=[full, full],
        ),
        compiler_params=pltpu.CompilerParams(vmem_limit_bytes=10 << 20),
        cost_estimate=pl.CostEstimate(
            flops=8 * rows * ff * width, bytes_accessed=6 << 20, transcendentals=0
        ),
        name="input_part",
    )(where, both, tail, gate_mat, gate_mat, up_mat, up_mat, *after)


def final_kernel(*refs):
    sums, out = refs[:-1], refs[-1]
    rows = out.shape[0]
    width = sums[0].shape[1]
    total = sums[0][...].astype(F32)
    for ref in sums[1:]:
        total = total + ref[...].astype(F32)
    out[:, :width] = total[:rows].astype(BF16)
    flat = decode(total[rows:], rows)
    lane = jnp.transpose(jnp.broadcast_to(flat, (out.shape[1] - width, rows)))
    out[:, width:] = lane.astype(BF16)


def stats_kernel(chips, cut_ref, *refs):
    near, far = refs[:chips], refs[chips : 2 * chips]
    own_k, oth_k, out, rows, gram = refs[2 * chips :]
    cut = cut_ref[0]
    width = near[0].shape[1]
    for k in range(chips):
        rows[:, at(block_of(cut, k, False, chips), width)] = near[k][...]
        rows[:, at(block_of(cut, k, True, chips), width)] = far[k][...]
    half = own_k.shape[0]
    gram[at(cut % 2, half), :] = own_k[...]
    gram[at(1 - cut % 2, half), :] = oth_k[...]
    share = out.shape[1]
    blocks = out.shape[0]
    per = BLOCK // share
    own = jnp.concatenate([rows[:, at(per * j + cut, share)] for j in range(blocks)], axis=1)
    mixed = dot(gram[...], own).astype(BF16)
    for j in range(blocks):
        out[j] = dot(
            mixed[:, j * share : (j + 1) * share], rows[:, j * BLOCK : (j + 1) * BLOCK], FIRST
        ) * (1.0 / FF)


def shards(tokens, out_grad, gate_logit, expert_ids, w_gate, w_up, w_down):
    experts = lax.axis_size("expert")
    cuts = lax.axis_size("cuts")
    chips = cuts // 2
    tok_rows, width = tokens.shape
    capacity = 2 * tok_rows // experts
    total = experts * capacity
    gate_mat, up_mat, down_mat = w_gate[0], w_up[0], w_down[0]
    ff, feats = down_mat.shape
    shape = jax.ShapeDtypeStruct
    cut = lax.axis_index("cuts").astype(jnp.int32)
    where = cut.reshape(1)

    def hop(x, k):
        if k == 0:
            return x
        return lax.ppermute(
            x, "cuts", [(2 * i + c, 2 * ((i + k) % chips) + c) for i in range(chips) for c in (0, 1)]
        )

    def swap(x):
        return lax.ppermute(x, "cuts", [(i, i ^ 1) for i in range(cuts)])

    def exchange(x):
        return lax.all_to_all(x, "expert", split_axis=0, concat_axis=0, tiled=True)

    ids = expert_ids.reshape(1, tok_rows)
    logit = gate_logit.reshape(1, tok_rows)
    packed, slot = pl.pallas_call(
        functools.partial(pack_kernel, capacity),
        out_shape=[shape((total, 2 * width), BF16), shape((8, tok_rows), jnp.int32)],
        in_specs=[pl.BlockSpec(memory_space=pltpu.SMEM)]
        + [pl.BlockSpec(memory_space=pltpu.HBM)] * 4,
        out_specs=[whole()] * 2,
        scratch_shapes=[
            VMEM((1, tok_rows), jnp.int32),
            VMEM((1, tok_rows), F32),
            VMEM((tok_rows, width), BF16),
            VMEM((tok_rows, width), BF16),
            pltpu.SemaphoreType.DMA((4,)),
        ],
        compiler_params=pltpu.CompilerParams(vmem_limit_bytes=8 << 20),
        name="pack",
    )(where, ids, logit, tokens, out_grad)
    routed = exchange(packed.reshape(experts, capacity, 2 * width)).reshape(total, 2 * width)
    tok_in, wt_in = routed[:, :width], routed[:, width:]
    mid = total // 2
    ahead_top, back_low = hop(tok_in[:mid], 1), hop(tok_in[mid:], chips - 1)
    ahead_low, back_top = hop(tok_in[mid:], 1), hop(tok_in[:mid], chips - 1)
    tok_near = [tok_in, ahead_top, ahead_low]
    tok_near += [hop(ahead_top, 1), hop(back_low, chips - 1), back_top, back_low]
    tok_far = [swap(x) for x in tok_near]
    wt_near = [hop(wt_in, k) for k in range(chips)]
    wt_swap = swap(wt_in)

    half = total // 2
    hidden, act, slope, gram_send, gram_keep = call(
        functools.partial(gates_kernel, chips),
        [
            shape((total, ff), BF16),
            shape((total, ff), F32),
            shape((total, ff), F32),
            shape((half, total), BF16),
            shape((half, total), BF16),
        ],
        (where, *tok_near, *tok_far, gate_mat, up_mat),
        0,
        "gates",
        scratch=[VMEM((total, total), F32)],
        limit=18,
        light=True,
    )
    def add(x, y):
        return (x.astype(F32) + y.astype(F32)).astype(BF16)

    def chip_swap(x, bit):
        return lax.ppermute(
            x, "cuts", [(2 * i + c, 2 * (i ^ bit) + c) for i in range(chips) for c in (0, 1)]
        )

    gram_sum = add(gram_keep, swap(gram_send))
    (first,) = call(
        functools.partial(own_hidden_kernel, chips),
        [shape((total, ff), F32)],
        (where, wt_in, wt_swap, down_mat),
        4 * total * width * ff,
        "own_hidden_grad",
        after=(hidden,),
        light=True,
    )
    wt_late, first = lax.optimization_barrier((wt_near[1:], first))
    wt_far = [wt_swap] + [swap(x) for x in wt_late]
    both, tail, relay_tail = call(
        functools.partial(hidden_kernel, chips),
        [
            shape((total, 2 * ff), BF16),
            shape((16, width), BF16),
            shape((16, width), BF16),
        ],
        (where, *wt_near[1:], *wt_far[1:], down_mat, first, hidden, act, slope),
        2 * total * (feats - 2 * width) * ff,
        "hidden_grad",
        scratch=[VMEM((total, ff), F32)],
    )

    def pieces(k, tail, after):
        keep, send = part(where, both, tail, gate_mat, up_mat, width, k, chips, after)
        return keep, swap(send)

    def total_of(*terms):
        return sum(x.astype(F32) for x in terms).astype(BF16)

    through = total_of(*pieces(2, relay_tail, ()))
    right = pieces(1, tail, ())
    left = pieces(chips - 1, tail, (through,))
    own = total_of(*pieces(0, tail, (through,)))
    top, low = hop(through[:mid], 1), hop(through[mid:], chips - 1)
    right = total_of(*right, jnp.pad(top, ((0, own.shape[0] - mid), (0, 0))))
    left = total_of(*left, jnp.pad(low, ((mid, 0), (0, 0))))
    sums = [own, hop(right, 1), hop(left, chips - 1)]
    gram_sum, _ = lax.optimization_barrier((gram_sum, left))
    gram_sum = add(gram_sum, chip_swap(gram_sum, 1))
    (payload,) = call(
        final_kernel,
        [shape((total, width + 128), BF16)],
        tuple(sums),
        0,
        "final",
        scalars=0,
        limit=8,
        after=(gram_sum,),
    )
    gram_sum, payload = lax.optimization_barrier((gram_sum, payload))
    gram_sum = add(gram_sum, chip_swap(gram_sum, 2))
    gram_other = swap(gram_sum)
    blocks = feats // BLOCK
    (stats,) = call(
        functools.partial(stats_kernel, chips),
        [shape((blocks, BLOCK // cuts, BLOCK), F32)],
        (where, *wt_near, *wt_far, gram_sum, gram_other),
        4 * total * total * feats // cuts + 2 * total * BLOCK * feats // cuts,
        "stats",
        scratch=[VMEM((total, feats), BF16), VMEM((total, total), BF16)],
        after=(payload,),
    )
    back = exchange(payload.reshape(experts, capacity, width + 128)).reshape(total, width + 128)
    input_grad, logit_grad = call(
        unpack_kernel,
        [shape((tok_rows, width), BF16), shape((1, tok_rows), F32)],
        (slot, logit, back),
        2 * tok_rows * total * (width + 128),
        "unpack",
        scalars=0,
    )
    return input_grad, logit_grad.reshape(tok_rows), stats[None]


def solution(mesh):
    return jax.shard_map(
        shards,
        mesh=mesh,
        in_specs=(
            P("expert", "cuts"),
            P("expert", "cuts"),
            P("expert"),
            P("expert", None),
            P("expert", None, "cuts"),
            P("expert", None, "cuts"),
            P("expert", "cuts", None),
        ),
        out_specs=(P("expert", "cuts"), P("expert"), P("expert", None, "cuts", None)),
        check_vma=False,
    )
```

time: 177 us -> 143 us (0.81)
  waiting for transfers between devices: 66.4 us -> 50.4 us
  Pallas kernels: 31.2 us -> 16.8 us
  blocking collectives: 26 us -> 34.3 us
  starting transfers between devices: 38.1 us -> 32.5 us
  local copies, waits for them, and re-layouts: 9.59 us -> 6.67 us
  other arithmetic: 2.91 us -> 0.69 us
    ppermute x18 -> x13, waiting for transfers between devices: 53.9 us -> 30.8 us  [hop(): lax.ppermute(x, 'cuts', [(2 * i + c, 2 * ((i + k) % chips) + c) for i in...]
    ppermute x0 -> x2, waiting for transfers between devices: none -> 10.2 us  [chip_swap(): lax.ppermute(x, 'cuts', [(2 * i + c, 2 * (i ^ bit) + c) for i in range(ch...]
    all_to_all x2 -> x1, starting transfers between devices: 14.6 us -> 5.24 us  [exchange(): return lax.all_to_all(x, 'expert', split_axis=0, concat_axis=0, tiled=True)]
    all_to_all x1, blocking collectives: 26 us -> 34.3 us  [exchange(): return lax.all_to_all(x, 'expert', split_axis=0, concat_axis=0, tiled=True)]
    pallas_call x4, Pallas kernels: 11.5 us -> 4.09 us  [part(): pl.pallas_call(part_kernel, out_shape=[out, out], grid_spec=pltpu.Prefetc...]
    pallas_call x7, Pallas kernels: 19.8 us -> 12.7 us  [the longest x6 11.3 us: call(): pl.pallas_call(kernel, out_shape=out, in_specs=specs, out_specs=[whole()]...]
    all_to_all x2 -> x1, waiting for transfers between devices: 9.84 us -> 2.93 us  [exchange(): return lax.all_to_all(x, 'expert', split_axis=0, concat_axis=0, tiled=True)]
    ppermute x15 -> x17, waiting for transfers between devices: 2.74 us -> 6.55 us  [swap(): return lax.ppermute(x, 'cuts', [(i, i ^ 1) for i in range(cuts)])]
  transfers between devices with their start and end apart: 35 -> 33, of which waited for: 15 -> 20; matrix products, arithmetic and copies ran while one was open for 2% -> 1% of each run, Pallas kernels for 12% -> 7%
where the time goes in v2:
time: 143 us; the launch traced here: 142 us
  waiting for transfers between devices  50.4 us (35%)
  blocking collectives  34.3 us (24%)
  starting transfers between devices  32.5 us (23%)
  Pallas kernels  16.8 us (12%)
  local copies, waits for them, and re-layouts  6.67 us (5%)
    all_to_all x1, blocking collectives, exchange(): return lax.all_to_all(x, 'expert', split_axis=0, concat_axis=0, tiled=True)  34.3 us
    ppermute x13, waiting for transfers between devices, hop(): lax.ppermute(x, 'cuts', [(2 * i + c, 2 * ((i + k) % chips) + c) for i in...  30.8 us
    ppermute x13, starting transfers between devices, hop(): lax.ppermute(x, 'cuts', [(2 * i + c, 2 * ((i + k) % chips) + c) for i in...  21.9 us
    pallas_call x6, Pallas kernels, call(): pl.pallas_call(kernel, out_shape=out, in_specs=specs, out_specs=[whole()]...  11.3 us
    ppermute x2, waiting for transfers between devices, chip_swap(): lax.ppermute(x, 'cuts', [(2 * i + c, 2 * (i ^ bit) + c) for i in range(ch...  10.2 us
    ppermute x17, waiting for transfers between devices, swap(): return lax.ppermute(x, 'cuts', [(i, i ^ 1) for i in range(cuts)])  6.55 us
    unnamed x46, local copies, waits for them, and re-layouts  6.51 us
    all_to_all x1, starting transfers between devices, exchange(): return lax.all_to_all(x, 'expert', split_axis=0, concat_axis=0, tiled=True)  5.24 us
  transfers between devices with their start and end apart: 33, of which 20 were waited for; matrix products, arithmetic and copies ran while one was open for 1% of the time, Pallas kernels for 7%

profile of v2, /device:TPU:32, one launch (start us, length us, event | category | flops | bytes accessed | tf_op | source)
XLA Modules:
  0.0 142.4 jit_solution(11148676399259497096)
XLA Ops:
  0.7 1.1 copy-done.18
  1.7 0.9 copy-done.19
  2.7 0.7 copy-done.20
  3.3 0.7 copy-done.22
  4.0 1.4 pack.1
  5.4 34.3 %all_to_all.10 = bf16[32,16,768]{2,1,0:T(8,128)(2,1)S(1)} all-to-all(bf16[32,16,768]{2,1,0:T(8,128)(2,1)S(1)} %bitcast.33), channel_id=1, replica_groups=mesh['expert'=32,'cuts'=8] {'expert'}, dimensions={0} | all-to-all | bytes 1572864 | tf_op jit(solution)/shard_map/all_to_all | solution.py:303
  39.8 2.8 %collective-permute-start.3 = (bf16[256,384]{1,0:T(8,128)(2,1)S(1)}, bf16[256,384]{1,0:T(8,128)(2,1)S(1)}, u32[]{:S(2)}, u32[]{:S(2)}) collective-permute-start(bf16[256,384]{1,0:T(8,128)(2,1)S(1)} %get-tuple-element.59), channel_id=1, source_target_pairs={{0,6},{1,7},{2,0},{3,1},{4,2},{5,3},{6,4},{7,5},{8,14},{9,15},{10,... | collective-permute-start | bytes 589832 | tf_op jit(solution)/shard_map/ppermute | solution.py:295
  42.6 3.2 %collective-permute-start.5 = (bf16[256,384]{1,0:T(8,128)(2,1)S(1)}, bf16[256,384]{1,0:T(8,128)(2,1)S(1)}, u32[]{:S(2)}, u32[]{:S(2)}) collective-permute-start(bf16[256,384]{1,0:T(8,128)(2,1)S(1)} %get-tuple-element.60), channel_id=1, source_target_pairs={{0,6},{1,7},{2,0},{3,1},{4,2},{5,3},{6,4},{7,5},{8,14},{9,15},{10,... | collective-permute-start | bytes 589832 | tf_op jit(solution)/shard_map/ppermute | solution.py:295
  45.8 1.3 collective-permute-done.3.refs_7_
  47.3 3.8 %collective-permute-start.4 = (bf16[256,384]{1,0:T(8,128)(2,1)S(1)}, bf16[256,384]{1,0:T(8,128)(2,1)S(1)}, u32[]{:S(2)}, u32[]{:S(2)}) collective-permute-start(bf16[256,384]{1,0:T(8,128)(2,1)S(1)} %collective-permute-done.3.refs_7_), channel_id=1, source_target_pairs={{0,6},{1,7},{2,0},{3,1},{4,2},{5,3},{6,4},{7,5},{8,14},{9,15},{10,... | collective-permute-start | bytes 589832 | tf_op jit(solution)/shard_map/ppermute | solution.py:295
  51.1 0.2 collective-permute-start.6
  51.3 0.3 collective-permute-start.8
  51.6 1.2 collective-permute-done.refs_2_
  52.7 0.5 collective-permute-start.7
  53.2 2.6 %collective-permute-done.4.refs_5_ = bf16[256,384]{1,0:T(8,128)(2,1)S(1)} collective-permute-done((bf16[256,384]{1,0:T(8,128)(2,1)S(1)}, bf16[256,384]{1,0:T(8,128)(2,1)S(1)}, u32[]{:S(2)}, u32[]{:S(2)}) %collective-permute-start.4) | collective-permute-done | bytes 196640 | tf_op jit(solution)/shard_map/ppermute | solution.py:295
  55.9 0.5 collective-permute-start.17
  56.4 3.7 %collective-permute-start.16 = (bf16[512,384]{1,0:T(8,128)(2,1)S(1)}, bf16[512,384]{1,0:T(8,128)(2,1)S(1)}, u32[]{:S(2)}, u32[]{:S(2)}) collective-permute-start(bf16[512,384]{1,0:T(8,128)(2,1)S(1)} %get-tuple-element.57.refs_1_), channel_id=1, source_target_pairs={{0,6},{1,7},{2,0},{3,1},{4,2},{5,3},{6,4},{7,5},{8,14},{9,15},{10,... | collective-permute-start | bytes 1179656 | tf_op jit(solution)/shard_map/ppermute | solution.py:295
  60.1 4.3 %collective-permute-done.2.refs_4_ = bf16[256,384]{1,0:T(8,128)(2,1)S(1)} collective-permute-done((bf16[256,384]{1,0:T(8,128)(2,1)S(1)}, bf16[256,384]{1,0:T(8,128)(2,1)S(1)}, u32[]{:S(2)}, u32[]{:S(2)}) %collective-permute-start.2) | collective-permute-done | bytes 196640 | tf_op jit(solution)/shard_map/ppermute | solution.py:295
  64.4 0.7 collective-permute-start.15
  65.1 1.9 %collective-permute-start.14 = (bf16[512,384]{1,0:T(8,128)(2,1)S(1)}, bf16[512,384]{1,0:T(8,128)(2,1)S(1)}, u32[]{:S(2)}, u32[]{:S(2)}) collective-permute-start(bf16[512,384]{1,0:T(8,128)(2,1)S(1)} %get-tuple-element.57.refs_1_), channel_id=1, source_target_pairs={{0,2},{1,3},{2,4},{3,5},{4,6},{5,7},{6,0},{7,1},{8,10},{9,11},{10,... | collective-permute-start | bytes 1179656 | tf_op jit(solution)/shard_map/ppermute | solution.py:295
  67.0 1.4 %collective-permute-done.9.refs_11_ = bf16[256,384]{1,0:T(8,128)(2,1)S(1)} collective-permute-done((bf16[256,384]{1,0:T(8,128)(2,1)S(1)}, bf16[256,384]{1,0:T(8,128)(2,1)S(1)}, u32[]{:S(2)}, u32[]{:S(2)}) %collective-permute-start.9) | collective-permute-done | bytes 196640 | tf_op jit(solution)/shard_map/ppermute | solution.py:300
  68.4 1.9 %copy-done.1 = bf16[1,3072,512]{2,1,0:T(8,128)(2,1)S(1)} copy-done((bf16[1,3072,512]{2,1,0:T(8,128)(2,1)S(1)}, bf16[1,3072,512]{2,1,0:T(8,128)(2,1)}, u32[]{:S(2)}) %copy-start.1) | copy-done | bytes 3145752
  70.3 4.1 %gates.1 = (bf16[512,512]{1,0:T(8,128)(2,1)S(1)}, f32[512,512]{1,0:T(8,128)S(1)}, f32[512,512]{1,0:T(8,128)S(1)}, bf16[256,512]{1,0:T(8,128)(2,1)S(1)}, bf16[256,512]{1,0:T(8,128)(2,1)S(1)}) custom-call(s32[1]{0:T(128)} %bitcast.cut_ref.refs_0_, bf16[512,384]{1,0:T(8,128)(2,1)S(1)} %get-tuple-element.58.refs_1_, ...), custom_call_target="tpu_custom_call" | custom-call | tf_op jit(solution)/shard_map/gates/pallas_call | solution.py:45
  74.4 0.6 own_hidden_grad.1.refs_8_
  75.1 2.1 %collective-permute-done.16.refs_3_.refs_4_ = bf16[512,384]{1,0:T(8,128)(2,1)S(1)} collective-permute-done((bf16[512,384]{1,0:T(8,128)(2,1)S(1)}, bf16[512,384]{1,0:T(8,128)(2,1)S(1)}, u32[]{:S(2)}, u32[]{:S(2)}) %collective-permute-start.16) | collective-permute-done | bytes 393248 | tf_op jit(solution)/shard_map/ppermute | solution.py:295
  77.2 0.8 collective-permute-done.15.refs_2_.refs_3_
  77.9 6.4 %collective-permute-done.14.refs_1_.refs_2_ = bf16[512,384]{1,0:T(8,128)(2,1)S(1)} collective-permute-done((bf16[512,384]{1,0:T(8,128)(2,1)S(1)}, bf16[512,384]{1,0:T(8,128)(2,1)S(1)}, u32[]{:S(2)}, u32[]{:S(2)}) %collective-permute-start.14) | collective-permute-done | bytes 393248 | tf_op jit(solution)/shard_map/ppermute | solution.py:295
  84.3 0.5 collective-permute-start.19
  84.8 1.2 collective-permute-done.18.refs_4_.refs_6_
  86.0 0.6 collective-permute-done.19.refs_5_.refs_7_
  86.6 0.6 collective-permute-done.20.refs_6_.refs_8_
  87.2 1.8 %hidden_grad.1 = (bf16[512,1024]{1,0:T(8,128)(2,1)S(1)}, bf16[16,384]{1,0:T(8,128)(2,1)S(1)}, bf16[16,384]{1,0:T(8,128)(2,1)S(1)}) custom-call(s32[1]{0:T(128)} %bitcast.cut_ref.refs_0_, bf16[512,384]{1,0:T(8,128)(2,1)S(1)} %collective-permute-done.14.refs_1_.refs_2_, bf16[512,384]{1,0:T(8,128)(2,1)S(1)} %collective-permute-done.15.refs_2_.refs_3_, ...), custom_call_target="tpu_custom_call" | custom-call | flops 1207959552 | bytes 10248196 | tf_op jit(solution)/shard_map/hidden_grad/pallas_call | solution.py:45
  89.0 0.2 copy-done.2
  89.2 1.0 input_part.4
  90.2 0.2 collective-permute-start.21
  90.5 0.4 collective-permute-start.13
  90.8 1.2 collective-permute-done.21
  92.1 0.1 add_convert_fusion.3.refs_0_
  92.2 1.0 input_part.5
  93.2 0.2 collective-permute-start.22
  93.4 1.0 input_part.7
  94.5 0.5 collective-permute-start.26
  94.9 0.9 collective-permute-start.23
  95.9 1.5 %collective-permute-start.27 = (bf16[256,384]{1,0:T(8,128)(2,1)S(1)}, bf16[256,384]{1,0:T(8,128)(2,1)S(1)}, u32[]{:S(2)}, u32[]{:S(2)}) collective-permute-start(bf16[256,384]{1,0:T(8,128)(2,1)S(1)} %slice.33), channel_id=1, source_target_pairs={{0,2},{1,3},{2,4},{3,5},{4,6},{5,7},{6,0},{7,1},{8,10},{9,11},{10,... | collective-permute-start | bytes 589832 | tf_op jit(solution)/shard_map/ppermute | solution.py:295
  97.5 1.0 input_part.6
  98.6 3.7 %collective-permute-done.23 = bf16[272,384]{1,0:T(8,128)(2,1)S(1)} collective-permute-done((bf16[272,384]{1,0:T(8,128)(2,1)S(1)}, bf16[272,384]{1,0:T(8,128)(2,1)S(1)}, u32[]{:S(2)}, u32[]{:S(2)}) %collective-permute-start.23) | collective-permute-done | bytes 208928 | tf_op jit(solution)/shard_map/ppermute | solution.py:295
  102.2 0.1 add_convert_fusion.2
  102.5 1.6 %collective-permute-done.27 = bf16[256,384]{1,0:T(8,128)(2,1)S(1)} collective-permute-done((bf16[256,384]{1,0:T(8,128)(2,1)S(1)}, bf16[256,384]{1,0:T(8,128)(2,1)S(1)}, u32[]{:S(2)}, u32[]{:S(2)}) %collective-permute-start.27) | collective-permute-done | bytes 196640 | tf_op jit(solution)/shard_map/ppermute | solution.py:295
  104.1 0.1 add_convert_fusion
  104.3 0.5 collective-permute-start.28
  104.8 2.8 %collective-permute-start.29 = (bf16[528,384]{1,0:T(8,128)(2,1)S(1)}, bf16[528,384]{1,0:T(8,128)(2,1)S(1)}, u32[]{:S(2)}, u32[]{:S(2)}) collective-permute-start(bf16[528,384]{1,0:T(8,128)(2,1)S(1)} %add_convert_fusion.2), channel_id=1, source_target_pairs={{0,6},{1,7},{2,0},{3,1},{4,2},{5,3},{6,4},{7,5},{8,14},{9,15},{10,... | collective-permute-start | bytes 1216520 | tf_op jit(solution)/shard_map/ppermute | solution.py:295
  107.6 0.1 add_convert_fusion.1.refs_0_
  107.7 4.0 %collective-permute-done.24 = bf16[256,512]{1,0:T(8,128)(2,1)S(1)} collective-permute-done((bf16[256,512]{1,0:T(8,128)(2,1)S(1)}, bf16[256,512]{1,0:T(8,128)(2,1)S(1)}, u32[]{:S(2)}, u32[]{:S(2)}) %collective-permute-start.24) | collective-permute-done | bytes 262176 | tf_op jit(solution)/shard_map/ppermute | solution.py:355
  111.8 4.7 %collective-permute-done.28.refs_1_ = bf16[528,384]{1,0:T(8,128)(2,1)S(1)} collective-permute-done((bf16[528,384]{1,0:T(8,128)(2,1)S(1)}, bf16[528,384]{1,0:T(8,128)(2,1)S(1)}, u32[]{:S(2)}, u32[]{:S(2)}) %collective-permute-start.28) | collective-permute-done | bytes 405536 | tf_op jit(solution)/shard_map/ppermute | solution.py:295
  116.5 2.2 %collective-permute-done.29.refs_2_ = bf16[528,384]{1,0:T(8,128)(2,1)S(1)} collective-permute-done((bf16[528,384]{1,0:T(8,128)(2,1)S(1)}, bf16[528,384]{1,0:T(8,128)(2,1)S(1)}, u32[]{:S(2)}, u32[]{:S(2)}) %collective-permute-start.29) | collective-permute-done | bytes 405536 | tf_op jit(solution)/shard_map/ppermute | solution.py:295
  118.7 1.1 final.1.refs_11_
  119.8 5.2 %all-to-all-start.1 = ((bf16[32,16,512]{2,1,0:T(8,128)(2,1)}), bf16[32,16,512]{2,1,0:T(8,128)(2,1)S(1)}, u32[]{:S(2)}, u32[]{:S(2)}) async-start(bf16[32,16,512]{2,1,0:T(8,128)(2,1)} %bitcast.8), calls=%async_computation.1 | async-start | bytes 1048576 | tf_op jit(solution)/shard_map/all_to_all | solution.py:303
  125.1 1.8 %collective-permute-start.30 = (bf16[256,512]{1,0:T(8,128)(2,1)S(1)}, bf16[256,512]{1,0:T(8,128)(2,1)S(1)}, u32[]{:S(2)}, u32[]{:S(2)}) collective-permute-start(bf16[256,512]{1,0:T(8,128)(2,1)S(1)} %add_convert_fusion.5.refs_3_), channel_id=1, source_target_pairs={{0,4},{1,5},{2,6},{3,7},{4,0},{5,1},{6,2},{7,3},{8,12},{9,13},{10,... | collective-permute-start | bytes 786440 | tf_op jit(solution)/shard_map/ppermute | solution.py:355
  126.9 6.2 %collective-permute-done.30 = bf16[256,512]{1,0:T(8,128)(2,1)S(1)} collective-permute-done((bf16[256,512]{1,0:T(8,128)(2,1)S(1)}, bf16[256,512]{1,0:T(8,128)(2,1)S(1)}, u32[]{:S(2)}, u32[]{:S(2)}) %collective-permute-start.30) | collective-permute-done | bytes 262176 | tf_op jit(solution)/shard_map/ppermute | solution.py:355
  133.2 1.5 %collective-permute-done.31.refs_10_ = bf16[256,512]{1,0:T(8,128)(2,1)S(1)} collective-permute-done((bf16[256,512]{1,0:T(8,128)(2,1)S(1)}, bf16[256,512]{1,0:T(8,128)(2,1)S(1)}, u32[]{:S(2)}, u32[]{:S(2)}) %collective-permute-start.31) | collective-permute-done | bytes 262176 | tf_op jit(solution)/shard_map/ppermute | solution.py:300
  134.8 1.0 copy-done.17
  135.8 2.5 %stats.1 = f32[3,128,1024]{2,1,0:T(8,128)} custom-call(s32[1]{0:T(128)} %bitcast.cut_ref.refs_0_, bf16[512,384]{1,0:T(8,128)(2,1)S(1)} %get-tuple-element.57.refs_1_, bf16[512,384]{1,0:T(8,128)(2,1)S(1)} %copy-done.9, bf16[512,384]{1,0:T(8,128)(2,1)S(1)} %copy-done.7, bf16[512,384]{1,0:T(8,128)(2,1)S(1)} %copy-done.5, bf16[512,384]{1,0:T(8,128)(2,1)S(1)} %copy-done.17, ...), custom_call_target="tpu_custom_call" | custom-call | flops 805306368 | bytes 5242884 | tf_op jit(solution)/shard_map/stats/pallas_call | solution.py:45
  138.3 2.9 %all-to-all-done.1 = bf16[32,16,512]{2,1,0:T(8,128)(2,1)S(1)} async-done(((bf16[32,16,512]{2,1,0:T(8,128)(2,1)}), bf16[32,16,512]{2,1,0:T(8,128)(2,1)S(1)}, u32[]{:S(2)}, u32[]{:S(2)}) %all-to-all-start.1) | async-done | bytes 524320 | tf_op jit(solution)/shard_map/all_to_all | solution.py:303
  141.3 1.2 unpack.1
  (71 shorter events, 0.8 us)
Async XLA Ops:
  0.6 67.8 %copy-start = (bf16[1,3072,512]{2,1,0:T(8,128)(2,1)S(1)}, bf16[1,3072,512]{2,1,0:T(8,128)(2,1)}, u32[]{:S(2)}) copy-start(bf16[1,3072,512]{2,1,0:T(8,128)(2,1)} %param.11) | copy-start | bytes 9437188
  0.6 1.1 copy-start.18
  1.7 0.9 copy-start.19
  2.7 0.7 copy-start.20
  3.3 0.7 copy-start.22
  39.8 7.4 %collective-permute-start.3 = (bf16[256,384]{1,0:T(8,128)(2,1)S(1)}, bf16[256,384]{1,0:T(8,128)(2,1)S(1)}, u32[]{:S(2)}, u32[]{:S(2)}) collective-permute-start(bf16[256,384]{1,0:T(8,128)(2,1)S(1)} %get-tuple-element.59), channel_id=1, source_target_pairs={{0,6},{1,7},{2,0},{3,1},{4,2},{5,3},{6,4},{7,5},{8,14},{9,15},{10,... | collective-permute-start | bytes 589832 | tf_op jit(solution)/shard_map/ppermute | solution.py:295
  42.6 8.4 %collective-permute-start.1 = (bf16[256,384]{1,0:T(8,128)(2,1)S(1)}, bf16[256,384]{1,0:T(8,128)(2,1)S(1)}, u32[]{:S(2)}, u32[]{:S(2)}) collective-permute-start(bf16[256,384]{1,0:T(8,128)(2,1)S(1)} %get-tuple-element.59), channel_id=1, source_target_pairs={{0,2},{1,3},{2,4},{3,5},{4,6},{5,7},{6,0},{7,1},{8,10},{9,11},{10,... | collective-permute-start | bytes 589832 | tf_op jit(solution)/shard_map/ppermute | solution.py:295
  42.6 8.7 %collective-permute-start.5 = (bf16[256,384]{1,0:T(8,128)(2,1)S(1)}, bf16[256,384]{1,0:T(8,128)(2,1)S(1)}, u32[]{:S(2)}, u32[]{:S(2)}) collective-permute-start(bf16[256,384]{1,0:T(8,128)(2,1)S(1)} %get-tuple-element.60), channel_id=1, source_target_pairs={{0,6},{1,7},{2,0},{3,1},{4,2},{5,3},{6,4},{7,5},{8,14},{9,15},{10,... | collective-permute-start | bytes 589832 | tf_op jit(solution)/shard_map/ppermute | solution.py:295
  45.8 6.9 %collective-permute-start = (bf16[256,384]{1,0:T(8,128)(2,1)S(1)}, bf16[256,384]{1,0:T(8,128)(2,1)S(1)}, u32[]{:S(2)}, u32[]{:S(2)}) collective-permute-start(bf16[256,384]{1,0:T(8,128)(2,1)S(1)} %get-tuple-element.60), channel_id=1, source_target_pairs={{0,2},{1,3},{2,4},{3,5},{4,6},{5,7},{6,0},{7,1},{8,10},{9,11},{10,... | collective-permute-start | bytes 589832 | tf_op jit(solution)/shard_map/ppermute | solution.py:295
  47.2 5.5 %collective-permute-start.12 = (bf16[256,384]{1,0:T(8,128)(2,1)S(1)}, bf16[256,384]{1,0:T(8,128)(2,1)S(1)}, u32[]{:S(2)}, u32[]{:S(2)}) collective-permute-start(bf16[256,384]{1,0:T(8,128)(2,1)S(1)} %collective-permute-done.3.refs_7_), channel_id=1, source_target_pairs={{0,1},{1,0},{2,3},{3,2},{4,5},{5,4},{6,7},{7,6},{8,9},{9,8},{10,11... | collective-permute-start | bytes 589832 | tf_op jit(solution)/shard_map/ppermute | solution.py:300
  47.3 8.6 %collective-permute-start.4 = (bf16[256,384]{1,0:T(8,128)(2,1)S(1)}, bf16[256,384]{1,0:T(8,128)(2,1)S(1)}, u32[]{:S(2)}, u32[]{:S(2)}) collective-permute-start(bf16[256,384]{1,0:T(8,128)(2,1)S(1)} %collective-permute-done.3.refs_7_), channel_id=1, source_target_pairs={{0,6},{1,7},{2,0},{3,1},{4,2},{5,3},{6,4},{7,5},{8,14},{9,15},{10,... | collective-permute-start | bytes 589832 | tf_op jit(solution)/shard_map/ppermute | solution.py:295
  51.1 14.0 %collective-permute-start.6 = (bf16[512,384]{1,0:T(8,128)(2,1)S(1)}, bf16[512,384]{1,0:T(8,128)(2,1)S(1)}, u32[]{:S(2)}, u32[]{:S(2)}) collective-permute-start(bf16[512,384]{1,0:T(8,128)(2,1)S(1)} %get-tuple-element.58.refs_1_), channel_id=1, source_target_pairs={{0,1},{1,0},{2,3},{3,2},{4,5},{5,4},{6,7},{7,6},{8,9},{9,8},{10,11... | collective-permute-start | bytes 1179656 | tf_op jit(solution)/shard_map/ppermute | solution.py:300
  51.3 4.6 %collective-permute-start.8 = (bf16[256,384]{1,0:T(8,128)(2,1)S(1)}, bf16[256,384]{1,0:T(8,128)(2,1)S(1)}, u32[]{:S(2)}, u32[]{:S(2)}) collective-permute-start(bf16[256,384]{1,0:T(8,128)(2,1)S(1)} %collective-permute-done.1.refs_3_), channel_id=1, source_target_pairs={{0,1},{1,0},{2,3},{3,2},{4,5},{5,4},{6,7},{7,6},{8,9},{9,8},{10,11... | collective-permute-start | bytes 589832 | tf_op jit(solution)/shard_map/ppermute | solution.py:300
  52.7 3.2 %collective-permute-start.11 = (bf16[256,384]{1,0:T(8,128)(2,1)S(1)}, bf16[256,384]{1,0:T(8,128)(2,1)S(1)}, u32[]{:S(2)}, u32[]{:S(2)}) collective-permute-start(bf16[256,384]{1,0:T(8,128)(2,1)S(1)} %collective-permute-done.5.refs_6_), channel_id=1, source_target_pairs={{0,1},{1,0},{2,3},{3,2},{4,5},{5,4},{6,7},{7,6},{8,9},{9,8},{10,11... | collective-permute-start | bytes 589832 | tf_op jit(solution)/shard_map/ppermute | solution.py:300
  52.7 3.7 %collective-permute-start.7 = (bf16[256,384]{1,0:T(8,128)(2,1)S(1)}, bf16[256,384]{1,0:T(8,128)(2,1)S(1)}, u32[]{:S(2)}, u32[]{:S(2)}) collective-permute-start(bf16[256,384]{1,0:T(8,128)(2,1)S(1)} %collective-permute-done.refs_2_), channel_id=1, source_target_pairs={{0,1},{1,0},{2,3},{3,2},{4,5},{5,4},{6,7},{7,6},{8,9},{9,8},{10,11... | collective-permute-start | bytes 589832 | tf_op jit(solution)/shard_map/ppermute | solution.py:300
  55.9 8.5 %collective-permute-start.2 = (bf16[256,384]{1,0:T(8,128)(2,1)S(1)}, bf16[256,384]{1,0:T(8,128)(2,1)S(1)}, u32[]{:S(2)}, u32[]{:S(2)}) collective-permute-start(bf16[256,384]{1,0:T(8,128)(2,1)S(1)} %collective-permute-done.refs_2_), channel_id=1, source_target_pairs={{0,2},{1,3},{2,4},{3,5},{4,6},{5,7},{6,0},{7,1},{8,10},{9,11},{10,... | collective-permute-start | bytes 589832 | tf_op jit(solution)/shard_map/ppermute | solution.py:295
  55.9 11.1 %collective-permute-start.10 = (bf16[256,384]{1,0:T(8,128)(2,1)S(1)}, bf16[256,384]{1,0:T(8,128)(2,1)S(1)}, u32[]{:S(2)}, u32[]{:S(2)}) collective-permute-start(bf16[256,384]{1,0:T(8,128)(2,1)S(1)} %collective-permute-done.4.refs_5_), channel_id=1, source_target_pairs={{0,1},{1,0},{2,3},{3,2},{4,5},{5,4},{6,7},{7,6},{8,9},{9,8},{10,11... | collective-permute-start | bytes 589832 | tf_op jit(solution)/shard_map/ppermute | solution.py:300
  55.9 18.5 %collective-permute-start.17 = (bf16[512,384]{1,0:T(8,128)(2,1)S(1)}, bf16[512,384]{1,0:T(8,128)(2,1)S(1)}, u32[]{:S(2)}, u32[]{:S(2)}) collective-permute-start(bf16[512,384]{1,0:T(8,128)(2,1)S(1)} %get-tuple-element.57.refs_1_), channel_id=1, source_target_pairs={{0,1},{1,0},{2,3},{3,2},{4,5},{5,4},{6,7},{7,6},{8,9},{9,8},{10,11... | collective-permute-start | bytes 1179656 | tf_op jit(solution)/shard_map/ppermute | solution.py:300
  56.4 20.8 %collective-permute-start.16 = (bf16[512,384]{1,0:T(8,128)(2,1)S(1)}, bf16[512,384]{1,0:T(8,128)(2,1)S(1)}, u32[]{:S(2)}, u32[]{:S(2)}) collective-permute-start(bf16[512,384]{1,0:T(8,128)(2,1)S(1)} %get-tuple-element.57.refs_1_), channel_id=1, source_target_pairs={{0,6},{1,7},{2,0},{3,1},{4,2},{5,3},{6,4},{7,5},{8,14},{9,15},{10,... | collective-permute-start | bytes 1179656 | tf_op jit(solution)/shard_map/ppermute | solution.py:295
  64.4 13.6 %collective-permute-start.15 = (bf16[512,384]{1,0:T(8,128)(2,1)S(1)}, bf16[512,384]{1,0:T(8,128)(2,1)S(1)}, u32[]{:S(2)}, u32[]{:S(2)}) collective-permute-start(bf16[512,384]{1,0:T(8,128)(2,1)S(1)} %get-tuple-element.57.refs_1_), channel_id=1, source_target_pairs={{0,4},{1,5},{2,6},{3,7},{4,0},{5,1},{6,2},{7,3},{8,12},{9,13},{10,... | collective-permute-start | bytes 1179656 | tf_op jit(solution)/shard_map/ppermute | solution.py:295
  65.1 19.2 %collective-permute-start.14 = (bf16[512,384]{1,0:T(8,128)(2,1)S(1)}, bf16[512,384]{1,0:T(8,128)(2,1)S(1)}, u32[]{:S(2)}, u32[]{:S(2)}) collective-permute-start(bf16[512,384]{1,0:T(8,128)(2,1)S(1)} %get-tuple-element.57.refs_1_), channel_id=1, source_target_pairs={{0,2},{1,3},{2,4},{3,5},{4,6},{5,7},{6,0},{7,1},{8,10},{9,11},{10,... | collective-permute-start | bytes 1179656 | tf_op jit(solution)/shard_map/ppermute | solution.py:295
  67.0 1.4 %collective-permute-start.9 = (bf16[256,384]{1,0:T(8,128)(2,1)S(1)}, bf16[256,384]{1,0:T(8,128)(2,1)S(1)}, u32[]{:S(2)}, u32[]{:S(2)}) collective-permute-start(bf16[256,384]{1,0:T(8,128)(2,1)S(1)} %collective-permute-done.2.refs_4_), channel_id=1, source_target_pairs={{0,1},{1,0},{2,3},{3,2},{4,5},{5,4},{6,7},{7,6},{8,9},{9,8},{10,11... | collective-permute-start | bytes 589832 | tf_op jit(solution)/shard_map/ppermute | solution.py:300
  68.4 1.9 %copy-start.1 = (bf16[1,3072,512]{2,1,0:T(8,128)(2,1)S(1)}, bf16[1,3072,512]{2,1,0:T(8,128)(2,1)}, u32[]{:S(2)}) copy-start(bf16[1,3072,512]{2,1,0:T(8,128)(2,1)} %param.12) | copy-start | bytes 9437188
  70.3 4.1 %copy-start.3 = (bf16[1,512,3072]{2,1,0:T(8,128)(2,1)S(1)}, bf16[1,512,3072]{2,1,0:T(8,128)(2,1)}, u32[]{:S(2)}) copy-start(bf16[1,512,3072]{2,1,0:T(8,128)(2,1)} %param.13) | copy-start | bytes 9437188
  74.4 14.5 %copy-start.16 = (bf16[512,384]{1,0:T(8,128)(2,1)}, bf16[512,384]{1,0:T(8,128)(2,1)S(1)}, u32[]{:S(2)}) copy-start(bf16[512,384]{1,0:T(8,128)(2,1)S(1)} %collective-permute-done.17.refs_2_.refs_5_) | copy-start | bytes 1179652
  77.2 11.8 %copy-start.4 = (bf16[512,384]{1,0:T(8,128)(2,1)}, bf16[512,384]{1,0:T(8,128)(2,1)S(1)}, u32[]{:S(2)}) copy-start(bf16[512,384]{1,0:T(8,128)(2,1)S(1)} %collective-permute-done.16.refs_3_.refs_4_) | copy-start | bytes 1179652
  77.9 11.0 %copy-start.6 = (bf16[512,384]{1,0:T(8,128)(2,1)}, bf16[512,384]{1,0:T(8,128)(2,1)S(1)}, u32[]{:S(2)}) copy-start(bf16[512,384]{1,0:T(8,128)(2,1)S(1)} %collective-permute-done.15.refs_2_.refs_3_) | copy-start | bytes 1179652
  84.3 4.7 %copy-start.8 = (bf16[512,384]{1,0:T(8,128)(2,1)}, bf16[512,384]{1,0:T(8,128)(2,1)S(1)}, u32[]{:S(2)}) copy-start(bf16[512,384]{1,0:T(8,128)(2,1)S(1)} %collective-permute-done.14.refs_1_.refs_2_) | copy-start | bytes 1179652
  84.3 1.7 %collective-permute-start.18 = (bf16[512,384]{1,0:T(8,128)(2,1)S(1)}, bf16[512,384]{1,0:T(8,128)(2,1)S(1)}, u32[]{:S(2)}, u32[]{:S(2)}) collective-permute-start(bf16[512,384]{1,0:T(8,128)(2,1)S(1)} %collective-permute-done.14.refs_1_.refs_2_), channel_id=1, source_target_pairs={{0,1},{1,0},{2,3},{3,2},{4,5},{5,4},{6,7},{7,6},{8,9},{9,8},{10,11... | collective-permute-start | bytes 1179656 | tf_op jit(solution)/shard_map/ppermute | solution.py:300
  84.3 2.3 %collective-permute-start.19 = (bf16[512,384]{1,0:T(8,128)(2,1)S(1)}, bf16[512,384]{1,0:T(8,128)(2,1)S(1)}, u32[]{:S(2)}, u32[]{:S(2)}) collective-permute-start(bf16[512,384]{1,0:T(8,128)(2,1)S(1)} %collective-permute-done.15.refs_2_.refs_3_), channel_id=1, source_target_pairs={{0,1},{1,0},{2,3},{3,2},{4,5},{5,4},{6,7},{7,6},{8,9},{9,8},{10,11... | collective-permute-start | bytes 1179656 | tf_op jit(solution)/shard_map/ppermute | solution.py:300
  84.8 2.3 %collective-permute-start.20 = (bf16[512,384]{1,0:T(8,128)(2,1)S(1)}, bf16[512,384]{1,0:T(8,128)(2,1)S(1)}, u32[]{:S(2)}, u32[]{:S(2)}) collective-permute-start(bf16[512,384]{1,0:T(8,128)(2,1)S(1)} %collective-permute-done.16.refs_3_.refs_4_), channel_id=1, source_target_pairs={{0,1},{1,0},{2,3},{3,2},{4,5},{5,4},{6,7},{7,6},{8,9},{9,8},{10,11... | collective-permute-start | bytes 1179656 | tf_op jit(solution)/shard_map/ppermute | solution.py:300
  86.0 2.9 %copy-start.10 = (bf16[512,384]{1,0:T(8,128)(2,1)}, bf16[512,384]{1,0:T(8,128)(2,1)S(1)}, u32[]{:S(2)}) copy-start(bf16[512,384]{1,0:T(8,128)(2,1)S(1)} %collective-permute-done.18.refs_4_.refs_6_) | copy-start | bytes 1179652
  86.6 2.4 %copy-start.12 = (bf16[512,384]{1,0:T(8,128)(2,1)}, bf16[512,384]{1,0:T(8,128)(2,1)S(1)}, u32[]{:S(2)}) copy-start(bf16[512,384]{1,0:T(8,128)(2,1)S(1)} %collective-permute-done.19.refs_5_.refs_7_) | copy-start | bytes 1179652
  87.2 1.8 %copy-start.14 = (bf16[512,384]{1,0:T(8,128)(2,1)}, bf16[512,384]{1,0:T(8,128)(2,1)S(1)}, u32[]{:S(2)}) copy-start(bf16[512,384]{1,0:T(8,128)(2,1)S(1)} %collective-permute-done.20.refs_6_.refs_8_) | copy-start | bytes 1179652
  87.2 2.0 %copy-start.2 = (bf16[1,3072,512]{2,1,0:T(8,128)(2,1)S(1)}, bf16[1,3072,512]{2,1,0:T(8,128)(2,1)}, u32[]{:S(2)}) copy-start(bf16[1,3072,512]{2,1,0:T(8,128)(2,1)} %param.12) | copy-start | bytes 9437188
  90.2 1.8 %collective-permute-start.21 = (bf16[528,384]{1,0:T(8,128)(2,1)S(1)}, bf16[528,384]{1,0:T(8,128)(2,1)S(1)}, u32[]{:S(2)}, u32[]{:S(2)}) collective-permute-start(bf16[528,384]{1,0:T(8,128)(2,1)S(1)} %get-tuple-element.45), channel_id=1, source_target_pairs={{0,1},{1,0},{2,3},{3,2},{4,5},{5,4},{6,7},{7,6},{8,9},{9,8},{10,11... | collective-permute-start | bytes 1216520 | tf_op jit(solution)/shard_map/ppermute | solution.py:300
  90.5 5.3 %collective-permute-start.13 = (bf16[256,512]{1,0:T(8,128)(2,1)S(1)}, bf16[256,512]{1,0:T(8,128)(2,1)S(1)}, u32[]{:S(2)}, u32[]{:S(2)}) collective-permute-start(bf16[256,512]{1,0:T(8,128)(2,1)S(1)} %get-tuple-element.33), channel_id=1, source_target_pairs={{0,1},{1,0},{2,3},{3,2},{4,5},{5,4},{6,7},{7,6},{8,9},{9,8},{10,11... | collective-permute-start | bytes 786440 | tf_op jit(solution)/shard_map/ppermute | solution.py:300
  93.2 9.0 %collective-permute-start.22 = (bf16[528,384]{1,0:T(8,128)(2,1)S(1)}, bf16[528,384]{1,0:T(8,128)(2,1)S(1)}, u32[]{:S(2)}, u32[]{:S(2)}) collective-permute-start(bf16[528,384]{1,0:T(8,128)(2,1)S(1)} %get-tuple-element.47), channel_id=1, source_target_pairs={{0,1},{1,0},{2,3},{3,2},{4,5},{5,4},{6,7},{7,6},{8,9},{9,8},{10,11... | collective-permute-start | bytes 1216520 | tf_op jit(solution)/shard_map/ppermute | solution.py:300
  94.5 8.0 %collective-permute-start.26 = (bf16[528,384]{1,0:T(8,128)(2,1)S(1)}, bf16[528,384]{1,0:T(8,128)(2,1)S(1)}, u32[]{:S(2)}, u32[]{:S(2)}) collective-permute-start(bf16[528,384]{1,0:T(8,128)(2,1)S(1)} %get-tuple-element.52), channel_id=1, source_target_pairs={{0,1},{1,0},{2,3},{3,2},{4,5},{5,4},{6,7},{7,6},{8,9},{9,8},{10,11... | collective-permute-start | bytes 1216520 | tf_op jit(solution)/shard_map/ppermute | solution.py:300
  94.9 7.3 %collective-permute-start.23 = (bf16[272,384]{1,0:T(8,128)(2,1)S(1)}, bf16[272,384]{1,0:T(8,128)(2,1)S(1)}, u32[]{:S(2)}, u32[]{:S(2)}) collective-permute-start(bf16[272,384]{1,0:T(8,128)(2,1)S(1)} %slice.32), channel_id=1, source_target_pairs={{0,6},{1,7},{2,0},{3,1},{4,2},{5,3},{6,4},{7,5},{8,14},{9,15},{10,... | collective-permute-start | bytes 626696 | tf_op jit(solution)/shard_map/ppermute | solution.py:295
  95.9 8.2 %collective-permute-start.27 = (bf16[256,384]{1,0:T(8,128)(2,1)S(1)}, bf16[256,384]{1,0:T(8,128)(2,1)S(1)}, u32[]{:S(2)}, u32[]{:S(2)}) collective-permute-start(bf16[256,384]{1,0:T(8,128)(2,1)S(1)} %slice.33), channel_id=1, source_target_pairs={{0,2},{1,3},{2,4},{3,5},{4,6},{5,7},{6,0},{7,1},{8,10},{9,11},{10,... | collective-permute-start | bytes 589832 | tf_op jit(solution)/shard_map/ppermute | solution.py:295
  98.5 9.1 %collective-permute-start.25 = (bf16[528,384]{1,0:T(8,128)(2,1)S(1)}, bf16[528,384]{1,0:T(8,128)(2,1)S(1)}, u32[]{:S(2)}, u32[]{:S(2)}) collective-permute-start(bf16[528,384]{1,0:T(8,128)(2,1)S(1)} %get-tuple-element.50), channel_id=1, source_target_pairs={{0,1},{1,0},{2,3},{3,2},{4,5},{5,4},{6,7},{7,6},{8,9},{9,8},{10,11... | collective-permute-start | bytes 1216520 | tf_op jit(solution)/shard_map/ppermute | solution.py:300
  102.4 9.3 %collective-permute-start.24 = (bf16[256,512]{1,0:T(8,128)(2,1)S(1)}, bf16[256,512]{1,0:T(8,128)(2,1)S(1)}, u32[]{:S(2)}, u32[]{:S(2)}) collective-permute-start(bf16[256,512]{1,0:T(8,128)(2,1)S(1)} %add_convert_fusion.6), channel_id=1, source_target_pairs={{0,2},{1,3},{2,0},{3,1},{4,6},{5,7},{6,4},{7,5},{8,10},{9,11},{10,... | collective-permute-start | bytes 786440 | tf_op jit(solution)/shard_map/ppermute | solution.py:355
  104.2 30.5 %copy-start.5 = (bf16[512,384]{1,0:T(8,128)(2,1)S(1)}, bf16[512,384]{1,0:T(8,128)(2,1)}, u32[]{:S(2)}) copy-start(bf16[512,384]{1,0:T(8,128)(2,1)} %copy-done.4) | copy-start | bytes 1179652
  104.2 30.5 %copy-start.7 = (bf16[512,384]{1,0:T(8,128)(2,1)S(1)}, bf16[512,384]{1,0:T(8,128)(2,1)}, u32[]{:S(2)}) copy-start(bf16[512,384]{1,0:T(8,128)(2,1)} %copy-done.6) | copy-start | bytes 1179652
  104.2 30.5 %copy-start.9 = (bf16[512,384]{1,0:T(8,128)(2,1)S(1)}, bf16[512,384]{1,0:T(8,128)(2,1)}, u32[]{:S(2)}) copy-start(bf16[512,384]{1,0:T(8,128)(2,1)} %copy-done.8) | copy-start | bytes 1179652
  104.2 30.5 %copy-start.11 = (bf16[512,384]{1,0:T(8,128)(2,1)S(1)}, bf16[512,384]{1,0:T(8,128)(2,1)}, u32[]{:S(2)}) copy-start(bf16[512,384]{1,0:T(8,128)(2,1)} %copy-done.10) | copy-start | bytes 1179652
  104.3 30.5 %copy-start.13 = (bf16[512,384]{1,0:T(8,128)(2,1)S(1)}, bf16[512,384]{1,0:T(8,128)(2,1)}, u32[]{:S(2)}) copy-start(bf16[512,384]{1,0:T(8,128)(2,1)} %copy-done.12) | copy-start | bytes 1179652
  104.3 30.5 %copy-start.15 = (bf16[512,384]{1,0:T(8,128)(2,1)S(1)}, bf16[512,384]{1,0:T(8,128)(2,1)}, u32[]{:S(2)}) copy-start(bf16[512,384]{1,0:T(8,128)(2,1)} %copy-done.14) | copy-start | bytes 1179652
  104.3 12.2 %collective-permute-start.28 = (bf16[528,384]{1,0:T(8,128)(2,1)S(1)}, bf16[528,384]{1,0:T(8,128)(2,1)S(1)}, u32[]{:S(2)}, u32[]{:S(2)}) collective-permute-start(bf16[528,384]{1,0:T(8,128)(2,1)S(1)} %add_convert_fusion), channel_id=1, source_target_pairs={{0,2},{1,3},{2,4},{3,5},{4,6},{5,7},{6,0},{7,1},{8,10},{9,11},{10,... | collective-permute-start | bytes 1216520 | tf_op jit(solution)/shard_map/ppermute | solution.py:295
  104.8 13.9 %collective-permute-start.29 = (bf16[528,384]{1,0:T(8,128)(2,1)S(1)}, bf16[528,384]{1,0:T(8,128)(2,1)S(1)}, u32[]{:S(2)}, u32[]{:S(2)}) collective-permute-start(bf16[528,384]{1,0:T(8,128)(2,1)S(1)} %add_convert_fusion.2), channel_id=1, source_target_pairs={{0,6},{1,7},{2,0},{3,1},{4,2},{5,3},{6,4},{7,5},{8,14},{9,15},{10,... | collective-permute-start | bytes 1216520 | tf_op jit(solution)/shard_map/ppermute | solution.py:295
  119.8 21.4 %all-to-all-start.1 = ((bf16[32,16,512]{2,1,0:T(8,128)(2,1)}), bf16[32,16,512]{2,1,0:T(8,128)(2,1)S(1)}, u32[]{:S(2)}, u32[]{:S(2)}) async-start(bf16[32,16,512]{2,1,0:T(8,128)(2,1)} %bitcast.8), calls=%async_computation.1 | async-start | bytes 1048576 | tf_op jit(solution)/shard_map/all_to_all | solution.py:303
  125.1 16.2 %copy-start.21 = (f32[256]{0:T(256)S(1)}, f32[256]{0:T(256)}, u32[]{:S(2)}) copy-start(f32[256]{0:T(256)} %param.9) | copy-start | bytes 3076
  125.1 8.0 %collective-permute-start.30 = (bf16[256,512]{1,0:T(8,128)(2,1)S(1)}, bf16[256,512]{1,0:T(8,128)(2,1)S(1)}, u32[]{:S(2)}, u32[]{:S(2)}) collective-permute-start(bf16[256,512]{1,0:T(8,128)(2,1)S(1)} %add_convert_fusion.5.refs_3_), channel_id=1, source_target_pairs={{0,4},{1,5},{2,6},{3,7},{4,0},{5,1},{6,2},{7,3},{8,12},{9,13},{10,... | collective-permute-start | bytes 786440 | tf_op jit(solution)/shard_map/ppermute | solution.py:355
  133.1 1.6 %collective-permute-start.31 = (bf16[256,512]{1,0:T(8,128)(2,1)S(1)}, bf16[256,512]{1,0:T(8,128)(2,1)S(1)}, u32[]{:S(2)}, u32[]{:S(2)}) collective-permute-start(bf16[256,512]{1,0:T(8,128)(2,1)S(1)} %add_convert_fusion.4.refs_9_), channel_id=1, source_target_pairs={{0,1},{1,0},{2,3},{3,2},{4,5},{5,4},{6,7},{7,6},{8,9},{9,8},{10,11... | collective-permute-start | bytes 786440 | tf_op jit(solution)/shard_map/ppermute | solution.py:300
  134.8 1.0 copy-start.17

commit v3 on v2

--- a/solution.py
+++ b/solution.py
@@ -28,7 +28,7 @@
     return pl.BlockSpec(memory_space=VMEM)
 
 
-def call(body, out, inputs, flops=0, name=None, scratch=(), scalars=1, limit=14, after=(), light=False):
+def call(body, out, inputs, flops=0, name=None, scratch=(), scalars=1, limit=14, after=(), light=True):
     moved = sum(x.size * x.dtype.itemsize for x in inputs) + sum(
         o.size * o.dtype.itemsize for o in out
     )
@@ -54,26 +54,7 @@
     )(*inputs, *after)
 
 
-def column(row):
-    return jnp.transpose(jnp.broadcast_to(row, (8, row.shape[1])))[:, :1]
-
-
-def pack_kernel(capacity, cut_ref, ids_hbm, logit_hbm, tok_hbm, grad_hbm, out, slot_out, *scratch):
-    ids_ref, logit_ref, tok_ref, grad_ref, sems = scratch
-    copies = [
-        pltpu.make_async_copy(src, dst, sems.at[n])
-        for n, (src, dst) in enumerate(
-            [
-                (ids_hbm, ids_ref),
-                (logit_hbm, logit_ref),
-                (grad_hbm, grad_ref),
-                (tok_hbm, tok_ref),
-            ]
-        )
-    ]
-    for copy in copies:
-        copy.start()
-    copies[0].wait()
+def pack_kernel(capacity, cut_ref, ids_ref, tok_ref, wt_ref, out, slot_out):
     ids = ids_ref[...]
     rows, width = tok_ref.shape
     total = out.shape[0]
@@ -84,12 +65,7 @@
     slot = ids * capacity + arrival.astype(jnp.int32)
     slot_out[...] = jnp.broadcast_to(slot, slot_out.shape)
     place = (slot == iota((total, rows), 0)).astype(F32).astype(BF16)
-    copies[1].wait()
-    score = column(jax.nn.sigmoid(logit_ref[...]))
-    copies[2].wait()
-    weighted = (score * grad_ref[...].astype(F32)).astype(BF16)
-    copies[3].wait()
-    both = jnp.concatenate([tok_ref[...], weighted], axis=1)
+    both = jnp.concatenate([tok_ref[...], wt_ref[...]], axis=1)
     out[...] = dot(place, both).astype(BF16)
 
 
@@ -115,27 +91,20 @@
 
 
 def gates_kernel(chips, cut_ref, *refs):
-    count = 2 * chips - 1
-    near, far = refs[:count], refs[count : 2 * count]
-    gate_ref, up_ref, hid_out, act_out, slope_out, send_out, keep_out, gram = refs[2 * count :]
+    near, far_own, far_ref = refs[:chips], refs[chips], refs[chips + 1]
+    gate_ref, up_ref, hid_out, act_out, slope_out, send_out, keep_out, gram = refs[chips + 2 :]
     cut = cut_ref[0]
     width = near[0].shape[1]
-
-    def rows_of(k):
-        parts = [
-            [side[0][...]] if k == 0 else [side[2 * k - 1][...], side[2 * k][...]]
-            for side in (near, far)
-        ]
-        return jnp.concatenate([jnp.concatenate(p, axis=0) for p in parts], axis=1)
-
     for ref, out in ((gate_ref, act_out), (up_ref, slope_out)):
         for k in range(chips):
+            far = far_ref[k - 1] if k else far_own[...]
+            rows = jnp.concatenate([near[k][...], far], axis=1)
             mat = [ref[at(block_of(cut, k, o, chips), width), :] for o in (False, True)]
             mat = jnp.concatenate(mat, axis=0)
             if k == 0:
-                out[...] = dot(rows_of(k), mat)
+                out[...] = dot(rows, mat)
             else:
-                out[...] += dot(rows_of(k), mat)
+                out[...] += dot(rows, mat)
     gate_pre = act_out[...]
     up_pre = slope_out[...]
     sig = jax.nn.sigmoid(gate_pre)
@@ -182,7 +151,7 @@
 def hidden_kernel(chips, cut_ref, *refs):
     near, far = refs[: chips - 1], refs[chips - 1 : 2 * chips - 2]
     down_ref, first_ref, hid_ref, act_ref, slope_ref = refs[2 * chips - 2 : 2 * chips + 3]
-    both_out, tail_out, relay_out, acc = refs[2 * chips + 3 :]
+    both_out, tail_out, acc = refs[2 * chips + 3 :]
     cut = cut_ref[0]
     for k in range(1, chips):
         start = first_ref if k == 1 else acc
@@ -194,8 +163,8 @@
     dots = jnp.sum(hid_ref[...].astype(F32) * grad, axis=1, keepdims=True)
     flat = jnp.transpose(jnp.broadcast_to(dots, (dots.shape[0], 128)))[:8]
     width = near[0].shape[1]
-    tail_out[...] = encode(flat, width, 2 * (cut % 2))
-    relay_out[...] = encode(flat, width, 4 + 2 * (cut % 2))
+    tail_out[0] = encode(flat, width, 2 * (cut % 2))
+    tail_out[1] = encode(flat, width, 4 + 2 * (cut % 2))
 
 
 def part_kernel(cut_ref, both_ref, tail_ref, gate_own, gate_oth, up_own, up_oth, *refs):
@@ -203,39 +172,46 @@
     gate = jnp.concatenate([gate_own[...], gate_oth[...]], axis=0)
     up = jnp.concatenate([up_own[...], up_oth[...]], axis=0)
     out = dot(both_ref[...], jnp.concatenate([gate, up], axis=1), LAST).astype(BF16)
-    total, width = both_ref.shape[0], keep_out.shape[1]
-    keep_out[:total, :] = out[:, :width]
-    send_out[:total, :] = out[:, width:]
-    keep_out[total:, :] = tail_ref[...]
-    send_out[total:, :] = tail_ref[...]
-
-
-def part(where, both, tail, gate_mat, up_mat, width, hop, chips, after):
+    total, width = both_ref.shape[0], keep_out.shape[2]
+    keep_out[0, :total, :] = out[:, :width]
+    send_out[0, :total, :] = out[:, width:]
+    keep_out[0, total:, :] = tail_ref[0]
+    send_out[0, total:, :] = tail_ref[0]
+
+
+def part(where, both, tail, gate_mat, up_mat, width, count, hop_of, chips, after=()):
     rows, ff = both.shape[0], gate_mat.shape[1]
     mats = [
-        pl.BlockSpec((width, ff), lambda i, w, o=o: (block_of(w[0], chips - hop, o, chips), 0))
+        pl.BlockSpec(
+            (width, ff), lambda i, w, o=o: (block_of(w[0], chips - hop_of(i), o, chips), 0)
+        )
         for o in (False, True, False, True)
     ]
-    long = rows + tail.shape[0]
-    out = jax.ShapeDtypeStruct((long, width), BF16)
-    full = pl.BlockSpec((long, width), lambda i, w: (0, 0))
+    long = rows + tail.shape[1]
+    out = jax.ShapeDtypeStruct((count, long, width), BF16)
+    block = pl.BlockSpec((1, long, width), lambda i, w: (i, 0, 0))
     return pl.pallas_call(
         part_kernel,
         out_shape=[out, out],
         grid_spec=pltpu.PrefetchScalarGridSpec(
             num_scalar_prefetch=1,
-            grid=(1,),
+            grid=(count,),
             in_specs=[
                 pl.BlockSpec((rows, 2 * ff), lambda i, w: (0, 0)),
-                pl.BlockSpec(tail.shape, lambda i, w: (0, 0)),
+                pl.BlockSpec(
+                    (1,) + tail.shape[1:],
+                    lambda i, w: (jnp.where(hop_of(i) == chips // 2, 1, 0), 0, 0),
+                ),
             ]
             + mats
             + [pl.BlockSpec(memory_space=pl.ANY)] * len(after),
-            out_specs=[full, full],
+            out_specs=[block, block],
         ),
-        compiler_params=pltpu.CompilerParams(vmem_limit_bytes=10 << 20),
+        compiler_params=pltpu.CompilerParams(vmem_limit_bytes=12 << 20),
         cost_estimate=pl.CostEstimate(
-            flops=8 * rows * ff * width, bytes_accessed=6 << 20, transcendentals=0
+            flops=8 * rows * ff * width * count,
+            bytes_accessed=(4 << 20) * count,
+            transcendentals=0,
         ),
         name="input_part",
     )(where, both, tail, gate_mat, gate_mat, up_mat, up_mat, *after)
@@ -304,33 +280,23 @@
 
     ids = expert_ids.reshape(1, tok_rows)
     logit = gate_logit.reshape(1, tok_rows)
-    packed, slot = pl.pallas_call(
+    score = jax.nn.sigmoid(gate_logit)
+    weighted = (score[:, None] * out_grad.astype(F32)).astype(BF16)
+    packed, slot = call(
         functools.partial(pack_kernel, capacity),
-        out_shape=[shape((total, 2 * width), BF16), shape((8, tok_rows), jnp.int32)],
-        in_specs=[pl.BlockSpec(memory_space=pltpu.SMEM)]
-        + [pl.BlockSpec(memory_space=pltpu.HBM)] * 4,
-        out_specs=[whole()] * 2,
-        scratch_shapes=[
-            VMEM((1, tok_rows), jnp.int32),
-            VMEM((1, tok_rows), F32),
-            VMEM((tok_rows, width), BF16),
-            VMEM((tok_rows, width), BF16),
-            pltpu.SemaphoreType.DMA((4,)),
-        ],
-        compiler_params=pltpu.CompilerParams(vmem_limit_bytes=8 << 20),
-        name="pack",
-    )(where, ids, logit, tokens, out_grad)
+        [shape((total, 2 * width), BF16), shape((8, tok_rows), jnp.int32)],
+        (where, ids, tokens, weighted),
+        0,
+        "pack",
+        limit=8,
+    )
     routed = exchange(packed.reshape(experts, capacity, 2 * width)).reshape(total, 2 * width)
     tok_in, wt_in = routed[:, :width], routed[:, width:]
     mid = total // 2
-    ahead_top, back_low = hop(tok_in[:mid], 1), hop(tok_in[mid:], chips - 1)
-    ahead_low, back_top = hop(tok_in[mid:], 1), hop(tok_in[:mid], chips - 1)
-    tok_near = [tok_in, ahead_top, ahead_low]
-    tok_near += [hop(ahead_top, 1), hop(back_low, chips - 1), back_top, back_low]
-    tok_far = [swap(x) for x in tok_near]
+    tok_near = [hop(tok_in, k) for k in range(chips)]
+    tok_far = [swap(tok_in), swap(jnp.stack(tok_near[1:]))]
     wt_near = [hop(wt_in, k) for k in range(chips)]
     wt_swap = swap(wt_in)
-
     half = total // 2
     hidden, act, slope, gram_send, gram_keep = call(
         functools.partial(gates_kernel, chips),
@@ -366,14 +332,15 @@
         after=(hidden,),
         light=True,
     )
-    wt_late, first = lax.optimization_barrier((wt_near[1:], first))
-    wt_far = [wt_swap] + [swap(x) for x in wt_late]
-    both, tail, relay_tail = call(
+    wt_far = [wt_swap]
+    for k in range(1, chips):
+        late, _ = lax.optimization_barrier((wt_near[k], first))
+        wt_far.append(swap(late))
+    both, tails = call(
         functools.partial(hidden_kernel, chips),
         [
             shape((total, 2 * ff), BF16),
-            shape((16, width), BF16),
-            shape((16, width), BF16),
+            shape((2, 16, width), BF16),
         ],
         (where, *wt_near[1:], *wt_far[1:], down_mat, first, hidden, act, slope),
         2 * total * (feats - 2 * width) * ff,
@@ -381,23 +348,26 @@
         scratch=[VMEM((total, ff), F32)],
     )
 
-    def pieces(k, tail, after):
-        keep, send = part(where, both, tail, gate_mat, up_mat, width, k, chips, after)
-        return keep, swap(send)
-
     def total_of(*terms):
         return sum(x.astype(F32) for x in terms).astype(BF16)
 
-    through = total_of(*pieces(2, relay_tail, ()))
-    right = pieces(1, tail, ())
-    left = pieces(chips - 1, tail, (through,))
-    own = total_of(*pieces(0, tail, (through,)))
+    keep, send = part(
+        where, both, tails, gate_mat, up_mat, width, chips - 1, lambda i: i + 1, chips
+    )
+    gram_sum, _ = lax.optimization_barrier((gram_sum, wt_near[-1]))
+    gram_sum = add(gram_sum, chip_swap(gram_sum, 1))
+    send, gram_sum = lax.optimization_barrier((send, gram_sum))
+    recv = swap(send)
+    through = total_of(keep[1], recv[1])
+    long = send.shape[1]
     top, low = hop(through[:mid], 1), hop(through[mid:], chips - 1)
-    right = total_of(*right, jnp.pad(top, ((0, own.shape[0] - mid), (0, 0))))
-    left = total_of(*left, jnp.pad(low, ((mid, 0), (0, 0))))
+    right = total_of(keep[0], recv[0], jnp.pad(top, ((0, long - mid), (0, 0))))
+    left = total_of(keep[2], recv[2], jnp.pad(low, ((mid, 0), (0, 0))))
+    keep, send = part(
+        where, both, tails, gate_mat, up_mat, width, 1, lambda i: 0, chips, (through,)
+    )
+    own = total_of(keep[0], swap(send)[0])
     sums = [own, hop(right, 1), hop(left, chips - 1)]
-    gram_sum, _ = lax.optimization_barrier((gram_sum, left))
-    gram_sum = add(gram_sum, chip_swap(gram_sum, 1))
     (payload,) = call(
         final_kernel,
         [shape((total, width + 128), BF16)],

time: 143 us -> 142 us (level)
  waiting for transfers between devices: 50.4 us -> 65.5 us
  starting transfers between devices: 32.5 us -> 19.2 us
  local copies, waits for them, and re-layouts: 6.67 us -> 2.85 us
  other arithmetic: 0.69 us -> 2.7 us
    ppermute x13 -> x10, waiting for transfers between devices: 30.8 us -> 45.7 us  [hop(): lax.ppermute(x, 'cuts', [(2 * i + c, 2 * ((i + k) % chips) + c) for i in...]
    ppermute x13 -> x10, starting transfers between devices: 21.9 us -> 10.2 us  [hop(): lax.ppermute(x, 'cuts', [(2 * i + c, 2 * ((i + k) % chips) + c) for i in...]
    unnamed x46 -> x16, local copies, waits for them, and re-layouts: 6.51 us -> 2.72 us
    ppermute x17 -> x10, starting transfers between devices: 3.5 us -> 1.75 us  [swap(): return lax.ppermute(x, 'cuts', [(i, i ^ 1) for i in range(cuts)])]
    all_to_all x1, starting transfers between devices: 5.24 us -> 6.69 us  [exchange(): return lax.all_to_all(x, 'expert', split_axis=0, concat_axis=0, tiled=True)]
    ppermute x17 -> x10, waiting for transfers between devices: 6.55 us -> 7.94 us  [swap(): return lax.ppermute(x, 'cuts', [(i, i ^ 1) for i in range(cuts)])]
    pallas_call x6 -> x7, Pallas kernels: 11.3 us -> 11.9 us  [call(): pl.pallas_call(kernel, out_shape=out, in_specs=specs, out_specs=[whole()]...]
    pallas_call x4 -> x2, Pallas kernels: 4.09 us -> 4.13 us  [part(): pl.pallas_call(part_kernel, out_shape=[out, out], grid_spec=pltpu.Prefetc...]
  transfers between devices with their start and end apart: 33 -> 23, of which waited for: 20 -> 17; matrix products, arithmetic and copies ran while one was open for 1% -> 0% of each run, Pallas kernels for 7% -> 9%
where the time goes in v3:
time: 142 us; the launch traced here: 141 us
  waiting for transfers between devices  65.5 us (46%)
  blocking collectives  34.3 us (24%)
  starting transfers between devices  19.2 us (14%)
  Pallas kernels  16 us (11%)
  local copies, waits for them, and re-layouts  2.85 us (2%)
  other arithmetic  2.7 us (2%)
    ppermute x10, waiting for transfers between devices, hop(): lax.ppermute(x, 'cuts', [(2 * i + c, 2 * ((i + k) % chips) + c) for i in...  45.7 us
    all_to_all x1, blocking collectives, exchange(): return lax.all_to_all(x, 'expert', split_axis=0, concat_axis=0, tiled=True)  34.3 us
    pallas_call x7, Pallas kernels, call(): pl.pallas_call(kernel, out_shape=out, in_specs=specs, out_specs=[whole()]...  11.9 us
    ppermute x10, starting transfers between devices, hop(): lax.ppermute(x, 'cuts', [(2 * i + c, 2 * ((i + k) % chips) + c) for i in...  10.2 us
    ppermute x2, waiting for transfers between devices, chip_swap(): lax.ppermute(x, 'cuts', [(2 * i + c, 2 * (i ^ bit) + c) for i in range(ch...  9.16 us
    ppermute x10, waiting for transfers between devices, swap(): return lax.ppermute(x, 'cuts', [(i, i ^ 1) for i in range(cuts)])  7.94 us
    all_to_all x1, starting transfers between devices, exchange(): return lax.all_to_all(x, 'expert', split_axis=0, concat_axis=0, tiled=True)  6.69 us
    pallas_call x2, Pallas kernels, part(): pl.pallas_call(part_kernel, out_shape=[out, out], grid_spec=pltpu.Prefetc...  4.13 us
  transfers between devices with their start and end apart: 23, of which 17 were waited for; matrix products, arithmetic and copies ran while one was open for 0% of the time, Pallas kernels for 9%

profile of v3, /device:TPU:32, one launch (start us, length us, event | category | flops | bytes accessed | tf_op | source)
XLA Modules:
  0.0 141.5 jit_solution(8092102966409117287)
XLA Ops:
  0.6 0.7 add_divide_fusion
  1.3 1.2 multiply_convert_fusion.refs_3_
  2.5 0.0 copy-start.5
  2.5 0.9 copy-done.5
  3.4 0.7 copy-done.7
  4.1 0.5 pack.1
  4.7 34.3 %all_to_all.10 = bf16[32,16,768]{2,1,0:T(8,128)(2,1)S(1)} all-to-all(bf16[32,16,768]{2,1,0:T(8,128)(2,1)S(1)} %bitcast.47), channel_id=1, replica_groups=mesh['expert'=32,'cuts'=8] {'expert'}, dimensions={0} | all-to-all | bytes 1572864 | tf_op jit(solution)/shard_map/all_to_all | solution.py:279
  39.0 0.1 fusion.3
  39.1 2.8 %collective-permute-start.6 = (bf16[512,384]{1,0:T(8,128)(2,1)S(1)}, bf16[512,384]{1,0:T(8,128)(2,1)S(1)}, u32[]{:S(2)}, u32[]{:S(2)}) collective-permute-start(bf16[512,384]{1,0:T(8,128)(2,1)S(1)} %get-tuple-element.51.refs_1_), channel_id=1, source_target_pairs={{0,6},{1,7},{2,0},{3,1},{4,2},{5,3},{6,4},{7,5},{8,14},{9,15},{10,... | collective-permute-start | bytes 1179656 | tf_op jit(solution)/shard_map/ppermute | solution.py:271
  41.9 0.8 collective-permute-start.5
  42.7 0.9 collective-permute-start.4
  43.6 12.9 %collective-permute-done.6.refs_4_ = bf16[512,384]{1,0:T(8,128)(2,1)S(1)} collective-permute-done((bf16[512,384]{1,0:T(8,128)(2,1)S(1)}, bf16[512,384]{1,0:T(8,128)(2,1)S(1)}, u32[]{:S(2)}, u32[]{:S(2)}) %collective-permute-start.6) | collective-permute-done | bytes 393248 | tf_op jit(solution)/shard_map/ppermute | solution.py:271
  56.5 3.7 %collective-permute-done.4.refs_2_ = bf16[512,384]{1,0:T(8,128)(2,1)S(1)} collective-permute-done((bf16[512,384]{1,0:T(8,128)(2,1)S(1)}, bf16[512,384]{1,0:T(8,128)(2,1)S(1)}, u32[]{:S(2)}, u32[]{:S(2)}) %collective-permute-start.4) | collective-permute-done | bytes 393248 | tf_op jit(solution)/shard_map/ppermute | solution.py:271
  60.2 0.2 pad_maximum_fusion
  60.3 0.1 collective-permute-start.8
  60.4 0.5 collective-permute-start.7
  60.9 0.1 collective-permute-start.3
  61.0 0.6 collective-permute-start.2
  61.6 0.8 collective-permute-start.1
  62.4 1.4 collective-permute-done.7.refs_5_
  63.9 4.1 %gates.1 = (bf16[512,512]{1,0:T(8,128)(2,1)S(1)}, f32[512,512]{1,0:T(8,128)S(1)}, f32[512,512]{1,0:T(8,128)S(1)}, bf16[256,512]{1,0:T(8,128)(2,1)S(1)}, bf16[256,512]{1,0:T(8,128)(2,1)S(1)}) custom-call(s32[1]{0:T(128)} %bitcast.refs_0_.cut_ref, bf16[512,384]{1,0:T(8,128)(2,1)S(1)} %get-tuple-element.51.refs_1_, ...), custom_call_target="tpu_custom_call" | custom-call | tf_op jit(solution)/shard_map/gates/pallas_call | solution.py:45
  68.0 0.2 collective-permute-start.12
  68.2 0.6 own_hidden_grad.1.refs_8_
  68.8 0.1 copy-done.3
  69.0 4.0 %collective-permute-done.2.refs_3_.refs_4_ = bf16[512,384]{1,0:T(8,128)(2,1)S(1)} collective-permute-done((bf16[512,384]{1,0:T(8,128)(2,1)S(1)}, bf16[512,384]{1,0:T(8,128)(2,1)S(1)}, u32[]{:S(2)}, u32[]{:S(2)}) %collective-permute-start.2) | collective-permute-done | bytes 393248 | tf_op jit(solution)/shard_map/ppermute | solution.py:271
  72.9 2.2 %collective-permute-done.1.refs_2_.refs_3_ = bf16[512,384]{1,0:T(8,128)(2,1)S(1)} collective-permute-done((bf16[512,384]{1,0:T(8,128)(2,1)S(1)}, bf16[512,384]{1,0:T(8,128)(2,1)S(1)}, u32[]{:S(2)}, u32[]{:S(2)}) %collective-permute-start.1) | collective-permute-done | bytes 393248 | tf_op jit(solution)/shard_map/ppermute | solution.py:271
  75.1 7.6 %collective-permute-done.refs_1_.refs_2_ = bf16[512,384]{1,0:T(8,128)(2,1)S(1)} collective-permute-done((bf16[512,384]{1,0:T(8,128)(2,1)S(1)}, bf16[512,384]{1,0:T(8,128)(2,1)S(1)}, u32[]{:S(2)}, u32[]{:S(2)}) %collective-permute-start) | collective-permute-done | bytes 393248 | tf_op jit(solution)/shard_map/ppermute | solution.py:271
  82.7 0.0 collective-permute-start.9
  82.8 0.5 collective-permute-start.10
  83.2 0.0 collective-permute-start.11
  83.3 0.1 add_convert_fusion.4
  83.3 0.1 collective-permute-start.13
  83.5 1.0 collective-permute-done.9.refs_4_.refs_6_
  84.5 0.6 collective-permute-done.10.refs_5_.refs_7_
  85.0 0.6 collective-permute-done.11.refs_6_.refs_8_
  85.6 1.8 %hidden_grad.1 = (bf16[512,1024]{1,0:T(8,128)(2,1)S(1)}, bf16[2,16,384]{2,1,0:T(8,128)(2,1)S(1)}) custom-call(s32[1]{0:T(128)} %bitcast.refs_0_.cut_ref, bf16[512,384]{1,0:T(8,128)(2,1)S(1)} %collective-permute-done.refs_1_.refs_2_, bf16[512,384]{1,0:T(8,128)(2,1)S(1)} %collective-permute-done.1.refs_2_.refs_3_, ...), custom_call_target="tpu_custom_call" | custom-call | tf_op jit(solution)/shard_map/hidden_grad/pallas_call | solution.py:45
  87.3 3.1 %input_part.2 = (bf16[3,528,384]{2,1,0:T(8,128)(2,1)S(1)}, bf16[3,528,384]{2,1,0:T(8,128)(2,1)S(1)}) custom-call(s32[1]{0:T(128)} %bitcast.refs_0_.cut_ref, bf16[512,1024]{1,0:T(8,128)(2,1)S(1)} %get-tuple-element.34.both_ref, bf16[2,16,384]{2,1,0:T(8,128)(2,1)S(1)} %get-tuple-element.35.tail_ref, bf16[3072,512]{1,0:T(8,128)(2,1)S(1)} %bitcast.31, ...), custom_call_target="tpu_custom_call" | custom-call | flops 2415919104 | bytes 12582912 | tf_op jit(solution)/shard_map/input_part/pallas_call | solution.py:193
  90.5 1.7 %collective-permute-done.13 = bf16[256,512]{1,0:T(8,128)(2,1)S(1)} collective-permute-done((bf16[256,512]{1,0:T(8,128)(2,1)S(1)}, bf16[256,512]{1,0:T(8,128)(2,1)S(1)}, u32[]{:S(2)}, u32[]{:S(2)}) %collective-permute-start.13) | collective-permute-done | bytes 262176 | tf_op jit(solution)/shard_map/ppermute | solution.py:321
  92.1 0.1 add_convert_fusion.3.refs_3_
  92.2 0.1 collective-permute-start.14
  92.3 2.9 %collective-permute-done.14 = bf16[3,528,384]{2,1,0:T(8,128)(2,1)S(1)} collective-permute-done((bf16[3,528,384]{2,1,0:T(8,128)(2,1)S(1)}, bf16[3,528,384]{2,1,0:T(8,128)(2,1)S(1)}, u32[]{:S(2)}, u32[]{:S(2)}) %collective-permute-start.14) | collective-permute-done | bytes 1216544 | tf_op jit(solution)/shard_map/ppermute | solution.py:276
  95.2 0.1 add_convert_fusion.1
  95.3 0.9 collective-permute-start.18
  96.3 1.3 collective-permute-start.16
  97.5 1.0 input_part.3
  98.6 0.1 collective-permute-start.15
  98.7 5.6 %collective-permute-done.16 = bf16[256,384]{1,0:T(8,128)(2,1)S(1)} collective-permute-done((bf16[256,384]{1,0:T(8,128)(2,1)S(1)}, bf16[256,384]{1,0:T(8,128)(2,1)S(1)}, u32[]{:S(2)}, u32[]{:S(2)}) %collective-permute-start.16) | collective-permute-done | bytes 196640 | tf_op jit(solution)/shard_map/ppermute | solution.py:271
  104.2 0.3 fusion
  104.5 0.5 collective-permute-start.19
  105.0 1.6 %collective-permute-start.17 = (bf16[528,384]{1,0:T(8,128)(2,1)S(1)}, bf16[528,384]{1,0:T(8,128)(2,1)S(1)}, u32[]{:S(2)}, u32[]{:S(2)}) collective-permute-start(bf16[528,384]{1,0:T(8,128)(2,1)S(1)} %get-tuple-element.50), channel_id=1, source_target_pairs={{0,2},{1,3},{2,4},{3,5},{4,6},{5,7},{6,0},{7,1},{8,10},{9,11},{10,... | collective-permute-start | bytes 1216520 | tf_op jit(solution)/shard_map/ppermute | solution.py:271
  106.6 0.1 fusion.2.refs_0_
  106.7 8.1 %collective-permute-done.19.refs_2_ = bf16[528,384]{1,0:T(8,128)(2,1)S(1)} collective-permute-done((bf16[528,384]{1,0:T(8,128)(2,1)S(1)}, bf16[528,384]{1,0:T(8,128)(2,1)S(1)}, u32[]{:S(2)}, u32[]{:S(2)}) %collective-permute-start.19) | collective-permute-done | bytes 405536 | tf_op jit(solution)/shard_map/ppermute | solution.py:271
  114.8 1.7 %collective-permute-done.17.refs_1_ = bf16[528,384]{1,0:T(8,128)(2,1)S(1)} collective-permute-done((bf16[528,384]{1,0:T(8,128)(2,1)S(1)}, bf16[528,384]{1,0:T(8,128)(2,1)S(1)}, u32[]{:S(2)}, u32[]{:S(2)}) %collective-permute-start.17) | collective-permute-done | bytes 405536 | tf_op jit(solution)/shard_map/ppermute | solution.py:271
  116.5 1.1 final.1.refs_11_
  117.7 6.7 %all-to-all-start.1 = ((bf16[32,16,512]{2,1,0:T(8,128)(2,1)}), bf16[32,16,512]{2,1,0:T(8,128)(2,1)S(1)}, u32[]{:S(2)}, u32[]{:S(2)}) async-start(bf16[32,16,512]{2,1,0:T(8,128)(2,1)} %bitcast.17), calls=%async_computation.1 | async-start | bytes 1048576 | tf_op jit(solution)/shard_map/all_to_all | solution.py:279
  124.4 0.5 collective-permute-start.20
  124.8 7.5 %collective-permute-done.20 = bf16[256,512]{1,0:T(8,128)(2,1)S(1)} collective-permute-done((bf16[256,512]{1,0:T(8,128)(2,1)S(1)}, bf16[256,512]{1,0:T(8,128)(2,1)S(1)}, u32[]{:S(2)}, u32[]{:S(2)}) %collective-permute-start.20) | collective-permute-done | bytes 262176 | tf_op jit(solution)/shard_map/ppermute | solution.py:321
  132.3 0.1 add_convert_fusion.2.refs_9_
  132.4 0.1 collective-permute-start.21
  132.5 1.5 %collective-permute-done.21.refs_10_ = bf16[256,512]{1,0:T(8,128)(2,1)S(1)} collective-permute-done((bf16[256,512]{1,0:T(8,128)(2,1)S(1)}, bf16[256,512]{1,0:T(8,128)(2,1)S(1)}, u32[]{:S(2)}, u32[]{:S(2)}) %collective-permute-start.21) | collective-permute-done | bytes 262176 | tf_op jit(solution)/shard_map/ppermute | solution.py:276
  134.0 1.0 copy-done.4
  135.0 2.6 %stats.1 = f32[3,128,1024]{2,1,0:T(8,128)} custom-call(s32[1]{0:T(128)} %bitcast.refs_0_.cut_ref, bf16[512,384]{1,0:T(8,128)(2,1)S(1)} %get-tuple-element.52.refs_1_, bf16[512,384]{1,0:T(8,128)(2,1)S(1)} %collective-permute-done.refs_1_.refs_2_, bf16[512,384]{1,0:T(8,128)(2,1)S(1)} %collective-permute-done.1.refs_2_.refs_3_, ...), custom_call_target="tpu_custom_call" | custom-call | tf_op jit(solution)/shard_map/stats/pallas_call | solution.py:45
  137.6 2.7 %all-to-all-done.1 = bf16[32,16,512]{2,1,0:T(8,128)(2,1)S(1)} async-done(((bf16[32,16,512]{2,1,0:T(8,128)(2,1)}), bf16[32,16,512]{2,1,0:T(8,128)(2,1)S(1)}, u32[]{:S(2)}, u32[]{:S(2)}) %all-to-all-start.1) | async-done | bytes 524320 | tf_op jit(solution)/shard_map/all_to_all | solution.py:279
  140.3 1.2 unpack.1
  (20 shorter events, 0.1 us)
Async XLA Ops:
  1.3 62.5 %copy-start.1 = (bf16[1,3072,512]{2,1,0:T(8,128)(2,1)S(1)}, bf16[1,3072,512]{2,1,0:T(8,128)(2,1)}, u32[]{:S(2)}) copy-start(bf16[1,3072,512]{2,1,0:T(8,128)(2,1)} %param.12) | copy-start | bytes 9437188
  2.5 0.9 copy-start.5
  3.4 0.7 copy-start.7
  39.0 24.9 %copy-start = (bf16[1,3072,512]{2,1,0:T(8,128)(2,1)S(1)}, bf16[1,3072,512]{2,1,0:T(8,128)(2,1)}, u32[]{:S(2)}) copy-start(bf16[1,3072,512]{2,1,0:T(8,128)(2,1)} %param.11) | copy-start | bytes 9437188
  39.1 17.4 %collective-permute-start.6 = (bf16[512,384]{1,0:T(8,128)(2,1)S(1)}, bf16[512,384]{1,0:T(8,128)(2,1)S(1)}, u32[]{:S(2)}, u32[]{:S(2)}) collective-permute-start(bf16[512,384]{1,0:T(8,128)(2,1)S(1)} %get-tuple-element.51.refs_1_), channel_id=1, source_target_pairs={{0,6},{1,7},{2,0},{3,1},{4,2},{5,3},{6,4},{7,5},{8,14},{9,15},{10,... | collective-permute-start | bytes 1179656 | tf_op jit(solution)/shard_map/ppermute | solution.py:271
  41.9 14.6 %collective-permute-start.5 = (bf16[512,384]{1,0:T(8,128)(2,1)S(1)}, bf16[512,384]{1,0:T(8,128)(2,1)S(1)}, u32[]{:S(2)}, u32[]{:S(2)}) collective-permute-start(bf16[512,384]{1,0:T(8,128)(2,1)S(1)} %get-tuple-element.51.refs_1_), channel_id=1, source_target_pairs={{0,4},{1,5},{2,6},{3,7},{4,0},{5,1},{6,2},{7,3},{8,12},{9,13},{10,... | collective-permute-start | bytes 1179656 | tf_op jit(solution)/shard_map/ppermute | solution.py:271
  42.7 17.5 %collective-permute-start.4 = (bf16[512,384]{1,0:T(8,128)(2,1)S(1)}, bf16[512,384]{1,0:T(8,128)(2,1)S(1)}, u32[]{:S(2)}, u32[]{:S(2)}) collective-permute-start(bf16[512,384]{1,0:T(8,128)(2,1)S(1)} %get-tuple-element.51.refs_1_), channel_id=1, source_target_pairs={{0,2},{1,3},{2,4},{3,5},{4,6},{5,7},{6,0},{7,1},{8,10},{9,11},{10,... | collective-permute-start | bytes 1179656 | tf_op jit(solution)/shard_map/ppermute | solution.py:271
  60.3 3.5 %collective-permute-start.8 = (bf16[3,512,384]{2,1,0:T(8,128)(2,1)S(1)}, bf16[3,512,384]{2,1,0:T(8,128)(2,1)S(1)}, u32[]{:S(2)}, u32[]{:S(2)}) collective-permute-start(bf16[3,512,384]{2,1,0:T(8,128)(2,1)S(1)} %pad_maximum_fusion), channel_id=1, source_target_pairs={{0,1},{1,0},{2,3},{3,2},{4,5},{5,4},{6,7},{7,6},{8,9},{9,8},{10,11... | collective-permute-start | bytes 3538952 | tf_op jit(solution)/shard_map/ppermute | solution.py:276
  60.4 3.4 %collective-permute-start.7 = (bf16[512,384]{1,0:T(8,128)(2,1)S(1)}, bf16[512,384]{1,0:T(8,128)(2,1)S(1)}, u32[]{:S(2)}, u32[]{:S(2)}) collective-permute-start(bf16[512,384]{1,0:T(8,128)(2,1)S(1)} %get-tuple-element.51.refs_1_), channel_id=1, source_target_pairs={{0,1},{1,0},{2,3},{3,2},{4,5},{5,4},{6,7},{7,6},{8,9},{9,8},{10,11... | collective-permute-start | bytes 1179656 | tf_op jit(solution)/shard_map/ppermute | solution.py:276
  60.9 7.3 %collective-permute-start.3 = (bf16[512,384]{1,0:T(8,128)(2,1)S(1)}, bf16[512,384]{1,0:T(8,128)(2,1)S(1)}, u32[]{:S(2)}, u32[]{:S(2)}) collective-permute-start(bf16[512,384]{1,0:T(8,128)(2,1)S(1)} %get-tuple-element.52.refs_1_), channel_id=1, source_target_pairs={{0,1},{1,0},{2,3},{3,2},{4,5},{5,4},{6,7},{7,6},{8,9},{9,8},{10,11... | collective-permute-start | bytes 1179656 | tf_op jit(solution)/shard_map/ppermute | solution.py:276
  61.0 11.9 %collective-permute-start.2 = (bf16[512,384]{1,0:T(8,128)(2,1)S(1)}, bf16[512,384]{1,0:T(8,128)(2,1)S(1)}, u32[]{:S(2)}, u32[]{:S(2)}) collective-permute-start(bf16[512,384]{1,0:T(8,128)(2,1)S(1)} %get-tuple-element.52.refs_1_), channel_id=1, source_target_pairs={{0,6},{1,7},{2,0},{3,1},{4,2},{5,3},{6,4},{7,5},{8,14},{9,15},{10,... | collective-permute-start | bytes 1179656 | tf_op jit(solution)/shard_map/ppermute | solution.py:271
  61.6 13.5 %collective-permute-start.1 = (bf16[512,384]{1,0:T(8,128)(2,1)S(1)}, bf16[512,384]{1,0:T(8,128)(2,1)S(1)}, u32[]{:S(2)}, u32[]{:S(2)}) collective-permute-start(bf16[512,384]{1,0:T(8,128)(2,1)S(1)} %get-tuple-element.52.refs_1_), channel_id=1, source_target_pairs={{0,4},{1,5},{2,6},{3,7},{4,0},{5,1},{6,2},{7,3},{8,12},{9,13},{10,... | collective-permute-start | bytes 1179656 | tf_op jit(solution)/shard_map/ppermute | solution.py:271
  63.8 18.9 %collective-permute-start = (bf16[512,384]{1,0:T(8,128)(2,1)S(1)}, bf16[512,384]{1,0:T(8,128)(2,1)S(1)}, u32[]{:S(2)}, u32[]{:S(2)}) collective-permute-start(bf16[512,384]{1,0:T(8,128)(2,1)S(1)} %get-tuple-element.52.refs_1_), channel_id=1, source_target_pairs={{0,2},{1,3},{2,4},{3,5},{4,6},{5,7},{6,0},{7,1},{8,10},{9,11},{10,... | collective-permute-start | bytes 1179656 | tf_op jit(solution)/shard_map/ppermute | solution.py:271
  63.8 4.4 %copy-start.2 = (bf16[1,512,3072]{2,1,0:T(8,128)(2,1)S(1)}, bf16[1,512,3072]{2,1,0:T(8,128)(2,1)}, u32[]{:S(2)}) copy-start(bf16[1,512,3072]{2,1,0:T(8,128)(2,1)} %param.13) | copy-start | bytes 9437188
  68.0 15.3 %collective-permute-start.12 = (bf16[256,512]{1,0:T(8,128)(2,1)S(1)}, bf16[256,512]{1,0:T(8,128)(2,1)S(1)}, u32[]{:S(2)}, u32[]{:S(2)}) collective-permute-start(bf16[256,512]{1,0:T(8,128)(2,1)S(1)} %get-tuple-element.38), channel_id=1, source_target_pairs={{0,1},{1,0},{2,3},{3,2},{4,5},{5,4},{6,7},{7,6},{8,9},{9,8},{10,11... | collective-permute-start | bytes 786440 | tf_op jit(solution)/shard_map/ppermute | solution.py:276
  68.2 0.7 copy-start.3
  82.7 1.7 %collective-permute-start.9 = (bf16[512,384]{1,0:T(8,128)(2,1)S(1)}, bf16[512,384]{1,0:T(8,128)(2,1)S(1)}, u32[]{:S(2)}, u32[]{:S(2)}) collective-permute-start(bf16[512,384]{1,0:T(8,128)(2,1)S(1)} %collective-permute-done.refs_1_.refs_2_), channel_id=1, source_target_pairs={{0,1},{1,0},{2,3},{3,2},{4,5},{5,4},{6,7},{7,6},{8,9},{9,8},{10,11... | collective-permute-start | bytes 1179656 | tf_op jit(solution)/shard_map/ppermute | solution.py:276
  82.8 2.3 %collective-permute-start.10 = (bf16[512,384]{1,0:T(8,128)(2,1)S(1)}, bf16[512,384]{1,0:T(8,128)(2,1)S(1)}, u32[]{:S(2)}, u32[]{:S(2)}) collective-permute-start(bf16[512,384]{1,0:T(8,128)(2,1)S(1)} %collective-permute-done.1.refs_2_.refs_3_), channel_id=1, source_target_pairs={{0,1},{1,0},{2,3},{3,2},{4,5},{5,4},{6,7},{7,6},{8,9},{9,8},{10,11... | collective-permute-start | bytes 1179656 | tf_op jit(solution)/shard_map/ppermute | solution.py:276
  83.2 2.3 %collective-permute-start.11 = (bf16[512,384]{1,0:T(8,128)(2,1)S(1)}, bf16[512,384]{1,0:T(8,128)(2,1)S(1)}, u32[]{:S(2)}, u32[]{:S(2)}) collective-permute-start(bf16[512,384]{1,0:T(8,128)(2,1)S(1)} %collective-permute-done.2.refs_3_.refs_4_), channel_id=1, source_target_pairs={{0,1},{1,0},{2,3},{3,2},{4,5},{5,4},{6,7},{7,6},{8,9},{9,8},{10,11... | collective-permute-start | bytes 1179656 | tf_op jit(solution)/shard_map/ppermute | solution.py:276
  83.3 8.8 %collective-permute-start.13 = (bf16[256,512]{1,0:T(8,128)(2,1)S(1)}, bf16[256,512]{1,0:T(8,128)(2,1)S(1)}, u32[]{:S(2)}, u32[]{:S(2)}) collective-permute-start(bf16[256,512]{1,0:T(8,128)(2,1)S(1)} %add_convert_fusion.4), channel_id=1, source_target_pairs={{0,2},{1,3},{2,0},{3,1},{4,6},{5,7},{6,4},{7,5},{8,10},{9,11},{10,... | collective-permute-start | bytes 786440 | tf_op jit(solution)/shard_map/ppermute | solution.py:321
  92.2 3.0 %collective-permute-start.14 = (bf16[3,528,384]{2,1,0:T(8,128)(2,1)S(1)}, bf16[3,528,384]{2,1,0:T(8,128)(2,1)S(1)}, u32[]{:S(2)}, u32[]{:S(2)}) collective-permute-start(bf16[3,528,384]{2,1,0:T(8,128)(2,1)S(1)} %get-tuple-element.42), channel_id=1, source_target_pairs={{0,1},{1,0},{2,3},{3,2},{4,5},{5,4},{6,7},{7,6},{8,9},{9,8},{10,11... | collective-permute-start | bytes 3649544 | tf_op jit(solution)/shard_map/ppermute | solution.py:276
  95.3 8.9 %collective-permute-start.18 = (bf16[272,384]{1,0:T(8,128)(2,1)S(1)}, bf16[272,384]{1,0:T(8,128)(2,1)S(1)}, u32[]{:S(2)}, u32[]{:S(2)}) collective-permute-start(bf16[272,384]{1,0:T(8,128)(2,1)S(1)} %slice_bitcast_fusion), channel_id=1, source_target_pairs={{0,6},{1,7},{2,0},{3,1},{4,2},{5,3},{6,4},{7,5},{8,14},{9,15},{10,... | collective-permute-start | bytes 626696 | tf_op jit(solution)/shard_map/ppermute | solution.py:271
  96.3 8.0 %collective-permute-start.16 = (bf16[256,384]{1,0:T(8,128)(2,1)S(1)}, bf16[256,384]{1,0:T(8,128)(2,1)S(1)}, u32[]{:S(2)}, u32[]{:S(2)}) collective-permute-start(bf16[256,384]{1,0:T(8,128)(2,1)S(1)} %slice_bitcast_fusion.1), channel_id=1, source_target_pairs={{0,2},{1,3},{2,4},{3,5},{4,6},{5,7},{6,0},{7,1},{8,10},{9,11},{10,... | collective-permute-start | bytes 589832 | tf_op jit(solution)/shard_map/ppermute | solution.py:271
  98.6 8.0 %collective-permute-start.15 = (bf16[1,528,384]{2,1,0:T(8,128)(2,1)S(1)}, bf16[1,528,384]{2,1,0:T(8,128)(2,1)S(1)}, u32[]{:S(2)}, u32[]{:S(2)}) collective-permute-start(bf16[1,528,384]{2,1,0:T(8,128)(2,1)S(1)} %get-tuple-element.44), channel_id=1, source_target_pairs={{0,1},{1,0},{2,3},{3,2},{4,5},{5,4},{6,7},{7,6},{8,9},{9,8},{10,11... | collective-permute-start | bytes 1216520 | tf_op jit(solution)/shard_map/ppermute | solution.py:276
  104.5 10.3 %collective-permute-start.19 = (bf16[528,384]{1,0:T(8,128)(2,1)S(1)}, bf16[528,384]{1,0:T(8,128)(2,1)S(1)}, u32[]{:S(2)}, u32[]{:S(2)}) collective-permute-start(bf16[528,384]{1,0:T(8,128)(2,1)S(1)} %get-tuple-element.49), channel_id=1, source_target_pairs={{0,6},{1,7},{2,0},{3,1},{4,2},{5,3},{6,4},{7,5},{8,14},{9,15},{10,... | collective-permute-start | bytes 1216520 | tf_op jit(solution)/shard_map/ppermute | solution.py:271
  105.0 11.5 %collective-permute-start.17 = (bf16[528,384]{1,0:T(8,128)(2,1)S(1)}, bf16[528,384]{1,0:T(8,128)(2,1)S(1)}, u32[]{:S(2)}, u32[]{:S(2)}) collective-permute-start(bf16[528,384]{1,0:T(8,128)(2,1)S(1)} %get-tuple-element.50), channel_id=1, source_target_pairs={{0,2},{1,3},{2,4},{3,5},{4,6},{5,7},{6,0},{7,1},{8,10},{9,11},{10,... | collective-permute-start | bytes 1216520 | tf_op jit(solution)/shard_map/ppermute | solution.py:271
  117.7 22.6 %all-to-all-start.1 = ((bf16[32,16,512]{2,1,0:T(8,128)(2,1)}), bf16[32,16,512]{2,1,0:T(8,128)(2,1)S(1)}, u32[]{:S(2)}, u32[]{:S(2)}) async-start(bf16[32,16,512]{2,1,0:T(8,128)(2,1)} %bitcast.17), calls=%async_computation.1 | async-start | bytes 1048576 | tf_op jit(solution)/shard_map/all_to_all | solution.py:279
  124.4 8.0 %collective-permute-start.20 = (bf16[256,512]{1,0:T(8,128)(2,1)S(1)}, bf16[256,512]{1,0:T(8,128)(2,1)S(1)}, u32[]{:S(2)}, u32[]{:S(2)}) collective-permute-start(bf16[256,512]{1,0:T(8,128)(2,1)S(1)} %add_convert_fusion.3.refs_3_), channel_id=1, source_target_pairs={{0,4},{1,5},{2,6},{3,7},{4,0},{5,1},{6,2},{7,3},{8,12},{9,13},{10,... | collective-permute-start | bytes 786440 | tf_op jit(solution)/shard_map/ppermute | solution.py:321
  132.3 7.9 %copy-start.6 = (f32[256]{0:T(256)S(1)}, f32[256]{0:T(256)}, u32[]{:S(2)}) copy-start(f32[256]{0:T(256)} %param.9) | copy-start | bytes 3076
  132.4 1.6 %collective-permute-start.21 = (bf16[256,512]{1,0:T(8,128)(2,1)S(1)}, bf16[256,512]{1,0:T(8,128)(2,1)S(1)}, u32[]{:S(2)}, u32[]{:S(2)}) collective-permute-start(bf16[256,512]{1,0:T(8,128)(2,1)S(1)} %add_convert_fusion.2.refs_9_), channel_id=1, source_target_pairs={{0,1},{1,0},{2,3},{3,2},{4,5},{5,4},{6,7},{7,6},{8,9},{9,8},{10,11... | collective-permute-start | bytes 786440 | tf_op jit(solution)/shard_map/ppermute | solution.py:276
  134.0 1.0 copy-start.4

commit v4 on v3

--- a/solution.py
+++ b/solution.py
@@ -54,10 +54,10 @@
     )(*inputs, *after)
 
 
-def pack_kernel(capacity, cut_ref, ids_ref, tok_ref, wt_ref, out, slot_out):
+def pack_kernel(capacity, cut_ref, ids_ref, tok_ref, wt_ref, tok_out, wt_out, slot_out):
     ids = ids_ref[...]
-    rows, width = tok_ref.shape
-    total = out.shape[0]
+    rows = ids.shape[1]
+    total = tok_out.shape[0]
     mine = ids == iota((total // capacity, rows), 0)
     earlier = (iota((rows, rows), 0) < iota((rows, rows), 1)).astype(F32).astype(BF16)
     before = dot(mine.astype(F32).astype(BF16), earlier)
@@ -65,8 +65,8 @@
     slot = ids * capacity + arrival.astype(jnp.int32)
     slot_out[...] = jnp.broadcast_to(slot, slot_out.shape)
     place = (slot == iota((total, rows), 0)).astype(F32).astype(BF16)
-    both = jnp.concatenate([tok_ref[...], wt_ref[...]], axis=1)
-    out[...] = dot(place, both).astype(BF16)
+    tok_out[...] = dot(place, tok_ref[...]).astype(BF16)
+    wt_out[...] = dot(place, wt_ref[...]).astype(BF16)
 
 
 def unpack_kernel(slot_ref, logit_ref, back_ref, grad_out, logit_out):
@@ -91,14 +91,13 @@
 
 
 def gates_kernel(chips, cut_ref, *refs):
-    near, far_own, far_ref = refs[:chips], refs[chips], refs[chips + 1]
-    gate_ref, up_ref, hid_out, act_out, slope_out, send_out, keep_out, gram = refs[chips + 2 :]
+    near, far = refs[:chips], refs[chips : 2 * chips]
+    gate_ref, up_ref, hid_out, act_out, slope_out, send_out, keep_out, gram = refs[2 * chips :]
     cut = cut_ref[0]
     width = near[0].shape[1]
     for ref, out in ((gate_ref, act_out), (up_ref, slope_out)):
         for k in range(chips):
-            far = far_ref[k - 1] if k else far_own[...]
-            rows = jnp.concatenate([near[k][...], far], axis=1)
+            rows = jnp.concatenate([near[k][...], far[k][...]], axis=1)
             mat = [ref[at(block_of(cut, k, o, chips), width), :] for o in (False, True)]
             mat = jnp.concatenate(mat, axis=0)
             if k == 0:
@@ -282,19 +281,25 @@
     logit = gate_logit.reshape(1, tok_rows)
     score = jax.nn.sigmoid(gate_logit)
     weighted = (score[:, None] * out_grad.astype(F32)).astype(BF16)
-    packed, slot = call(
+    tok_pack, wt_pack, slot = call(
         functools.partial(pack_kernel, capacity),
-        [shape((total, 2 * width), BF16), shape((8, tok_rows), jnp.int32)],
+        [
+            shape((total, width), BF16),
+            shape((total, width), BF16),
+            shape((8, tok_rows), jnp.int32),
+        ],
         (where, ids, tokens, weighted),
         0,
         "pack",
         limit=8,
     )
-    routed = exchange(packed.reshape(experts, capacity, 2 * width)).reshape(total, 2 * width)
-    tok_in, wt_in = routed[:, :width], routed[:, width:]
+    tok_in = exchange(tok_pack.reshape(experts, capacity, width)).reshape(total, width)
+    wt_pack, tok_in = lax.optimization_barrier((wt_pack, tok_in))
+    wt_in = exchange(wt_pack.reshape(experts, capacity, width)).reshape(total, width)
     mid = total // 2
     tok_near = [hop(tok_in, k) for k in range(chips)]
-    tok_far = [swap(tok_in), swap(jnp.stack(tok_near[1:]))]
+    tok_far = [swap(x) for x in tok_near]
+    wt_in, _ = lax.optimization_barrier((wt_in, tok_far))
     wt_near = [hop(wt_in, k) for k in range(chips)]
     wt_swap = swap(wt_in)
     half = total // 2
@@ -312,6 +317,7 @@
         "gates",
         scratch=[VMEM((total, total), F32)],
         limit=18,
+        after=(wt_swap,),
         light=True,
     )
     def add(x, y):

time: 142 us -> 137 us (0.965)
  waiting for transfers between devices: 65.5 us -> 51.7 us
  local copies, waits for them, and re-layouts: 2.85 us -> 14.7 us
  blocking collectives: 34.3 us -> 26 us
  starting transfers between devices: 19.2 us -> 24.1 us
    ppermute x10, waiting for transfers between devices: 45.7 us -> 33.8 us  [hop(): lax.ppermute(x, 'cuts', [(2 * i + c, 2 * ((i + k) % chips) + c) for i in...]
    unnamed x16 -> x36, local copies, waits for them, and re-layouts: 2.72 us -> 14.6 us
    all_to_all x1, blocking collectives: 34.3 us -> 26 us  [exchange(): return lax.all_to_all(x, 'expert', split_axis=0, concat_axis=0, tiled=True)]
    all_to_all x1 -> x2, starting transfers between devices: 6.69 us -> 9.43 us  [exchange(): return lax.all_to_all(x, 'expert', split_axis=0, concat_axis=0, tiled=True)]
    ppermute x10, starting transfers between devices: 10.2 us -> 12.6 us  [hop(): lax.ppermute(x, 'cuts', [(2 * i + c, 2 * ((i + k) % chips) + c) for i in...]
    ppermute x10 -> x12, waiting for transfers between devices: 7.94 us -> 6.56 us  [swap(): return lax.ppermute(x, 'cuts', [(i, i ^ 1) for i in range(cuts)])]
    all_to_all x1 -> x2, waiting for transfers between devices: 2.7 us -> 3.34 us  [exchange(): return lax.all_to_all(x, 'expert', split_axis=0, concat_axis=0, tiled=True)]
  transfers between devices with their start and end apart: 23 -> 26, of which waited for: 17 -> 16; matrix products, arithmetic and copies ran while one was open for 0% -> 0% of each run, Pallas kernels for 9% -> 10%
where the time goes in v4:
time: 137 us; the launch traced here: 136 us
  waiting for transfers between devices  51.7 us (38%)
  blocking collectives  26 us (19%)
  starting transfers between devices  24.1 us (18%)
  Pallas kernels  16.8 us (12%)
  local copies, waits for them, and re-layouts  14.7 us (11%)
  other arithmetic  2.38 us (2%)
    ppermute x10, waiting for transfers between devices, hop(): lax.ppermute(x, 'cuts', [(2 * i + c, 2 * ((i + k) % chips) + c) for i in...  33.8 us
    all_to_all x1, blocking collectives, exchange(): return lax.all_to_all(x, 'expert', split_axis=0, concat_axis=0, tiled=True)  26 us
    unnamed x36, local copies, waits for them, and re-layouts  14.6 us
    pallas_call x7, Pallas kernels, call(): pl.pallas_call(kernel, out_shape=out, in_specs=specs, out_specs=[whole()]...  12.7 us
    ppermute x10, starting transfers between devices, hop(): lax.ppermute(x, 'cuts', [(2 * i + c, 2 * ((i + k) % chips) + c) for i in...  12.6 us
    all_to_all x2, starting transfers between devices, exchange(): return lax.all_to_all(x, 'expert', split_axis=0, concat_axis=0, tiled=True)  9.43 us
    ppermute x2, waiting for transfers between devices, chip_swap(): lax.ppermute(x, 'cuts', [(2 * i + c, 2 * (i ^ bit) + c) for i in range(ch...  7.96 us
    ppermute x12, waiting for transfers between devices, swap(): return lax.ppermute(x, 'cuts', [(i, i ^ 1) for i in range(cuts)])  6.56 us
  transfers between devices with their start and end apart: 26, of which 16 were waited for; matrix products, arithmetic and copies ran while one was open for 0% of the time, Pallas kernels for 10%

profile of v4, /device:TPU:32, one launch (start us, length us, event | category | flops | bytes accessed | tf_op | source)
XLA Modules:
  0.0 136.4 jit_solution(14578724194883196300)
XLA Ops:
  0.6 0.7 add_divide_fusion
  1.3 1.0 multiply_convert_fusion.refs_3_
  2.4 0.9 copy-done.15
  3.3 0.7 copy-done.17
  4.0 1.3 pack.1
  5.3 26.0 %all_to_all.15 = bf16[32,16,384]{2,1,0:T(8,128)(2,1)S(1)} all-to-all(bf16[32,16,384]{2,1,0:T(8,128)(2,1)S(1)} %bitcast.54), channel_id=1, replica_groups=mesh['expert'=32,'cuts'=8] {'expert'}, dimensions={0} | all-to-all | bytes 786432 | tf_op jit(solution)/shard_map/all_to_all | solution.py:278
  31.3 2.8 %collective-permute-start.5 = (bf16[512,384]{1,0:T(8,128)(2,1)S(1)}, bf16[512,384]{1,0:T(8,128)(2,1)S(1)}, u32[]{:S(2)}, u32[]{:S(2)}) collective-permute-start(bf16[512,384]{1,0:T(8,128)(2,1)S(1)} %bitcast.49), channel_id=1, source_target_pairs={{0,6},{1,7},{2,0},{3,1},{4,2},{5,3},{6,4},{7,5},{8,14},{9,15},{10,... | collective-permute-start | bytes 1179656 | tf_op jit(solution)/shard_map/ppermute | solution.py:270
  34.1 0.8 collective-permute-start.3
  34.9 0.9 collective-permute-start.1
  35.8 4.8 %all-to-all-start.1 = ((bf16[32,16,384]{2,1,0:T(8,128)(2,1)}), bf16[32,16,384]{2,1,0:T(8,128)(2,1)S(1)}, u32[]{:S(2)}, u32[]{:S(2)}) async-start(bf16[32,16,384]{2,1,0:T(8,128)(2,1)} %bitcast.5), calls=%async_computation.1 | async-start | bytes 786432 | tf_op jit(solution)/shard_map/all_to_all | solution.py:278
  40.7 8.4 %collective-permute-done.5.refs_4_ = bf16[512,384]{1,0:T(8,128)(2,1)S(1)} collective-permute-done((bf16[512,384]{1,0:T(8,128)(2,1)S(1)}, bf16[512,384]{1,0:T(8,128)(2,1)S(1)}, u32[]{:S(2)}, u32[]{:S(2)}) %collective-permute-start.5) | collective-permute-done | bytes 393248 | tf_op jit(solution)/shard_map/ppermute | solution.py:270
  49.1 0.5 collective-permute-start.4
  49.6 3.2 %collective-permute-done.1.refs_2_ = bf16[512,384]{1,0:T(8,128)(2,1)S(1)} collective-permute-done((bf16[512,384]{1,0:T(8,128)(2,1)S(1)}, bf16[512,384]{1,0:T(8,128)(2,1)S(1)}, u32[]{:S(2)}, u32[]{:S(2)}) %collective-permute-start.1) | collective-permute-done | bytes 393248 | tf_op jit(solution)/shard_map/ppermute | solution.py:270
  52.8 0.8 copy-done.7
  53.6 0.6 all-to-all-done.1
  54.2 0.7 copy-done.9
  54.9 0.8 copy-done.11
  55.7 0.7 copy-done.13
  56.5 2.4 %collective-permute-start.9 = (bf16[512,384]{1,0:T(8,128)(2,1)S(1)}, bf16[512,384]{1,0:T(8,128)(2,1)S(1)}, u32[]{:S(2)}, u32[]{:S(2)}) collective-permute-start(bf16[512,384]{1,0:T(8,128)(2,1)S(1)} %bitcast.43), channel_id=1, source_target_pairs={{0,6},{1,7},{2,0},{3,1},{4,2},{5,3},{6,4},{7,5},{8,14},{9,15},{10,... | collective-permute-start | bytes 1179656 | tf_op jit(solution)/shard_map/ppermute | solution.py:270
  58.8 1.5 %collective-permute-start.8 = (bf16[512,384]{1,0:T(8,128)(2,1)S(1)}, bf16[512,384]{1,0:T(8,128)(2,1)S(1)}, u32[]{:S(2)}, u32[]{:S(2)}) collective-permute-start(bf16[512,384]{1,0:T(8,128)(2,1)S(1)} %bitcast.44), channel_id=1, source_target_pairs={{0,4},{1,5},{2,6},{3,7},{4,0},{5,1},{6,2},{7,3},{8,12},{9,13},{10,... | collective-permute-start | bytes 1179656 | tf_op jit(solution)/shard_map/ppermute | solution.py:270
  60.3 1.9 %copy-done = bf16[1,3072,512]{2,1,0:T(8,128)(2,1)S(1)} copy-done((bf16[1,3072,512]{2,1,0:T(8,128)(2,1)S(1)}, bf16[1,3072,512]{2,1,0:T(8,128)(2,1)}, u32[]{:S(2)}) %copy-start) | copy-done | bytes 3145752
  62.2 1.9 %copy-done.2 = bf16[1,3072,512]{2,1,0:T(8,128)(2,1)S(1)} copy-done((bf16[1,3072,512]{2,1,0:T(8,128)(2,1)S(1)}, bf16[1,3072,512]{2,1,0:T(8,128)(2,1)}, u32[]{:S(2)}) %copy-start.2) | copy-done | bytes 3145752
  64.1 1.0 copy-done.8
  65.1 1.0 copy-done.10
  66.1 1.0 copy-done.12
  67.1 1.0 copy-done.14
  68.1 4.1 %gates.1 = (bf16[512,512]{1,0:T(8,128)(2,1)S(1)}, f32[512,512]{1,0:T(8,128)S(1)}, f32[512,512]{1,0:T(8,128)S(1)}, bf16[256,512]{1,0:T(8,128)(2,1)S(1)}, bf16[256,512]{1,0:T(8,128)(2,1)S(1)}) custom-call(s32[1]{0:T(128)} %bitcast.refs_0_.cut_ref, bf16[512,384]{1,0:T(8,128)(2,1)S(1)} %bitcast.53, bf16[512,384]{1,0:T(8,128)(2,1)S(1)} %collective-permute-done.1.refs_2_, ...), custom_call_target="tpu_custom_call" | custom-call | tf_op jit(solution)/shard_map/gates/pallas_call | solution.py:45
  72.2 0.1 collective-permute-start.14
  72.3 0.6 own_hidden_grad.1.refs_8_
  73.0 3.4 %collective-permute-done.9.refs_3_.refs_4_ = bf16[512,384]{1,0:T(8,128)(2,1)S(1)} collective-permute-done((bf16[512,384]{1,0:T(8,128)(2,1)S(1)}, bf16[512,384]{1,0:T(8,128)(2,1)S(1)}, u32[]{:S(2)}, u32[]{:S(2)}) %collective-permute-start.9) | collective-permute-done | bytes 393248 | tf_op jit(solution)/shard_map/ppermute | solution.py:270
  76.3 3.7 %collective-permute-done.7.refs_1_.refs_2_ = bf16[512,384]{1,0:T(8,128)(2,1)S(1)} collective-permute-done((bf16[512,384]{1,0:T(8,128)(2,1)S(1)}, bf16[512,384]{1,0:T(8,128)(2,1)S(1)}, u32[]{:S(2)}, u32[]{:S(2)}) %collective-permute-start.7) | collective-permute-done | bytes 393248 | tf_op jit(solution)/shard_map/ppermute | solution.py:270
  80.0 0.5 collective-permute-start.12
  80.6 0.1 collective-permute-start.15
  80.7 1.0 collective-permute-done.11.refs_4_.refs_6_
  81.7 0.6 collective-permute-done.12.refs_5_.refs_7_
  82.3 0.6 collective-permute-done.13.refs_6_.refs_8_
  82.9 1.7 %hidden_grad.1 = (bf16[512,1024]{1,0:T(8,128)(2,1)S(1)}, bf16[2,16,384]{2,1,0:T(8,128)(2,1)S(1)}) custom-call(s32[1]{0:T(128)} %bitcast.refs_0_.cut_ref, bf16[512,384]{1,0:T(8,128)(2,1)S(1)} %collective-permute-done.7.refs_1_.refs_2_, bf16[512,384]{1,0:T(8,128)(2,1)S(1)} %collective-permute-done.8.refs_2_.refs_3_, ...), custom_call_target="tpu_custom_call" | custom-call | tf_op jit(solution)/shard_map/hidden_grad/pallas_call | solution.py:45
  84.6 0.3 copy-done.1
  84.9 0.9 copy-done.3
  85.8 3.1 %input_part.2 = (bf16[3,528,384]{2,1,0:T(8,128)(2,1)S(1)}, bf16[3,528,384]{2,1,0:T(8,128)(2,1)S(1)}) custom-call(s32[1]{0:T(128)} %bitcast.refs_0_.cut_ref, bf16[512,1024]{1,0:T(8,128)(2,1)S(1)} %get-tuple-element.42.both_ref, bf16[2,16,384]{2,1,0:T(8,128)(2,1)S(1)} %get-tuple-element.43.tail_ref, bf16[3072,512]{1,0:T(8,128)(2,1)S(1)} %bitcast.30, ...), custom_call_target="tpu_custom_call" | custom-call | flops 2415919104 | bytes 12582912 | tf_op jit(solution)/shard_map/input_part/pallas_call | solution.py:192
  88.9 0.5 collective-permute-done.15
  89.6 2.9 %collective-permute-done.16 = bf16[3,528,384]{2,1,0:T(8,128)(2,1)S(1)} collective-permute-done((bf16[3,528,384]{2,1,0:T(8,128)(2,1)S(1)}, bf16[3,528,384]{2,1,0:T(8,128)(2,1)S(1)}, u32[]{:S(2)}, u32[]{:S(2)}) %collective-permute-start.16) | collective-permute-done | bytes 1216544 | tf_op jit(solution)/shard_map/ppermute | solution.py:275
  92.5 0.1 add_convert_fusion.1
  92.6 0.7 collective-permute-start.20
  93.3 1.5 %collective-permute-start.18 = (bf16[256,384]{1,0:T(8,128)(2,1)S(1)}, bf16[256,384]{1,0:T(8,128)(2,1)S(1)}, u32[]{:S(2)}, u32[]{:S(2)}) collective-permute-start(bf16[256,384]{1,0:T(8,128)(2,1)S(1)} %slice_bitcast_fusion.1), channel_id=1, source_target_pairs={{0,2},{1,3},{2,4},{3,5},{4,6},{5,7},{6,0},{7,1},{8,10},{9,11},{10,... | collective-permute-start | bytes 589832 | tf_op jit(solution)/shard_map/ppermute | solution.py:270
  94.8 1.0 input_part.3
  95.8 0.1 collective-permute-start.17
  95.9 5.3 %collective-permute-done.18 = bf16[256,384]{1,0:T(8,128)(2,1)S(1)} collective-permute-done((bf16[256,384]{1,0:T(8,128)(2,1)S(1)}, bf16[256,384]{1,0:T(8,128)(2,1)S(1)}, u32[]{:S(2)}, u32[]{:S(2)}) %collective-permute-start.18) | collective-permute-done | bytes 196640 | tf_op jit(solution)/shard_map/ppermute | solution.py:270
  101.3 0.3 fusion
  101.5 0.5 collective-permute-start.21
  102.0 1.6 %collective-permute-start.19 = (bf16[528,384]{1,0:T(8,128)(2,1)S(1)}, bf16[528,384]{1,0:T(8,128)(2,1)S(1)}, u32[]{:S(2)}, u32[]{:S(2)}) collective-permute-start(bf16[528,384]{1,0:T(8,128)(2,1)S(1)} %get-tuple-element.58), channel_id=1, source_target_pairs={{0,2},{1,3},{2,4},{3,5},{4,6},{5,7},{6,0},{7,1},{8,10},{9,11},{10,... | collective-permute-start | bytes 1216520 | tf_op jit(solution)/shard_map/ppermute | solution.py:270
  103.6 0.1 fusion.2.refs_0_
  103.7 8.1 %collective-permute-done.21.refs_2_ = bf16[528,384]{1,0:T(8,128)(2,1)S(1)} collective-permute-done((bf16[528,384]{1,0:T(8,128)(2,1)S(1)}, bf16[528,384]{1,0:T(8,128)(2,1)S(1)}, u32[]{:S(2)}, u32[]{:S(2)}) %collective-permute-start.21) | collective-permute-done | bytes 405536 | tf_op jit(solution)/shard_map/ppermute | solution.py:270
  111.9 1.7 %collective-permute-done.19.refs_1_ = bf16[528,384]{1,0:T(8,128)(2,1)S(1)} collective-permute-done((bf16[528,384]{1,0:T(8,128)(2,1)S(1)}, bf16[528,384]{1,0:T(8,128)(2,1)S(1)}, u32[]{:S(2)}, u32[]{:S(2)}) %collective-permute-start.19) | collective-permute-done | bytes 405536 | tf_op jit(solution)/shard_map/ppermute | solution.py:270
  113.6 1.1 final.1.refs_11_
  114.7 4.7 %all-to-all-start.2 = ((bf16[32,16,512]{2,1,0:T(8,128)(2,1)}), bf16[32,16,512]{2,1,0:T(8,128)(2,1)S(1)}, u32[]{:S(2)}, u32[]{:S(2)}) async-start(bf16[32,16,512]{2,1,0:T(8,128)(2,1)} %bitcast.16), calls=%async_computation.2 | async-start | bytes 1048576 | tf_op jit(solution)/shard_map/all_to_all | solution.py:278
  119.3 0.5 collective-permute-start.22
  119.8 7.5 %collective-permute-done.22 = bf16[256,512]{1,0:T(8,128)(2,1)S(1)} collective-permute-done((bf16[256,512]{1,0:T(8,128)(2,1)S(1)}, bf16[256,512]{1,0:T(8,128)(2,1)S(1)}, u32[]{:S(2)}, u32[]{:S(2)}) %collective-permute-start.22) | collective-permute-done | bytes 262176 | tf_op jit(solution)/shard_map/ppermute | solution.py:327
  127.4 0.1 collective-permute-start.23
  127.5 1.5 %collective-permute-done.23.refs_10_ = bf16[256,512]{1,0:T(8,128)(2,1)S(1)} collective-permute-done((bf16[256,512]{1,0:T(8,128)(2,1)S(1)}, bf16[256,512]{1,0:T(8,128)(2,1)S(1)}, u32[]{:S(2)}, u32[]{:S(2)}) %collective-permute-start.23) | collective-permute-done | bytes 262176 | tf_op jit(solution)/shard_map/ppermute | solution.py:275
  129.0 1.0 copy-done.6
  130.0 2.5 %stats.1 = f32[3,128,1024]{2,1,0:T(8,128)} custom-call(s32[1]{0:T(128)} %bitcast.refs_0_.cut_ref, bf16[512,384]{1,0:T(8,128)(2,1)S(1)} %bitcast.47, bf16[512,384]{1,0:T(8,128)(2,1)S(1)} %collective-permute-done.7.refs_1_.refs_2_, bf16[512,384]{1,0:T(8,128)(2,1)S(1)} %collective-permute-done.8.refs_2_.refs_3_, ...), custom_call_target="tpu_custom_call" | custom-call | tf_op jit(solution)/shard_map/stats/pallas_call | solution.py:45
  132.5 2.7 %all-to-all-done.2 = bf16[32,16,512]{2,1,0:T(8,128)(2,1)S(1)} async-done(((bf16[32,16,512]{2,1,0:T(8,128)(2,1)}), bf16[32,16,512]{2,1,0:T(8,128)(2,1)S(1)}, u32[]{:S(2)}, u32[]{:S(2)}) %all-to-all-start.2) | async-done | bytes 524320 | tf_op jit(solution)/shard_map/all_to_all | solution.py:278
  135.3 1.2 unpack.1
  (44 shorter events, 0.5 us)
Async XLA Ops:
  2.4 0.9 copy-start.15
  3.3 0.7 copy-start.17
  31.3 17.8 %collective-permute-start.5 = (bf16[512,384]{1,0:T(8,128)(2,1)S(1)}, bf16[512,384]{1,0:T(8,128)(2,1)S(1)}, u32[]{:S(2)}, u32[]{:S(2)}) collective-permute-start(bf16[512,384]{1,0:T(8,128)(2,1)S(1)} %bitcast.49), channel_id=1, source_target_pairs={{0,6},{1,7},{2,0},{3,1},{4,2},{5,3},{6,4},{7,5},{8,14},{9,15},{10,... | collective-permute-start | bytes 1179656 | tf_op jit(solution)/shard_map/ppermute | solution.py:270
  34.1 15.0 %collective-permute-start.3 = (bf16[512,384]{1,0:T(8,128)(2,1)S(1)}, bf16[512,384]{1,0:T(8,128)(2,1)S(1)}, u32[]{:S(2)}, u32[]{:S(2)}) collective-permute-start(bf16[512,384]{1,0:T(8,128)(2,1)S(1)} %bitcast.50), channel_id=1, source_target_pairs={{0,4},{1,5},{2,6},{3,7},{4,0},{5,1},{6,2},{7,3},{8,12},{9,13},{10,... | collective-permute-start | bytes 1179656 | tf_op jit(solution)/shard_map/ppermute | solution.py:270
  34.9 17.9 %collective-permute-start.1 = (bf16[512,384]{1,0:T(8,128)(2,1)S(1)}, bf16[512,384]{1,0:T(8,128)(2,1)S(1)}, u32[]{:S(2)}, u32[]{:S(2)}) collective-permute-start(bf16[512,384]{1,0:T(8,128)(2,1)S(1)} %bitcast.51), channel_id=1, source_target_pairs={{0,2},{1,3},{2,4},{3,5},{4,6},{5,7},{6,0},{7,1},{8,10},{9,11},{10,... | collective-permute-start | bytes 1179656 | tf_op jit(solution)/shard_map/ppermute | solution.py:270
  35.8 18.4 %all-to-all-start.1 = ((bf16[32,16,384]{2,1,0:T(8,128)(2,1)}), bf16[32,16,384]{2,1,0:T(8,128)(2,1)S(1)}, u32[]{:S(2)}, u32[]{:S(2)}) async-start(bf16[32,16,384]{2,1,0:T(8,128)(2,1)} %bitcast.5), calls=%async_computation.1 | async-start | bytes 786432 | tf_op jit(solution)/shard_map/all_to_all | solution.py:278
  40.6 12.2 %collective-permute-start = (bf16[512,384]{1,0:T(8,128)(2,1)S(1)}, bf16[512,384]{1,0:T(8,128)(2,1)S(1)}, u32[]{:S(2)}, u32[]{:S(2)}) collective-permute-start(bf16[512,384]{1,0:T(8,128)(2,1)S(1)} %bitcast.52), channel_id=1, source_target_pairs={{0,1},{1,0},{2,3},{3,2},{4,5},{5,4},{6,7},{7,6},{8,9},{9,8},{10,11... | collective-permute-start | bytes 1179656 | tf_op jit(solution)/shard_map/ppermute | solution.py:275
  49.1 5.1 %collective-permute-start.6 = (bf16[512,384]{1,0:T(8,128)(2,1)S(1)}, bf16[512,384]{1,0:T(8,128)(2,1)S(1)}, u32[]{:S(2)}, u32[]{:S(2)}) collective-permute-start(bf16[512,384]{1,0:T(8,128)(2,1)S(1)} %collective-permute-done.5.refs_4_), channel_id=1, source_target_pairs={{0,1},{1,0},{2,3},{3,2},{4,5},{5,4},{6,7},{7,6},{8,9},{9,8},{10,11... | collective-permute-start | bytes 1179656 | tf_op jit(solution)/shard_map/ppermute | solution.py:275
  49.1 5.8 %collective-permute-start.4 = (bf16[512,384]{1,0:T(8,128)(2,1)S(1)}, bf16[512,384]{1,0:T(8,128)(2,1)S(1)}, u32[]{:S(2)}, u32[]{:S(2)}) collective-permute-start(bf16[512,384]{1,0:T(8,128)(2,1)S(1)} %collective-permute-done.3.refs_3_), channel_id=1, source_target_pairs={{0,1},{1,0},{2,3},{3,2},{4,5},{5,4},{6,7},{7,6},{8,9},{9,8},{10,11... | collective-permute-start | bytes 1179656 | tf_op jit(solution)/shard_map/ppermute | solution.py:275
  52.8 2.9 %collective-permute-start.2 = (bf16[512,384]{1,0:T(8,128)(2,1)S(1)}, bf16[512,384]{1,0:T(8,128)(2,1)S(1)}, u32[]{:S(2)}, u32[]{:S(2)}) collective-permute-start(bf16[512,384]{1,0:T(8,128)(2,1)S(1)} %collective-permute-done.1.refs_2_), channel_id=1, source_target_pairs={{0,1},{1,0},{2,3},{3,2},{4,5},{5,4},{6,7},{7,6},{8,9},{9,8},{10,11... | collective-permute-start | bytes 1179656 | tf_op jit(solution)/shard_map/ppermute | solution.py:275
  52.8 0.8 copy-start.7
  54.2 0.7 copy-start.9
  54.9 0.8 copy-start.11
  55.7 0.7 copy-start.13
  56.5 3.9 %collective-permute-start.10 = (bf16[512,384]{1,0:T(8,128)(2,1)S(1)}, bf16[512,384]{1,0:T(8,128)(2,1)S(1)}, u32[]{:S(2)}, u32[]{:S(2)}) collective-permute-start(bf16[512,384]{1,0:T(8,128)(2,1)S(1)} %bitcast.42), channel_id=1, source_target_pairs={{0,1},{1,0},{2,3},{3,2},{4,5},{5,4},{6,7},{7,6},{8,9},{9,8},{10,11... | collective-permute-start | bytes 1179656 | tf_op jit(solution)/shard_map/ppermute | solution.py:275
  56.5 19.9 %collective-permute-start.9 = (bf16[512,384]{1,0:T(8,128)(2,1)S(1)}, bf16[512,384]{1,0:T(8,128)(2,1)S(1)}, u32[]{:S(2)}, u32[]{:S(2)}) collective-permute-start(bf16[512,384]{1,0:T(8,128)(2,1)S(1)} %bitcast.43), channel_id=1, source_target_pairs={{0,6},{1,7},{2,0},{3,1},{4,2},{5,3},{6,4},{7,5},{8,14},{9,15},{10,... | collective-permute-start | bytes 1179656 | tf_op jit(solution)/shard_map/ppermute | solution.py:270
  58.8 17.5 %collective-permute-start.8 = (bf16[512,384]{1,0:T(8,128)(2,1)S(1)}, bf16[512,384]{1,0:T(8,128)(2,1)S(1)}, u32[]{:S(2)}, u32[]{:S(2)}) collective-permute-start(bf16[512,384]{1,0:T(8,128)(2,1)S(1)} %bitcast.44), channel_id=1, source_target_pairs={{0,4},{1,5},{2,6},{3,7},{4,0},{5,1},{6,2},{7,3},{8,12},{9,13},{10,... | collective-permute-start | bytes 1179656 | tf_op jit(solution)/shard_map/ppermute | solution.py:270
  60.3 19.7 %collective-permute-start.7 = (bf16[512,384]{1,0:T(8,128)(2,1)S(1)}, bf16[512,384]{1,0:T(8,128)(2,1)S(1)}, u32[]{:S(2)}, u32[]{:S(2)}) collective-permute-start(bf16[512,384]{1,0:T(8,128)(2,1)S(1)} %bitcast.45), channel_id=1, source_target_pairs={{0,2},{1,3},{2,4},{3,5},{4,6},{5,7},{6,0},{7,1},{8,10},{9,11},{10,... | collective-permute-start | bytes 1179656 | tf_op jit(solution)/shard_map/ppermute | solution.py:270
  60.3 1.9 %copy-start = (bf16[1,3072,512]{2,1,0:T(8,128)(2,1)S(1)}, bf16[1,3072,512]{2,1,0:T(8,128)(2,1)}, u32[]{:S(2)}) copy-start(bf16[1,3072,512]{2,1,0:T(8,128)(2,1)} %param.11) | copy-start | bytes 9437188
  62.2 1.9 %copy-start.2 = (bf16[1,3072,512]{2,1,0:T(8,128)(2,1)S(1)}, bf16[1,3072,512]{2,1,0:T(8,128)(2,1)}, u32[]{:S(2)}) copy-start(bf16[1,3072,512]{2,1,0:T(8,128)(2,1)} %param.12) | copy-start | bytes 9437188
  64.1 1.0 copy-start.8
  65.1 1.0 copy-start.10
  66.1 1.0 copy-start.12
  67.1 1.0 copy-start.14
  68.1 4.2 %copy-start.4 = (bf16[1,512,3072]{2,1,0:T(8,128)(2,1)S(1)}, bf16[1,512,3072]{2,1,0:T(8,128)(2,1)}, u32[]{:S(2)}) copy-start(bf16[1,512,3072]{2,1,0:T(8,128)(2,1)} %param.13) | copy-start | bytes 9437188
  72.2 8.3 %collective-permute-start.14 = (bf16[256,512]{1,0:T(8,128)(2,1)S(1)}, bf16[256,512]{1,0:T(8,128)(2,1)S(1)}, u32[]{:S(2)}, u32[]{:S(2)}) collective-permute-start(bf16[256,512]{1,0:T(8,128)(2,1)S(1)} %get-tuple-element.46), channel_id=1, source_target_pairs={{0,1},{1,0},{2,3},{3,2},{4,5},{5,4},{6,7},{7,6},{8,9},{9,8},{10,11... | collective-permute-start | bytes 786440 | tf_op jit(solution)/shard_map/ppermute | solution.py:275
  80.0 1.7 %collective-permute-start.11 = (bf16[512,384]{1,0:T(8,128)(2,1)S(1)}, bf16[512,384]{1,0:T(8,128)(2,1)S(1)}, u32[]{:S(2)}, u32[]{:S(2)}) collective-permute-start(bf16[512,384]{1,0:T(8,128)(2,1)S(1)} %collective-permute-done.7.refs_1_.refs_2_), channel_id=1, source_target_pairs={{0,1},{1,0},{2,3},{3,2},{4,5},{5,4},{6,7},{7,6},{8,9},{9,8},{10,11... | collective-permute-start | bytes 1179656 | tf_op jit(solution)/shard_map/ppermute | solution.py:275
  80.0 2.3 %collective-permute-start.12 = (bf16[512,384]{1,0:T(8,128)(2,1)S(1)}, bf16[512,384]{1,0:T(8,128)(2,1)S(1)}, u32[]{:S(2)}, u32[]{:S(2)}) collective-permute-start(bf16[512,384]{1,0:T(8,128)(2,1)S(1)} %collective-permute-done.8.refs_2_.refs_3_), channel_id=1, source_target_pairs={{0,1},{1,0},{2,3},{3,2},{4,5},{5,4},{6,7},{7,6},{8,9},{9,8},{10,11... | collective-permute-start | bytes 1179656 | tf_op jit(solution)/shard_map/ppermute | solution.py:275
  80.5 2.3 %collective-permute-start.13 = (bf16[512,384]{1,0:T(8,128)(2,1)S(1)}, bf16[512,384]{1,0:T(8,128)(2,1)S(1)}, u32[]{:S(2)}, u32[]{:S(2)}) collective-permute-start(bf16[512,384]{1,0:T(8,128)(2,1)S(1)} %collective-permute-done.9.refs_3_.refs_4_), channel_id=1, source_target_pairs={{0,1},{1,0},{2,3},{3,2},{4,5},{5,4},{6,7},{7,6},{8,9},{9,8},{10,11... | collective-permute-start | bytes 1179656 | tf_op jit(solution)/shard_map/ppermute | solution.py:275
  80.6 8.8 %collective-permute-start.15 = (bf16[256,512]{1,0:T(8,128)(2,1)S(1)}, bf16[256,512]{1,0:T(8,128)(2,1)S(1)}, u32[]{:S(2)}, u32[]{:S(2)}) collective-permute-start(bf16[256,512]{1,0:T(8,128)(2,1)S(1)} %add_convert_fusion.4), channel_id=1, source_target_pairs={{0,2},{1,3},{2,0},{3,1},{4,6},{5,7},{6,4},{7,5},{8,10},{9,11},{10,... | collective-permute-start | bytes 786440 | tf_op jit(solution)/shard_map/ppermute | solution.py:327
  82.9 1.7 %copy-start.5 = (bf16[512,384]{1,0:T(8,128)(2,1)}, bf16[512,384]{1,0:T(8,128)(2,1)S(1)}, u32[]{:S(2)}) copy-start(bf16[512,384]{1,0:T(8,128)(2,1)S(1)} %collective-permute-done.13.refs_6_.refs_8_) | copy-start | bytes 1179652
  82.9 2.0 %copy-start.1 = (bf16[1,3072,512]{2,1,0:T(8,128)(2,1)S(1)}, bf16[1,3072,512]{2,1,0:T(8,128)(2,1)}, u32[]{:S(2)}) copy-start(bf16[1,3072,512]{2,1,0:T(8,128)(2,1)} %param.11) | copy-start | bytes 9437188
  82.9 3.0 %copy-start.3 = (bf16[1,3072,512]{2,1,0:T(8,128)(2,1)S(1)}, bf16[1,3072,512]{2,1,0:T(8,128)(2,1)}, u32[]{:S(2)}) copy-start(bf16[1,3072,512]{2,1,0:T(8,128)(2,1)} %param.12) | copy-start | bytes 9437188
  89.5 3.0 %collective-permute-start.16 = (bf16[3,528,384]{2,1,0:T(8,128)(2,1)S(1)}, bf16[3,528,384]{2,1,0:T(8,128)(2,1)S(1)}, u32[]{:S(2)}, u32[]{:S(2)}) collective-permute-start(bf16[3,528,384]{2,1,0:T(8,128)(2,1)S(1)} %get-tuple-element.50), channel_id=1, source_target_pairs={{0,1},{1,0},{2,3},{3,2},{4,5},{5,4},{6,7},{7,6},{8,9},{9,8},{10,11... | collective-permute-start | bytes 3649544 | tf_op jit(solution)/shard_map/ppermute | solution.py:275
  92.6 8.7 %collective-permute-start.20 = (bf16[272,384]{1,0:T(8,128)(2,1)S(1)}, bf16[272,384]{1,0:T(8,128)(2,1)S(1)}, u32[]{:S(2)}, u32[]{:S(2)}) collective-permute-start(bf16[272,384]{1,0:T(8,128)(2,1)S(1)} %slice_bitcast_fusion), channel_id=1, source_target_pairs={{0,6},{1,7},{2,0},{3,1},{4,2},{5,3},{6,4},{7,5},{8,14},{9,15},{10,... | collective-permute-start | bytes 626696 | tf_op jit(solution)/shard_map/ppermute | solution.py:270
  93.3 8.0 %collective-permute-start.18 = (bf16[256,384]{1,0:T(8,128)(2,1)S(1)}, bf16[256,384]{1,0:T(8,128)(2,1)S(1)}, u32[]{:S(2)}, u32[]{:S(2)}) collective-permute-start(bf16[256,384]{1,0:T(8,128)(2,1)S(1)} %slice_bitcast_fusion.1), channel_id=1, source_target_pairs={{0,2},{1,3},{2,4},{3,5},{4,6},{5,7},{6,0},{7,1},{8,10},{9,11},{10,... | collective-permute-start | bytes 589832 | tf_op jit(solution)/shard_map/ppermute | solution.py:270
  95.8 7.8 %collective-permute-start.17 = (bf16[1,528,384]{2,1,0:T(8,128)(2,1)S(1)}, bf16[1,528,384]{2,1,0:T(8,128)(2,1)S(1)}, u32[]{:S(2)}, u32[]{:S(2)}) collective-permute-start(bf16[1,528,384]{2,1,0:T(8,128)(2,1)S(1)} %get-tuple-element.52), channel_id=1, source_target_pairs={{0,1},{1,0},{2,3},{3,2},{4,5},{5,4},{6,7},{7,6},{8,9},{9,8},{10,11... | collective-permute-start | bytes 1216520 | tf_op jit(solution)/shard_map/ppermute | solution.py:275
  101.5 10.3 %collective-permute-start.21 = (bf16[528,384]{1,0:T(8,128)(2,1)S(1)}, bf16[528,384]{1,0:T(8,128)(2,1)S(1)}, u32[]{:S(2)}, u32[]{:S(2)}) collective-permute-start(bf16[528,384]{1,0:T(8,128)(2,1)S(1)} %get-tuple-element.57), channel_id=1, source_target_pairs={{0,6},{1,7},{2,0},{3,1},{4,2},{5,3},{6,4},{7,5},{8,14},{9,15},{10,... | collective-permute-start | bytes 1216520 | tf_op jit(solution)/shard_map/ppermute | solution.py:270
  102.0 11.5 %collective-permute-start.19 = (bf16[528,384]{1,0:T(8,128)(2,1)S(1)}, bf16[528,384]{1,0:T(8,128)(2,1)S(1)}, u32[]{:S(2)}, u32[]{:S(2)}) collective-permute-start(bf16[528,384]{1,0:T(8,128)(2,1)S(1)} %get-tuple-element.58), channel_id=1, source_target_pairs={{0,2},{1,3},{2,4},{3,5},{4,6},{5,7},{6,0},{7,1},{8,10},{9,11},{10,... | collective-permute-start | bytes 1216520 | tf_op jit(solution)/shard_map/ppermute | solution.py:270
  114.7 20.6 %all-to-all-start.2 = ((bf16[32,16,512]{2,1,0:T(8,128)(2,1)}), bf16[32,16,512]{2,1,0:T(8,128)(2,1)S(1)}, u32[]{:S(2)}, u32[]{:S(2)}) async-start(bf16[32,16,512]{2,1,0:T(8,128)(2,1)} %bitcast.16), calls=%async_computation.2 | async-start | bytes 1048576 | tf_op jit(solution)/shard_map/all_to_all | solution.py:278
  119.3 8.0 %collective-permute-start.22 = (bf16[256,512]{1,0:T(8,128)(2,1)S(1)}, bf16[256,512]{1,0:T(8,128)(2,1)S(1)}, u32[]{:S(2)}, u32[]{:S(2)}) collective-permute-start(bf16[256,512]{1,0:T(8,128)(2,1)S(1)} %add_convert_fusion.3.refs_3_), channel_id=1, source_target_pairs={{0,4},{1,5},{2,6},{3,7},{4,0},{5,1},{6,2},{7,3},{8,12},{9,13},{10,... | collective-permute-start | bytes 786440 | tf_op jit(solution)/shard_map/ppermute | solution.py:327
  127.3 7.9 %copy-start.16 = (f32[256]{0:T(256)S(1)}, f32[256]{0:T(256)}, u32[]{:S(2)}) copy-start(f32[256]{0:T(256)} %param.9) | copy-start | bytes 3076
  127.4 1.6 %collective-permute-start.23 = (bf16[256,512]{1,0:T(8,128)(2,1)S(1)}, bf16[256,512]{1,0:T(8,128)(2,1)S(1)}, u32[]{:S(2)}, u32[]{:S(2)}) collective-permute-start(bf16[256,512]{1,0:T(8,128)(2,1)S(1)} %add_convert_fusion.2.refs_9_), channel_id=1, source_target_pairs={{0,1},{1,0},{2,3},{3,2},{4,5},{5,4},{6,7},{7,6},{8,9},{9,8},{10,11... | collective-permute-start | bytes 786440 | tf_op jit(solution)/shard_map/ppermute | solution.py:275
  129.0 1.0 copy-start.6

commit v5 on v4

--- a/solution.py
+++ b/solution.py
@@ -54,7 +54,7 @@
     )(*inputs, *after)
 
 
-def pack_kernel(capacity, cut_ref, ids_ref, tok_ref, wt_ref, tok_out, wt_out, slot_out):
+def pack_kernel(capacity, cut_ref, ids_ref, tok_ref, tok_out, slot_out):
     ids = ids_ref[...]
     rows = ids.shape[1]
     total = tok_out.shape[0]
@@ -66,6 +66,11 @@
     slot_out[...] = jnp.broadcast_to(slot, slot_out.shape)
     place = (slot == iota((total, rows), 0)).astype(F32).astype(BF16)
     tok_out[...] = dot(place, tok_ref[...]).astype(BF16)
+
+
+def pack_wt_kernel(slot_ref, wt_ref, wt_out):
+    shape = (wt_out.shape[0], slot_ref.shape[1])
+    place = (slot_ref[:1] == iota(shape, 0)).astype(F32).astype(BF16)
     wt_out[...] = dot(place, wt_ref[...]).astype(BF16)
 
 
@@ -279,22 +284,27 @@
 
     ids = expert_ids.reshape(1, tok_rows)
     logit = gate_logit.reshape(1, tok_rows)
-    score = jax.nn.sigmoid(gate_logit)
-    weighted = (score[:, None] * out_grad.astype(F32)).astype(BF16)
-    tok_pack, wt_pack, slot = call(
+    tok_pack, slot = call(
         functools.partial(pack_kernel, capacity),
-        [
-            shape((total, width), BF16),
-            shape((total, width), BF16),
-            shape((8, tok_rows), jnp.int32),
-        ],
-        (where, ids, tokens, weighted),
+        [shape((total, width), BF16), shape((8, tok_rows), jnp.int32)],
+        (where, ids, tokens),
         0,
         "pack",
         limit=8,
     )
     tok_in = exchange(tok_pack.reshape(experts, capacity, width)).reshape(total, width)
-    wt_pack, tok_in = lax.optimization_barrier((wt_pack, tok_in))
+    late_grad, late_logit, tok_in = lax.optimization_barrier((out_grad, gate_logit, tok_in))
+    score = jax.nn.sigmoid(late_logit)
+    weighted = (score[:, None] * late_grad.astype(F32)).astype(BF16)
+    (wt_pack,) = call(
+        pack_wt_kernel,
+        [shape((total, width), BF16)],
+        (slot, weighted),
+        0,
+        "pack_wt",
+        scalars=0,
+        limit=8,
+    )
     wt_in = exchange(wt_pack.reshape(experts, capacity, width)).reshape(total, width)
     mid = total // 2
     tok_near = [hop(tok_in, k) for k in range(chips)]

time: 137 us -> 137 us (level)
    ppermute x10, waiting for transfers between devices: 33.8 us -> 31 us  [hop(): lax.ppermute(x, 'cuts', [(2 * i + c, 2 * ((i + k) % chips) + c) for i in...]
    all_to_all x2, waiting for transfers between devices: 3.34 us -> 6.11 us  [exchange(): return lax.all_to_all(x, 'expert', split_axis=0, concat_axis=0, tiled=True)]
    pallas_call x7 -> x8, Pallas kernels: 12.7 us -> 12.8 us  [call(): pl.pallas_call(kernel, out_shape=out, in_specs=specs, out_specs=[whole()]...]
  transfers between devices with their start and end apart: 26 -> 26, of which waited for: 16 -> 16; matrix products, arithmetic and copies ran while one was open for 0% -> 2% of each run, Pallas kernels for 10% -> 10%
where the time goes in v5:
time: 137 us
  waiting for transfers between devices  51.6 us (38%)
  blocking collectives  26 us (19%)
  starting transfers between devices  24.1 us (18%)
  Pallas kernels  16.9 us (12%)
  local copies, waits for them, and re-layouts  14.7 us (11%)
  other arithmetic  2.38 us (2%)
    ppermute x10, waiting for transfers between devices, hop(): lax.ppermute(x, 'cuts', [(2 * i + c, 2 * ((i + k) % chips) + c) for i in...  31 us
    all_to_all x1, blocking collectives, exchange(): return lax.all_to_all(x, 'expert', split_axis=0, concat_axis=0, tiled=True)  26 us
    unnamed x36, local copies, waits for them, and re-layouts  14.6 us
    pallas_call x8, Pallas kernels, call(): pl.pallas_call(kernel, out_shape=out, in_specs=specs, out_specs=[whole()]...  12.8 us
    ppermute x10, starting transfers between devices, hop(): lax.ppermute(x, 'cuts', [(2 * i + c, 2 * ((i + k) % chips) + c) for i in...  12.6 us
    all_to_all x2, starting transfers between devices, exchange(): return lax.all_to_all(x, 'expert', split_axis=0, concat_axis=0, tiled=True)  9.43 us
    ppermute x2, waiting for transfers between devices, chip_swap(): lax.ppermute(x, 'cuts', [(2 * i + c, 2 * (i ^ bit) + c) for i in range(ch...  7.96 us
    ppermute x12, waiting for transfers between devices, swap(): return lax.ppermute(x, 'cuts', [(i, i ^ 1) for i in range(cuts)])  6.54 us
  transfers between devices with their start and end apart: 26, of which 16 were waited for; matrix products, arithmetic and copies ran while one was open for 2% of the time, Pallas kernels for 10%

profile of v5, /device:TPU:32, one launch (start us, length us, event | category | flops | bytes accessed | tf_op | source)
XLA Modules:
  0.0 136.6 jit_solution(15334208799802985501)
XLA Ops:
  0.6 0.9 copy-done.15
  1.6 0.7 copy-done.17
  2.2 0.5 pack.1
  2.7 26.0 %all_to_all.15 = bf16[32,16,384]{2,1,0:T(8,128)(2,1)S(1)} all-to-all(bf16[32,16,384]{2,1,0:T(8,128)(2,1)S(1)} %bitcast.54), channel_id=1, replica_groups=mesh['expert'=32,'cuts'=8] {'expert'}, dimensions={0} | all-to-all | bytes 786432 | tf_op jit(solution)/shard_map/all_to_all | solution.py:283
  28.7 2.8 %collective-permute-start.5 = (bf16[512,384]{1,0:T(8,128)(2,1)S(1)}, bf16[512,384]{1,0:T(8,128)(2,1)S(1)}, u32[]{:S(2)}, u32[]{:S(2)}) collective-permute-start(bf16[512,384]{1,0:T(8,128)(2,1)S(1)} %bitcast.49), channel_id=1, source_target_pairs={{0,6},{1,7},{2,0},{3,1},{4,2},{5,3},{6,4},{7,5},{8,14},{9,15},{10,... | collective-permute-start | bytes 1179656 | tf_op jit(solution)/shard_map/ppermute | solution.py:275
  31.5 0.8 collective-permute-start.3
  32.3 0.9 collective-permute-start.1
  33.2 0.7 add_divide_fusion
  33.9 1.0 multiply_convert_fusion.refs_1_
  34.9 1.0 pack_wt.1
  36.0 4.8 %all-to-all-start.1 = ((bf16[32,16,384]{2,1,0:T(8,128)(2,1)}), bf16[32,16,384]{2,1,0:T(8,128)(2,1)S(1)}, u32[]{:S(2)}, u32[]{:S(2)}) async-start(bf16[32,16,384]{2,1,0:T(8,128)(2,1)} %bitcast.5), calls=%async_computation.1 | async-start | bytes 786432 | tf_op jit(solution)/shard_map/all_to_all | solution.py:283
  40.8 5.7 %collective-permute-done.5.refs_4_ = bf16[512,384]{1,0:T(8,128)(2,1)S(1)} collective-permute-done((bf16[512,384]{1,0:T(8,128)(2,1)S(1)}, bf16[512,384]{1,0:T(8,128)(2,1)S(1)}, u32[]{:S(2)}, u32[]{:S(2)}) %collective-permute-start.5) | collective-permute-done | bytes 393248 | tf_op jit(solution)/shard_map/ppermute | solution.py:275
  46.5 0.5 collective-permute-start.4
  47.0 3.2 %collective-permute-done.1.refs_2_ = bf16[512,384]{1,0:T(8,128)(2,1)S(1)} collective-permute-done((bf16[512,384]{1,0:T(8,128)(2,1)S(1)}, bf16[512,384]{1,0:T(8,128)(2,1)S(1)}, u32[]{:S(2)}, u32[]{:S(2)}) %collective-permute-start.1) | collective-permute-done | bytes 393248 | tf_op jit(solution)/shard_map/ppermute | solution.py:275
  50.2 0.8 copy-done.7
  50.9 3.4 %all-to-all-done.1 = bf16[32,16,384]{2,1,0:T(8,128)(2,1)S(1)} async-done(((bf16[32,16,384]{2,1,0:T(8,128)(2,1)}), bf16[32,16,384]{2,1,0:T(8,128)(2,1)S(1)}, u32[]{:S(2)}, u32[]{:S(2)}) %all-to-all-start.1) | async-done | bytes 393248 | tf_op jit(solution)/shard_map/all_to_all | solution.py:283
  54.4 0.7 copy-done.9
  55.1 0.8 copy-done.11
  55.9 0.7 copy-done.13
  56.6 2.3 %collective-permute-start.9 = (bf16[512,384]{1,0:T(8,128)(2,1)S(1)}, bf16[512,384]{1,0:T(8,128)(2,1)S(1)}, u32[]{:S(2)}, u32[]{:S(2)}) collective-permute-start(bf16[512,384]{1,0:T(8,128)(2,1)S(1)} %bitcast.43), channel_id=1, source_target_pairs={{0,6},{1,7},{2,0},{3,1},{4,2},{5,3},{6,4},{7,5},{8,14},{9,15},{10,... | collective-permute-start | bytes 1179656 | tf_op jit(solution)/shard_map/ppermute | solution.py:275
  59.0 1.5 %collective-permute-start.8 = (bf16[512,384]{1,0:T(8,128)(2,1)S(1)}, bf16[512,384]{1,0:T(8,128)(2,1)S(1)}, u32[]{:S(2)}, u32[]{:S(2)}) collective-permute-start(bf16[512,384]{1,0:T(8,128)(2,1)S(1)} %bitcast.44), channel_id=1, source_target_pairs={{0,4},{1,5},{2,6},{3,7},{4,0},{5,1},{6,2},{7,3},{8,12},{9,13},{10,... | collective-permute-start | bytes 1179656 | tf_op jit(solution)/shard_map/ppermute | solution.py:275
  60.5 1.9 %copy-done = bf16[1,3072,512]{2,1,0:T(8,128)(2,1)S(1)} copy-done((bf16[1,3072,512]{2,1,0:T(8,128)(2,1)S(1)}, bf16[1,3072,512]{2,1,0:T(8,128)(2,1)}, u32[]{:S(2)}) %copy-start) | copy-done | bytes 3145752
  62.4 1.9 %copy-done.2 = bf16[1,3072,512]{2,1,0:T(8,128)(2,1)S(1)} copy-done((bf16[1,3072,512]{2,1,0:T(8,128)(2,1)S(1)}, bf16[1,3072,512]{2,1,0:T(8,128)(2,1)}, u32[]{:S(2)}) %copy-start.2) | copy-done | bytes 3145752
  64.3 1.0 copy-done.8
  65.3 1.0 copy-done.10
  66.3 1.0 copy-done.12
  67.3 1.0 copy-done.14
  68.3 4.1 %gates.1 = (bf16[512,512]{1,0:T(8,128)(2,1)S(1)}, f32[512,512]{1,0:T(8,128)S(1)}, f32[512,512]{1,0:T(8,128)S(1)}, bf16[256,512]{1,0:T(8,128)(2,1)S(1)}, bf16[256,512]{1,0:T(8,128)(2,1)S(1)}) custom-call(s32[1]{0:T(128)} %bitcast.refs_0_.cut_ref, bf16[512,384]{1,0:T(8,128)(2,1)S(1)} %bitcast.53, bf16[512,384]{1,0:T(8,128)(2,1)S(1)} %collective-permute-done.1.refs_2_, ...), custom_call_target="tpu_custom_call" | custom-call | tf_op jit(solution)/shard_map/gates/pallas_call | solution.py:45
  72.4 0.1 collective-permute-start.14
  72.5 0.6 own_hidden_grad.1.refs_8_
  73.1 3.4 %collective-permute-done.9.refs_3_.refs_4_ = bf16[512,384]{1,0:T(8,128)(2,1)S(1)} collective-permute-done((bf16[512,384]{1,0:T(8,128)(2,1)S(1)}, bf16[512,384]{1,0:T(8,128)(2,1)S(1)}, u32[]{:S(2)}, u32[]{:S(2)}) %collective-permute-start.9) | collective-permute-done | bytes 393248 | tf_op jit(solution)/shard_map/ppermute | solution.py:275
  76.5 3.7 %collective-permute-done.7.refs_1_.refs_2_ = bf16[512,384]{1,0:T(8,128)(2,1)S(1)} collective-permute-done((bf16[512,384]{1,0:T(8,128)(2,1)S(1)}, bf16[512,384]{1,0:T(8,128)(2,1)S(1)}, u32[]{:S(2)}, u32[]{:S(2)}) %collective-permute-start.7) | collective-permute-done | bytes 393248 | tf_op jit(solution)/shard_map/ppermute | solution.py:275
  80.2 0.5 collective-permute-start.12
  80.8 0.1 collective-permute-start.15
  80.9 1.0 collective-permute-done.11.refs_4_.refs_6_
  81.9 0.6 collective-permute-done.12.refs_5_.refs_7_
  82.4 0.6 collective-permute-done.13.refs_6_.refs_8_
  83.0 1.7 %hidden_grad.1 = (bf16[512,1024]{1,0:T(8,128)(2,1)S(1)}, bf16[2,16,384]{2,1,0:T(8,128)(2,1)S(1)}) custom-call(s32[1]{0:T(128)} %bitcast.refs_0_.cut_ref, bf16[512,384]{1,0:T(8,128)(2,1)S(1)} %collective-permute-done.7.refs_1_.refs_2_, bf16[512,384]{1,0:T(8,128)(2,1)S(1)} %collective-permute-done.8.refs_2_.refs_3_, ...), custom_call_target="tpu_custom_call" | custom-call | tf_op jit(solution)/shard_map/hidden_grad/pallas_call | solution.py:45
  84.7 0.3 copy-done.1
  85.0 0.9 copy-done.3
  86.0 3.1 %input_part.2 = (bf16[3,528,384]{2,1,0:T(8,128)(2,1)S(1)}, bf16[3,528,384]{2,1,0:T(8,128)(2,1)S(1)}) custom-call(s32[1]{0:T(128)} %bitcast.refs_0_.cut_ref, bf16[512,1024]{1,0:T(8,128)(2,1)S(1)} %get-tuple-element.42.both_ref, bf16[2,16,384]{2,1,0:T(8,128)(2,1)S(1)} %get-tuple-element.43.tail_ref, bf16[3072,512]{1,0:T(8,128)(2,1)S(1)} %bitcast.30, ...), custom_call_target="tpu_custom_call" | custom-call | flops 2415919104 | bytes 12582912 | tf_op jit(solution)/shard_map/input_part/pallas_call | solution.py:197
  89.1 0.5 collective-permute-done.15
  89.6 0.1 collective-permute-start.16
  89.7 2.9 %collective-permute-done.16 = bf16[3,528,384]{2,1,0:T(8,128)(2,1)S(1)} collective-permute-done((bf16[3,528,384]{2,1,0:T(8,128)(2,1)S(1)}, bf16[3,528,384]{2,1,0:T(8,128)(2,1)S(1)}, u32[]{:S(2)}, u32[]{:S(2)}) %collective-permute-start.16) | collective-permute-done | bytes 1216544 | tf_op jit(solution)/shard_map/ppermute | solution.py:280
  92.6 0.1 add_convert_fusion.1
  92.7 0.7 collective-permute-start.20
  93.5 1.5 %collective-permute-start.18 = (bf16[256,384]{1,0:T(8,128)(2,1)S(1)}, bf16[256,384]{1,0:T(8,128)(2,1)S(1)}, u32[]{:S(2)}, u32[]{:S(2)}) collective-permute-start(bf16[256,384]{1,0:T(8,128)(2,1)S(1)} %slice_bitcast_fusion.1), channel_id=1, source_target_pairs={{0,2},{1,3},{2,4},{3,5},{4,6},{5,7},{6,0},{7,1},{8,10},{9,11},{10,... | collective-permute-start | bytes 589832 | tf_op jit(solution)/shard_map/ppermute | solution.py:275
  95.0 1.0 input_part.3
  96.1 5.3 %collective-permute-done.18 = bf16[256,384]{1,0:T(8,128)(2,1)S(1)} collective-permute-done((bf16[256,384]{1,0:T(8,128)(2,1)S(1)}, bf16[256,384]{1,0:T(8,128)(2,1)S(1)}, u32[]{:S(2)}, u32[]{:S(2)}) %collective-permute-start.18) | collective-permute-done | bytes 196640 | tf_op jit(solution)/shard_map/ppermute | solution.py:275
  101.4 0.3 fusion
  101.7 0.5 collective-permute-start.21
  102.2 1.6 %collective-permute-start.19 = (bf16[528,384]{1,0:T(8,128)(2,1)S(1)}, bf16[528,384]{1,0:T(8,128)(2,1)S(1)}, u32[]{:S(2)}, u32[]{:S(2)}) collective-permute-start(bf16[528,384]{1,0:T(8,128)(2,1)S(1)} %get-tuple-element.58), channel_id=1, source_target_pairs={{0,2},{1,3},{2,4},{3,5},{4,6},{5,7},{6,0},{7,1},{8,10},{9,11},{10,... | collective-permute-start | bytes 1216520 | tf_op jit(solution)/shard_map/ppermute | solution.py:275
  103.8 0.1 fusion.2.refs_0_
  103.9 8.1 %collective-permute-done.21.refs_2_ = bf16[528,384]{1,0:T(8,128)(2,1)S(1)} collective-permute-done((bf16[528,384]{1,0:T(8,128)(2,1)S(1)}, bf16[528,384]{1,0:T(8,128)(2,1)S(1)}, u32[]{:S(2)}, u32[]{:S(2)}) %collective-permute-start.21) | collective-permute-done | bytes 405536 | tf_op jit(solution)/shard_map/ppermute | solution.py:275
  112.0 1.7 %collective-permute-done.19.refs_1_ = bf16[528,384]{1,0:T(8,128)(2,1)S(1)} collective-permute-done((bf16[528,384]{1,0:T(8,128)(2,1)S(1)}, bf16[528,384]{1,0:T(8,128)(2,1)S(1)}, u32[]{:S(2)}, u32[]{:S(2)}) %collective-permute-start.19) | collective-permute-done | bytes 405536 | tf_op jit(solution)/shard_map/ppermute | solution.py:275
  113.7 1.1 final.1.refs_11_
  114.8 4.7 %all-to-all-start.2 = ((bf16[32,16,512]{2,1,0:T(8,128)(2,1)}), bf16[32,16,512]{2,1,0:T(8,128)(2,1)S(1)}, u32[]{:S(2)}, u32[]{:S(2)}) async-start(bf16[32,16,512]{2,1,0:T(8,128)(2,1)} %bitcast.16), calls=%async_computation.2 | async-start | bytes 1048576 | tf_op jit(solution)/shard_map/all_to_all | solution.py:283
  119.5 0.5 collective-permute-start.22
  120.0 7.5 %collective-permute-done.22 = bf16[256,512]{1,0:T(8,128)(2,1)S(1)} collective-permute-done((bf16[256,512]{1,0:T(8,128)(2,1)S(1)}, bf16[256,512]{1,0:T(8,128)(2,1)S(1)}, u32[]{:S(2)}, u32[]{:S(2)}) %collective-permute-start.22) | collective-permute-done | bytes 262176 | tf_op jit(solution)/shard_map/ppermute | solution.py:337
  127.6 1.5 %collective-permute-done.23.refs_10_ = bf16[256,512]{1,0:T(8,128)(2,1)S(1)} collective-permute-done((bf16[256,512]{1,0:T(8,128)(2,1)S(1)}, bf16[256,512]{1,0:T(8,128)(2,1)S(1)}, u32[]{:S(2)}, u32[]{:S(2)}) %collective-permute-start.23) | collective-permute-done | bytes 262176 | tf_op jit(solution)/shard_map/ppermute | solution.py:280
  129.2 1.0 copy-done.6
  130.2 2.5 %stats.1 = f32[3,128,1024]{2,1,0:T(8,128)} custom-call(s32[1]{0:T(128)} %bitcast.refs_0_.cut_ref, bf16[512,384]{1,0:T(8,128)(2,1)S(1)} %bitcast.47, bf16[512,384]{1,0:T(8,128)(2,1)S(1)} %collective-permute-done.7.refs_1_.refs_2_, bf16[512,384]{1,0:T(8,128)(2,1)S(1)} %collective-permute-done.8.refs_2_.refs_3_, ...), custom_call_target="tpu_custom_call" | custom-call | tf_op jit(solution)/shard_map/stats/pallas_call | solution.py:45
  132.7 2.7 %all-to-all-done.2 = bf16[32,16,512]{2,1,0:T(8,128)(2,1)S(1)} async-done(((bf16[32,16,512]{2,1,0:T(8,128)(2,1)}), bf16[32,16,512]{2,1,0:T(8,128)(2,1)S(1)}, u32[]{:S(2)}, u32[]{:S(2)}) %all-to-all-start.2) | async-done | bytes 524320 | tf_op jit(solution)/shard_map/all_to_all | solution.py:283
  135.4 1.2 unpack.1
  (45 shorter events, 0.6 us)
Async XLA Ops:
  0.6 0.9 copy-start.15
  1.6 0.7 copy-start.17
  28.7 17.8 %collective-permute-start.5 = (bf16[512,384]{1,0:T(8,128)(2,1)S(1)}, bf16[512,384]{1,0:T(8,128)(2,1)S(1)}, u32[]{:S(2)}, u32[]{:S(2)}) collective-permute-start(bf16[512,384]{1,0:T(8,128)(2,1)S(1)} %bitcast.49), channel_id=1, source_target_pairs={{0,6},{1,7},{2,0},{3,1},{4,2},{5,3},{6,4},{7,5},{8,14},{9,15},{10,... | collective-permute-start | bytes 1179656 | tf_op jit(solution)/shard_map/ppermute | solution.py:275
  31.5 15.0 %collective-permute-start.3 = (bf16[512,384]{1,0:T(8,128)(2,1)S(1)}, bf16[512,384]{1,0:T(8,128)(2,1)S(1)}, u32[]{:S(2)}, u32[]{:S(2)}) collective-permute-start(bf16[512,384]{1,0:T(8,128)(2,1)S(1)} %bitcast.50), channel_id=1, source_target_pairs={{0,4},{1,5},{2,6},{3,7},{4,0},{5,1},{6,2},{7,3},{8,12},{9,13},{10,... | collective-permute-start | bytes 1179656 | tf_op jit(solution)/shard_map/ppermute | solution.py:275
  32.3 17.9 %collective-permute-start.1 = (bf16[512,384]{1,0:T(8,128)(2,1)S(1)}, bf16[512,384]{1,0:T(8,128)(2,1)S(1)}, u32[]{:S(2)}, u32[]{:S(2)}) collective-permute-start(bf16[512,384]{1,0:T(8,128)(2,1)S(1)} %bitcast.51), channel_id=1, source_target_pairs={{0,2},{1,3},{2,4},{3,5},{4,6},{5,7},{6,0},{7,1},{8,10},{9,11},{10,... | collective-permute-start | bytes 1179656 | tf_op jit(solution)/shard_map/ppermute | solution.py:275
  36.0 18.4 %all-to-all-start.1 = ((bf16[32,16,384]{2,1,0:T(8,128)(2,1)}), bf16[32,16,384]{2,1,0:T(8,128)(2,1)S(1)}, u32[]{:S(2)}, u32[]{:S(2)}) async-start(bf16[32,16,384]{2,1,0:T(8,128)(2,1)} %bitcast.5), calls=%async_computation.1 | async-start | bytes 786432 | tf_op jit(solution)/shard_map/all_to_all | solution.py:283
  40.7 9.5 %collective-permute-start = (bf16[512,384]{1,0:T(8,128)(2,1)S(1)}, bf16[512,384]{1,0:T(8,128)(2,1)S(1)}, u32[]{:S(2)}, u32[]{:S(2)}) collective-permute-start(bf16[512,384]{1,0:T(8,128)(2,1)S(1)} %bitcast.52), channel_id=1, source_target_pairs={{0,1},{1,0},{2,3},{3,2},{4,5},{5,4},{6,7},{7,6},{8,9},{9,8},{10,11... | collective-permute-start | bytes 1179656 | tf_op jit(solution)/shard_map/ppermute | solution.py:280
  46.5 7.9 %collective-permute-start.6 = (bf16[512,384]{1,0:T(8,128)(2,1)S(1)}, bf16[512,384]{1,0:T(8,128)(2,1)S(1)}, u32[]{:S(2)}, u32[]{:S(2)}) collective-permute-start(bf16[512,384]{1,0:T(8,128)(2,1)S(1)} %collective-permute-done.5.refs_4_), channel_id=1, source_target_pairs={{0,1},{1,0},{2,3},{3,2},{4,5},{5,4},{6,7},{7,6},{8,9},{9,8},{10,11... | collective-permute-start | bytes 1179656 | tf_op jit(solution)/shard_map/ppermute | solution.py:280
  46.5 8.6 %collective-permute-start.4 = (bf16[512,384]{1,0:T(8,128)(2,1)S(1)}, bf16[512,384]{1,0:T(8,128)(2,1)S(1)}, u32[]{:S(2)}, u32[]{:S(2)}) collective-permute-start(bf16[512,384]{1,0:T(8,128)(2,1)S(1)} %collective-permute-done.3.refs_3_), channel_id=1, source_target_pairs={{0,1},{1,0},{2,3},{3,2},{4,5},{5,4},{6,7},{7,6},{8,9},{9,8},{10,11... | collective-permute-start | bytes 1179656 | tf_op jit(solution)/shard_map/ppermute | solution.py:280
  50.2 5.7 %collective-permute-start.2 = (bf16[512,384]{1,0:T(8,128)(2,1)S(1)}, bf16[512,384]{1,0:T(8,128)(2,1)S(1)}, u32[]{:S(2)}, u32[]{:S(2)}) collective-permute-start(bf16[512,384]{1,0:T(8,128)(2,1)S(1)} %collective-permute-done.1.refs_2_), channel_id=1, source_target_pairs={{0,1},{1,0},{2,3},{3,2},{4,5},{5,4},{6,7},{7,6},{8,9},{9,8},{10,11... | collective-permute-start | bytes 1179656 | tf_op jit(solution)/shard_map/ppermute | solution.py:280
  50.2 0.8 copy-start.7
  54.4 0.7 copy-start.9
  55.1 0.8 copy-start.11
  55.9 0.7 copy-start.13
  56.6 3.9 %collective-permute-start.10 = (bf16[512,384]{1,0:T(8,128)(2,1)S(1)}, bf16[512,384]{1,0:T(8,128)(2,1)S(1)}, u32[]{:S(2)}, u32[]{:S(2)}) collective-permute-start(bf16[512,384]{1,0:T(8,128)(2,1)S(1)} %bitcast.42), channel_id=1, source_target_pairs={{0,1},{1,0},{2,3},{3,2},{4,5},{5,4},{6,7},{7,6},{8,9},{9,8},{10,11... | collective-permute-start | bytes 1179656 | tf_op jit(solution)/shard_map/ppermute | solution.py:280
  56.6 19.9 %collective-permute-start.9 = (bf16[512,384]{1,0:T(8,128)(2,1)S(1)}, bf16[512,384]{1,0:T(8,128)(2,1)S(1)}, u32[]{:S(2)}, u32[]{:S(2)}) collective-permute-start(bf16[512,384]{1,0:T(8,128)(2,1)S(1)} %bitcast.43), channel_id=1, source_target_pairs={{0,6},{1,7},{2,0},{3,1},{4,2},{5,3},{6,4},{7,5},{8,14},{9,15},{10,... | collective-permute-start | bytes 1179656 | tf_op jit(solution)/shard_map/ppermute | solution.py:275
  59.0 17.5 %collective-permute-start.8 = (bf16[512,384]{1,0:T(8,128)(2,1)S(1)}, bf16[512,384]{1,0:T(8,128)(2,1)S(1)}, u32[]{:S(2)}, u32[]{:S(2)}) collective-permute-start(bf16[512,384]{1,0:T(8,128)(2,1)S(1)} %bitcast.44), channel_id=1, source_target_pairs={{0,4},{1,5},{2,6},{3,7},{4,0},{5,1},{6,2},{7,3},{8,12},{9,13},{10,... | collective-permute-start | bytes 1179656 | tf_op jit(solution)/shard_map/ppermute | solution.py:275
  60.5 19.7 %collective-permute-start.7 = (bf16[512,384]{1,0:T(8,128)(2,1)S(1)}, bf16[512,384]{1,0:T(8,128)(2,1)S(1)}, u32[]{:S(2)}, u32[]{:S(2)}) collective-permute-start(bf16[512,384]{1,0:T(8,128)(2,1)S(1)} %bitcast.45), channel_id=1, source_target_pairs={{0,2},{1,3},{2,4},{3,5},{4,6},{5,7},{6,0},{7,1},{8,10},{9,11},{10,... | collective-permute-start | bytes 1179656 | tf_op jit(solution)/shard_map/ppermute | solution.py:275
  60.5 1.9 %copy-start = (bf16[1,3072,512]{2,1,0:T(8,128)(2,1)S(1)}, bf16[1,3072,512]{2,1,0:T(8,128)(2,1)}, u32[]{:S(2)}) copy-start(bf16[1,3072,512]{2,1,0:T(8,128)(2,1)} %param.11) | copy-start | bytes 9437188
  62.4 1.9 %copy-start.2 = (bf16[1,3072,512]{2,1,0:T(8,128)(2,1)S(1)}, bf16[1,3072,512]{2,1,0:T(8,128)(2,1)}, u32[]{:S(2)}) copy-start(bf16[1,3072,512]{2,1,0:T(8,128)(2,1)} %param.12) | copy-start | bytes 9437188
  64.3 1.0 copy-start.8
  65.3 1.0 copy-start.10
  66.3 1.0 copy-start.12
  67.3 1.0 copy-start.14
  68.3 4.2 %copy-start.4 = (bf16[1,512,3072]{2,1,0:T(8,128)(2,1)S(1)}, bf16[1,512,3072]{2,1,0:T(8,128)(2,1)}, u32[]{:S(2)}) copy-start(bf16[1,512,3072]{2,1,0:T(8,128)(2,1)} %param.13) | copy-start | bytes 9437188
  72.4 8.3 %collective-permute-start.14 = (bf16[256,512]{1,0:T(8,128)(2,1)S(1)}, bf16[256,512]{1,0:T(8,128)(2,1)S(1)}, u32[]{:S(2)}, u32[]{:S(2)}) collective-permute-start(bf16[256,512]{1,0:T(8,128)(2,1)S(1)} %get-tuple-element.46), channel_id=1, source_target_pairs={{0,1},{1,0},{2,3},{3,2},{4,5},{5,4},{6,7},{7,6},{8,9},{9,8},{10,11... | collective-permute-start | bytes 786440 | tf_op jit(solution)/shard_map/ppermute | solution.py:280
  80.2 1.7 %collective-permute-start.11 = (bf16[512,384]{1,0:T(8,128)(2,1)S(1)}, bf16[512,384]{1,0:T(8,128)(2,1)S(1)}, u32[]{:S(2)}, u32[]{:S(2)}) collective-permute-start(bf16[512,384]{1,0:T(8,128)(2,1)S(1)} %collective-permute-done.7.refs_1_.refs_2_), channel_id=1, source_target_pairs={{0,1},{1,0},{2,3},{3,2},{4,5},{5,4},{6,7},{7,6},{8,9},{9,8},{10,11... | collective-permute-start | bytes 1179656 | tf_op jit(solution)/shard_map/ppermute | solution.py:280
  80.2 2.3 %collective-permute-start.12 = (bf16[512,384]{1,0:T(8,128)(2,1)S(1)}, bf16[512,384]{1,0:T(8,128)(2,1)S(1)}, u32[]{:S(2)}, u32[]{:S(2)}) collective-permute-start(bf16[512,384]{1,0:T(8,128)(2,1)S(1)} %collective-permute-done.8.refs_2_.refs_3_), channel_id=1, source_target_pairs={{0,1},{1,0},{2,3},{3,2},{4,5},{5,4},{6,7},{7,6},{8,9},{9,8},{10,11... | collective-permute-start | bytes 1179656 | tf_op jit(solution)/shard_map/ppermute | solution.py:280
  80.7 2.3 %collective-permute-start.13 = (bf16[512,384]{1,0:T(8,128)(2,1)S(1)}, bf16[512,384]{1,0:T(8,128)(2,1)S(1)}, u32[]{:S(2)}, u32[]{:S(2)}) collective-permute-start(bf16[512,384]{1,0:T(8,128)(2,1)S(1)} %collective-permute-done.9.refs_3_.refs_4_), channel_id=1, source_target_pairs={{0,1},{1,0},{2,3},{3,2},{4,5},{5,4},{6,7},{7,6},{8,9},{9,8},{10,11... | collective-permute-start | bytes 1179656 | tf_op jit(solution)/shard_map/ppermute | solution.py:280
  80.8 8.8 %collective-permute-start.15 = (bf16[256,512]{1,0:T(8,128)(2,1)S(1)}, bf16[256,512]{1,0:T(8,128)(2,1)S(1)}, u32[]{:S(2)}, u32[]{:S(2)}) collective-permute-start(bf16[256,512]{1,0:T(8,128)(2,1)S(1)} %add_convert_fusion.4), channel_id=1, source_target_pairs={{0,2},{1,3},{2,0},{3,1},{4,6},{5,7},{6,4},{7,5},{8,10},{9,11},{10,... | collective-permute-start | bytes 786440 | tf_op jit(solution)/shard_map/ppermute | solution.py:337
  83.0 1.7 %copy-start.5 = (bf16[512,384]{1,0:T(8,128)(2,1)}, bf16[512,384]{1,0:T(8,128)(2,1)S(1)}, u32[]{:S(2)}) copy-start(bf16[512,384]{1,0:T(8,128)(2,1)S(1)} %collective-permute-done.13.refs_6_.refs_8_) | copy-start | bytes 1179652
  83.0 2.0 %copy-start.1 = (bf16[1,3072,512]{2,1,0:T(8,128)(2,1)S(1)}, bf16[1,3072,512]{2,1,0:T(8,128)(2,1)}, u32[]{:S(2)}) copy-start(bf16[1,3072,512]{2,1,0:T(8,128)(2,1)} %param.11) | copy-start | bytes 9437188
  83.0 3.0 %copy-start.3 = (bf16[1,3072,512]{2,1,0:T(8,128)(2,1)S(1)}, bf16[1,3072,512]{2,1,0:T(8,128)(2,1)}, u32[]{:S(2)}) copy-start(bf16[1,3072,512]{2,1,0:T(8,128)(2,1)} %param.12) | copy-start | bytes 9437188
  89.6 3.0 %collective-permute-start.16 = (bf16[3,528,384]{2,1,0:T(8,128)(2,1)S(1)}, bf16[3,528,384]{2,1,0:T(8,128)(2,1)S(1)}, u32[]{:S(2)}, u32[]{:S(2)}) collective-permute-start(bf16[3,528,384]{2,1,0:T(8,128)(2,1)S(1)} %get-tuple-element.50), channel_id=1, source_target_pairs={{0,1},{1,0},{2,3},{3,2},{4,5},{5,4},{6,7},{7,6},{8,9},{9,8},{10,11... | collective-permute-start | bytes 3649544 | tf_op jit(solution)/shard_map/ppermute | solution.py:280
  92.7 8.7 %collective-permute-start.20 = (bf16[272,384]{1,0:T(8,128)(2,1)S(1)}, bf16[272,384]{1,0:T(8,128)(2,1)S(1)}, u32[]{:S(2)}, u32[]{:S(2)}) collective-permute-start(bf16[272,384]{1,0:T(8,128)(2,1)S(1)} %slice_bitcast_fusion), channel_id=1, source_target_pairs={{0,6},{1,7},{2,0},{3,1},{4,2},{5,3},{6,4},{7,5},{8,14},{9,15},{10,... | collective-permute-start | bytes 626696 | tf_op jit(solution)/shard_map/ppermute | solution.py:275
  93.5 8.0 %collective-permute-start.18 = (bf16[256,384]{1,0:T(8,128)(2,1)S(1)}, bf16[256,384]{1,0:T(8,128)(2,1)S(1)}, u32[]{:S(2)}, u32[]{:S(2)}) collective-permute-start(bf16[256,384]{1,0:T(8,128)(2,1)S(1)} %slice_bitcast_fusion.1), channel_id=1, source_target_pairs={{0,2},{1,3},{2,4},{3,5},{4,6},{5,7},{6,0},{7,1},{8,10},{9,11},{10,... | collective-permute-start | bytes 589832 | tf_op jit(solution)/shard_map/ppermute | solution.py:275
  96.0 7.8 %collective-permute-start.17 = (bf16[1,528,384]{2,1,0:T(8,128)(2,1)S(1)}, bf16[1,528,384]{2,1,0:T(8,128)(2,1)S(1)}, u32[]{:S(2)}, u32[]{:S(2)}) collective-permute-start(bf16[1,528,384]{2,1,0:T(8,128)(2,1)S(1)} %get-tuple-element.52), channel_id=1, source_target_pairs={{0,1},{1,0},{2,3},{3,2},{4,5},{5,4},{6,7},{7,6},{8,9},{9,8},{10,11... | collective-permute-start | bytes 1216520 | tf_op jit(solution)/shard_map/ppermute | solution.py:280
  101.7 10.3 %collective-permute-start.21 = (bf16[528,384]{1,0:T(8,128)(2,1)S(1)}, bf16[528,384]{1,0:T(8,128)(2,1)S(1)}, u32[]{:S(2)}, u32[]{:S(2)}) collective-permute-start(bf16[528,384]{1,0:T(8,128)(2,1)S(1)} %get-tuple-element.57), channel_id=1, source_target_pairs={{0,6},{1,7},{2,0},{3,1},{4,2},{5,3},{6,4},{7,5},{8,14},{9,15},{10,... | collective-permute-start | bytes 1216520 | tf_op jit(solution)/shard_map/ppermute | solution.py:275
  102.2 11.5 %collective-permute-start.19 = (bf16[528,384]{1,0:T(8,128)(2,1)S(1)}, bf16[528,384]{1,0:T(8,128)(2,1)S(1)}, u32[]{:S(2)}, u32[]{:S(2)}) collective-permute-start(bf16[528,384]{1,0:T(8,128)(2,1)S(1)} %get-tuple-element.58), channel_id=1, source_target_pairs={{0,2},{1,3},{2,4},{3,5},{4,6},{5,7},{6,0},{7,1},{8,10},{9,11},{10,... | collective-permute-start | bytes 1216520 | tf_op jit(solution)/shard_map/ppermute | solution.py:275
  114.8 20.6 %all-to-all-start.2 = ((bf16[32,16,512]{2,1,0:T(8,128)(2,1)}), bf16[32,16,512]{2,1,0:T(8,128)(2,1)S(1)}, u32[]{:S(2)}, u32[]{:S(2)}) async-start(bf16[32,16,512]{2,1,0:T(8,128)(2,1)} %bitcast.16), calls=%async_computation.2 | async-start | bytes 1048576 | tf_op jit(solution)/shard_map/all_to_all | solution.py:283
  119.5 8.0 %collective-permute-start.22 = (bf16[256,512]{1,0:T(8,128)(2,1)S(1)}, bf16[256,512]{1,0:T(8,128)(2,1)S(1)}, u32[]{:S(2)}, u32[]{:S(2)}) collective-permute-start(bf16[256,512]{1,0:T(8,128)(2,1)S(1)} %add_convert_fusion.3.refs_3_), channel_id=1, source_target_pairs={{0,4},{1,5},{2,6},{3,7},{4,0},{5,1},{6,2},{7,3},{8,12},{9,13},{10,... | collective-permute-start | bytes 786440 | tf_op jit(solution)/shard_map/ppermute | solution.py:337
  127.5 7.9 %copy-start.16 = (f32[256]{0:T(256)S(1)}, f32[256]{0:T(256)}, u32[]{:S(2)}) copy-start(f32[256]{0:T(256)} %param.9) | copy-start | bytes 3076
  127.5 1.6 %collective-permute-start.23 = (bf16[256,512]{1,0:T(8,128)(2,1)S(1)}, bf16[256,512]{1,0:T(8,128)(2,1)S(1)}, u32[]{:S(2)}, u32[]{:S(2)}) collective-permute-start(bf16[256,512]{1,0:T(8,128)(2,1)S(1)} %add_convert_fusion.2.refs_9_), channel_id=1, source_target_pairs={{0,1},{1,0},{2,3},{3,2},{4,5},{5,4},{6,7},{7,6},{8,9},{9,8},{10,11... | collective-permute-start | bytes 786440 | tf_op jit(solution)/shard_map/ppermute | solution.py:280
  129.2 1.0 copy-start.6
